TPU v7x, 256 devices: a whole 4x4x8 slice. The times are simulated.
256 devices in a mesh: row: 32 (over y, x, core), col: 8 (over z).
Axes of the slice: x: 4, y: 4, z: 8, core: 2. Of those that a mesh axis runs over, the one named last changes fastest.
Arguments:
- kernel: float32 [20480, 20480], P('row', 'col'), as said below
Outputs:
- factored: float32 [20480, 20480], P('row', 'col')
Inputs may be any that keep to these rules, and one draw needn't show every extreme that they name: `kernel`: in global order symmetric positive definite; its eigenvalues are at least 0.05.
All inputs are finite; a program needn't handle non-finite values.
Results may differ from a plain program's by a relative error of at most 0.0003.
Values sent between devices are 32-bit elements; how exact they have to be, the bound alone decides.
No kernel may reach another device: no remote copies, remote signals or barrier semaphores. Data moves between devices by JAX's collectives and lax.ppermute only.
A program may use at most 128 MiB of HBM per device.

v0:
```python
import jax
import jax.numpy as jnp
from jax import lax
from jax.sharding import PartitionSpec as P

NB = 128


def broadcast(value, axis, source):
    kept = jnp.where(lax.axis_index(axis) == source, value, 0).astype(value.dtype)
    return lax.psum(kept, axis)


def local(kernel):
    rows_here, cols_here = kernel.shape
    nrow = lax.axis_size("row")
    ncol = lax.axis_size("col")
    row_idx = lax.axis_index("row")
    col_idx = lax.axis_index("col")
    blocks_r = rows_here // NB
    blocks_c = cols_here // NB
    groups = nrow // ncol
    rows_g = jnp.arange(blocks_r, dtype=jnp.int32) * nrow + row_idx
    cols_g = jnp.arange(blocks_c, dtype=jnp.int32) * ncol + col_idx

    def factor_panel(matrix, step):
        start_r = step // nrow * NB
        start_c = step // ncol * NB
        corner = matrix[start_r : start_r + NB, start_c : start_c + NB]
        corner = broadcast(corner, "row", step % nrow)
        lower = jnp.linalg.cholesky(corner)
        inverse = lax.linalg.triangular_solve(
            lower, jnp.eye(NB, dtype=lower.dtype), left_side=True, lower=True
        )
        column = matrix[:, start_c : start_c + NB]
        solved = jnp.dot(column, inverse.T, precision=lax.Precision.HIGHEST).reshape(
            blocks_r, NB, NB
        )
        panel = jnp.where(
            (rows_g < step)[:, None, None],
            jnp.float32(0.0),
            jnp.where((rows_g == step)[:, None, None], lower[None], solved),
        )
        panel = panel.reshape(rows_here, NB)
        rows_side = broadcast(panel, "col", step % ncol)
        whole = lax.all_gather(rows_side, "row", axis=0, tiled=True)
        stacked = whole.reshape(groups, ncol, blocks_r, NB, NB)
        picked = lax.dynamic_index_in_dim(stacked, col_idx, 1, keepdims=False)
        cols_side = picked.transpose(1, 0, 2, 3).reshape(cols_here, NB)
        return (rows_side, cols_side)

    def product(left, right):
        return jnp.dot(left, right.T, precision=lax.Precision.HIGHEST)

    rows_first, cols_first = factor_panel(kernel, 0)
    updated = kernel - product(rows_first, cols_first)
    rows_second, cols_second = factor_panel(updated, 1)
    updated = updated - product(rows_second, cols_second)
    row_mask = jnp.repeat(rows_g < 2, NB)
    col_mask = jnp.repeat(cols_g >= 2, NB)
    result = jnp.where(row_mask[:, None] & col_mask[None, :], jnp.float32(0.0), updated)
    for step, rows_side in ((0, rows_first), (1, rows_second)):
        start_c = step // ncol * NB
        current = result[:, start_c : start_c + NB]
        chosen = jnp.where(col_idx == step % ncol, rows_side, current)
        result = lax.dynamic_update_slice(result, chosen, (0, start_c))
    return result


def solution(mesh):
    return jax.shard_map(
        local,
        mesh=mesh,
        in_specs=(P("row", "col"),),
        out_specs=P("row", "col"),
        check_vma=False,
    )
```

profile of v0, /device:TPU:1, one launch (start us, length us, event | category | flops | bytes accessed | tf_op | source)
XLA Modules:
  0.0 624.3 jit_solution(14654516166776597486)
XLA Ops:
  6.5 8.1 %copy.29 = f32[640,2560]{0,1:T(8,128)} copy(f32[640,2560]{1,0:T(8,128)} %param.4) | data formatting | bytes 13107200 | tf_op args[0]
  14.7 1.5 slice_select_fusion.2
  16.4 109.8 %all-reduce.5.cloned.1.call-done = f32[128,128]{0,1:T(8,128)} async-done(((f32[128,128]{0,1:T(8,128)}), f32[128,128]{0,1:T(8,128)}) %all-reduce.5.cloned.1.call-update) | async-done | bytes 65552 | tf_op jit(solution)/shard_map/psum | solution.py:11
  126.1 0.9 copy.25
  127.1 0.9 fusion.15
  127.9 11.7 %cholesky.44 = f32[128,128]{1,0:T(8,128)S(1)} custom-call(f32[128,128]{1,0:T(8,128)S(1)} %fusion.15), custom_call_target="Cholesky" | custom-call | tf_op jit(solution)/shard_map/jit(cholesky)/cholesky | solution.py:31
  139.7 0.7 compare_reduce_fusion.1
  140.3 0.6 select_bitcast_fusion.1
  141.2 9.8 %custom-call.6 = f32[1,128,128]{1,2,0:T(8,128)S(1)} custom-call(f32[1,128,128]{2,1,0:T(8,128)S(1)} %get-tuple-element.9), custom_call_target="InvertDiagBlocksLowerTriangular" | custom-call | tf_op jit(solution)/shard_map/triangular_solve/custom-call.0 | solution.py:32
  151.3 2.2 fusion.2
  153.5 67.1 %all-reduce.7.cloned.1.call-done = f32[640,128]{0,1:T(8,128)} async-done(((f32[640,128]{0,1:T(8,128)}), f32[640,128]{0,1:T(8,128)}) %all-reduce.7.cloned.1.call-update) | async-done | bytes 327696 | tf_op jit(solution)/shard_map/psum | solution.py:11
  220.8 68.6 %all-gather.3.cloned.1.call-done = f32[20480,128]{0,1:T(8,128)} async-done(((f32[640,128]{0,1:T(8,128)}), f32[20480,128]{0,1:T(8,128)}) %all-gather.3.cloned.1.call-update) | async-done | bytes 10485776 | tf_op jit(solution)/shard_map/all_gather | solution.py:46
  289.4 11.7 %copy.27 = f32[20480,128]{1,0:T(8,128)} copy(f32[20480,128]{0,1:T(8,128)} %all-gather.3.cloned.1.call-done) | data formatting | bytes 20971520 | tf_op jit(solution)/shard_map/all_gather | solution.py:46
  301.1 1.4 dynamic-slice_bitcast_fusion.1
  302.6 7.9 %convolution_subtract_fusion = f32[640,2560]{0,1:T(8,128)S(1)} fusion(f32[640,2560]{0,1:T(8,128)} %copy.29, f32[640,128]{0,1:T(8,128)S(1)} %copy-done.1, f32[2560,128]{1,0:T(8,128)S(1)} %bitcast.60), kind=kOutput, calls=%fused_computation.1 | convolution fusion | flops 2518220800 | bytes 14745600 | tf_op jit(solution)/shard_map/dot_general | solution.py:53
  310.5 2.8 copy-done
  314.3 105.0 %all-reduce.9.cloned.1.call-done = f32[128,128]{0,1:T(8,128)} async-done(((f32[128,128]{0,1:T(8,128)}), f32[128,128]{0,1:T(8,128)}) %all-reduce.9.cloned.1.call-update) | async-done | bytes 65552 | tf_op jit(solution)/shard_map/psum | solution.py:11
  419.3 0.9 copy.31
  420.2 0.9 fusion.13
  421.1 11.7 %cholesky.55 = f32[128,128]{1,0:T(8,128)S(1)} custom-call(f32[128,128]{1,0:T(8,128)S(1)} %fusion.13), custom_call_target="Cholesky" | custom-call | tf_op jit(solution)/shard_map/jit(cholesky)/cholesky | solution.py:31
  432.8 0.7 compare_reduce_fusion
  434.4 9.8 %custom-call.7 = f32[1,128,128]{1,2,0:T(8,128)S(1)} custom-call(f32[1,128,128]{2,1,0:T(8,128)S(1)} %get-tuple-element.6), custom_call_target="InvertDiagBlocksLowerTriangular" | custom-call | tf_op jit(solution)/shard_map/triangular_solve/custom-call.0 | solution.py:32
  444.5 2.1 fusion.4
  446.7 67.1 %all-reduce.11.cloned.1.call-done = f32[640,128]{0,1:T(8,128)} async-done(((f32[640,128]{0,1:T(8,128)}), f32[640,128]{0,1:T(8,128)}) %all-reduce.11.cloned.1.call-update) | async-done | bytes 327696 | tf_op jit(solution)/shard_map/psum | solution.py:11
  514.0 68.4 %all-gather.5.cloned.1.call-done = f32[20480,128]{0,1:T(8,128)} async-done(((f32[640,128]{0,1:T(8,128)}), f32[20480,128]{0,1:T(8,128)}) %all-gather.5.cloned.1.call-update) | async-done | bytes 10485776 | tf_op jit(solution)/shard_map/all_gather | solution.py:46
  582.4 11.7 %copy.34 = f32[20480,128]{1,0:T(8,128)} copy(f32[20480,128]{0,1:T(8,128)} %all-gather.5.cloned.1.call-done) | data formatting | bytes 20971520 | tf_op jit(solution)/shard_map/all_gather | solution.py:46
  594.1 1.4 dynamic-slice_bitcast_fusion
  595.6 8.4 %subtract_select_fusion = f32[640,2560]{0,1:T(8,128)S(1)} fusion(f32[640,2560]{0,1:T(8,128)} %copy-done, f32[640,128]{0,1:T(8,128)S(1)} %copy-done.2, f32[2560,128]{1,0:T(8,128)S(1)} %bitcast.61, pred[640]{0:T(1024)(128)(4,1)S(1)} %broadcast_bitcast_fusion.5, pred[2560]{0:T(1024)(128)(4,1)S(1)} %broadcast_bitcast_fusion), kind=kOutput, calls=%fused_computation | convolution fusion | flops 2521497600 | bytes 14748800 | tf_op jit(solution)/shard_map/dot_general | solution.py:53
  604.1 2.7 copy.45
  606.8 1.7 fusion.7
  608.5 0.8 select_dynamic-update-slice_fusion
  609.3 8.1 %copy.37 = f32[640,2560]{1,0:T(8,128)} copy(f32[640,2560]{0,1:T(8,128)} %select_dynamic-update-slice_fusion) | data formatting | bytes 13107200 | tf_op jit(solution)/shard_map/dynamic_update_slice | solution.py:66
  (39 shorter events, 3.5 us)
Async XLA Ops:
  6.5 119.6 %all-reduce.5.cloned.1.call-start = ((), (), s32[]{:S(2)}) async-start(), calls=%async_computation | async-start | bytes 131072 | tf_op jit(solution)/shard_map/psum | solution.py:11
  16.1 204.5 %all-reduce.7.cloned.1.call-start = ((), (), s32[]{:S(2)}) async-start(), calls=%async_computation.1 | async-start | bytes 655360 | tf_op jit(solution)/shard_map/psum | solution.py:11
  153.5 135.9 %all-gather.3.cloned.1.call-start = ((), (), s32[]{:S(2)}) async-start(), calls=%async_computation.2 | async-start | bytes 10813440 | tf_op jit(solution)/shard_map/all_gather | solution.py:46
  220.6 198.7 %all-reduce.9.cloned.1.call-start = ((), (), s32[]{:S(2)}) async-start(), calls=%async_computation.3 | async-start | bytes 131072 | tf_op jit(solution)/shard_map/psum | solution.py:11
  220.8 81.8 %copy-start.1 = (f32[640,128]{0,1:T(8,128)S(1)}, f32[640,128]{0,1:T(8,128)}, u32[]{:S(2)}) copy-start(f32[640,128]{0,1:T(8,128)} %all-reduce.7.cloned.1.call-done) | copy-start | bytes 983044
  310.5 2.8 copy-start
  314.0 199.8 %all-reduce.11.cloned.1.call-start = ((), (), s32[]{:S(2)}) async-start(), calls=%async_computation.4 | async-start | bytes 655360 | tf_op jit(solution)/shard_map/psum | solution.py:11
  446.6 135.7 %all-gather.5.cloned.1.call-start = ((), (), s32[]{:S(2)}) async-start(), calls=%async_computation.5 | async-start | bytes 10813440 | tf_op jit(solution)/shard_map/all_gather | solution.py:46
  514.0 81.7 %copy-start.2 = (f32[640,128]{0,1:T(8,128)S(1)}, f32[640,128]{0,1:T(8,128)}, u32[]{:S(2)}) copy-start(f32[640,128]{0,1:T(8,128)} %all-reduce.11.cloned.1.call-done) | copy-start | bytes 983044
Sparse Core Ops, SparseCore 0:
  16.3 109.8 all-reduce.4
  153.6 66.9 all-reduce.6
  223.3 66.0 all-gather.2
  314.1 105.1 all-reduce.8
  446.8 66.9 all-reduce.10
  516.3 66.0 all-gather.4
where the time goes:
time: 626 us; the launch traced here: 624 us
  waiting for transfers between devices  486 us (78%)
  other arithmetic  52.1 us (8%)
  local copies, waits for them, and re-layouts  50.9 us (8%)
  matrix products  21.2 us (3%)
  between operations  13.7 us (2%)
    psum x4, waiting for transfers between devices, broadcast(): return lax.psum(kept, axis)  349 us
    all_gather x2, waiting for transfers between devices, factor_panel(): whole = lax.all_gather(rows_side, 'row', axis=0, tiled=True)  137 us
    another operation x6, other arithmetic, factor_panel(): lower = jnp.linalg.cholesky(corner)  24.8 us
    all_gather x2, local copies, waits for them, and re-layouts, factor_panel(): whole = lax.all_gather(rows_side, 'row', axis=0, tiled=True)  23.5 us
    another operation x4, other arithmetic, factor_panel(): lax.linalg.triangular_solve(lower, jnp.eye(NB, dtype=lower.dtype), left_s...  20.9 us
    dot_general x2, matrix products, product(): return jnp.dot(left, right.T, precision=lax.Precision.HIGHEST)  16.4 us
    unnamed x8, local copies, waits for them, and re-layouts  13.7 us
  transfers between devices with their start and end apart: 6, of which 6 were waited for; matrix products, arithmetic and copies ran while one was open for 0% of the time, Pallas kernels for 0%

commit v1 on v0

v1 whole, which is shorter than its diff:
```python
import jax
import jax.numpy as jnp
from jax import lax
from jax.experimental import pallas as pl
from jax.experimental.pallas import tpu as pltpu
from jax.sharding import PartitionSpec as P

NB = 128
HIGHEST = lax.Precision.HIGHEST
F32 = jnp.float32
BF16 = jnp.bfloat16


def bc(v): return jnp.broadcast_to(v,(8,NB))
def eliminate4(full):
    eye=(lax.broadcasted_iota(jnp.int32,(NB,NB),0)==lax.broadcasted_iota(jnp.int32,(NB,NB),1)).astype(F32)
    G=NB//8
    A=[full[8*g:8*g+8,:] for g in range(G)]
    I=[eye[8*g:8*g+8,:] for g in range(G)]
    sub=lax.broadcasted_iota(jnp.int32,(8,NB),0)
    lane=lax.broadcasted_iota(jnp.int32,(8,NB),1)
    outU=[];outW=[]
    for k in range(0,NB,4):
        g0,s=divmod(k,8)
        C=[bc(A[g0][:,k+a:k+a+1]) for a in range(4)]
        D=[[bc(C[a][s+b:s+b+1,:]) if b<=a else None for b in range(4)] for a in range(4)]
        ra=[bc(A[g0][s+b:s+b+1,:]) for b in range(4)]
        ri=[bc(I[g0][s+b:s+b+1,:]) for b in range(4)]
        p00,p10,p11=D[0][0],D[1][0],D[1][1]
        ip=1.0/(p00*p11-p10*p10)
        i00,i10,i11=p11*ip,-p10*ip,p00*ip
        q20,q21,q30,q31=D[2][0],D[2][1],D[3][0],D[3][1]
        t02=i00*q20+i10*q21; t12=i10*q20+i11*q21
        t03=i00*q30+i10*q31; t13=i10*q30+i11*q31
        s22=D[2][2]-(q20*t02+q21*t12)
        s32=D[3][2]-(q30*t02+q31*t12)
        s33=D[3][3]-(q30*t03+q31*t13)
        isd=1.0/(s22*s33-s32*s32)
        j22,j32,j33=s33*isd,-s32*isd,s22*isd
        def solve(r):
            y2=r[2]-(t02*r[0]+t12*r[1])
            y3=r[3]-(t03*r[0]+t13*r[1])
            x2=j22*y2+j32*y3; x3=j32*y2+j33*y3
            x0=(i00*r[0]+i10*r[1])-(t02*x2+t03*x3)
            x1=(i10*r[0]+i11*r[1])-(t12*x2+t13*x3)
            return [x0,x1,x2,x3],y2,y3
        xa,ya2,ya3=solve(ra)
        xi,yi2,yi3=solve(ri)
        for g in range(g0,G):
            if g==g0:
                if s==4: continue
                c=[jnp.where(sub>=4,v,0.0) for v in C]
            else:
                c=[bc(A[g][:,k+a:k+a+1]) for a in range(4)]
            A[g]=A[g]-((c[0]*xa[0]+c[1]*xa[1])+(c[2]*xa[2]+c[3]*xa[3]))
            I[g]=I[g]-((c[0]*xi[0]+c[1]*xi[1])+(c[2]*xi[2]+c[3]*xi[3]))
        def rsq(x):
            r=lax.rsqrt(x); return r*(1.5-0.5*x*r*r)
        def norm2(d00,d10,d11,r0,r1):
            rs0=rsq(d00); l10=d10*rs0; e=d11-l10*l10; rs1=rsq(e)
            return lambda r0,r1:(r0*rs0,(r1-l10*(r0*rs0))*rs1)
        nP=norm2(p00,p10,p11,None,None); nS=norm2(s22,s32,s33,None,None)
        u=[*nP(ra[0],ra[1]),*nS(ya2,ya3)]
        w=[*nP(ri[0],ri[1]),*nS(yi2,yi3)]
        for b in range(4):
            u[b]=jnp.where(lane>=k+b,u[b],0.0)
        if s==0:
            hu,hw=u,w
        else:
            uu=hu+u; ww=hw+w
            ru=uu[7]; rw=ww[7]
            for b in range(6,-1,-1):
                ru=jnp.where(sub==b,uu[b],ru); rw=jnp.where(sub==b,ww[b],rw)
            outU.append(ru); outW.append(rw)
    return jnp.concatenate(outU,0), jnp.concatenate(outW,0)


def mm(a, b):
    return jnp.dot(a, b, precision=HIGHEST, preferred_element_type=F32)


def mmt(a, b):
    return lax.dot_general(a, b, (((1,), (1,)), ((), ())), precision=HIGHEST, preferred_element_type=F32)


def factor_kernel(top, bottom, l_ref, w_ref):
    zero = jnp.zeros((NB, NB), F32)
    u0, w0 = eliminate4(top[:, :NB])
    l10 = mmt(bottom[:, :NB], w0)
    u1, w1 = eliminate4(bottom[:, NB:] - mmt(l10, l10))
    l_ref[:NB, :NB] = u0.T
    l_ref[:NB, NB:] = zero
    l_ref[NB:, :NB] = l10
    l_ref[NB:, NB:] = u1.T
    w_ref[:NB, :NB] = w0
    w_ref[:NB, NB:] = zero
    w_ref[NB:, :NB] = -mm(mm(w1, l10), w0)
    w_ref[NB:, NB:] = w1


def factor(top, bottom):
    return pl.pallas_call(
        factor_kernel, out_shape=[jax.ShapeDtypeStruct((2 * NB, 2 * NB), F32)] * 2, name="factor"
    )(top, bottom)


def split(v):
    hi = v.astype(BF16)
    return hi, (v - hi.astype(F32)).astype(BF16)


def update_kernel(info, k_ref, first_ref, second_ref, b0_ref, b1_ref, l_ref, w_ref, out_ref, rows, rhi, rlo):
    step = pl.program_id(0)
    d, z = info[2], info[3]

    @pl.when(step == 0)
    def _():
        solved = mmt(first_ref[...], w_ref[:, :NB]) + mmt(second_ref[...], w_ref[:, NB:])
        rows[...] = solved
        hi, lo = split(solved)
        rhi[...] = hi
        rlo[...] = lo

        @pl.when(d == 0)
        def _():
            rows[:NB, :] = l_ref[:NB, :]

        @pl.when(d == 1)
        def _():
            rows[:NB, NB:] = l_ref[NB:, NB:]

    cols = mm(w_ref[:, :NB], b0_ref[0]) + mm(w_ref[:, NB:], b1_ref[0])
    chi, clo = split(cols)
    dot = lambda a, b: jnp.dot(a, b, preferred_element_type=F32)
    prod = dot(rhi[...], chi) + (dot(rlo[...], chi) + dot(rhi[...], clo))
    out_ref[...] = k_ref[...] - prod

    @pl.when(d < 2)
    def _():
        out_ref[:NB, :] = jnp.zeros((NB, out_ref.shape[1]), F32)

    @pl.when((step == 0) & (z == 0))
    def _():
        out_ref[:, :NB] = rows[:, :NB]

    @pl.when((step == 0) & (z == 1))
    def _():
        out_ref[:, :NB] = rows[:, NB:]


def update(info, kernel, first, second, b0, b1, low, inv):
    r, c = kernel.shape
    w = c // 4
    whole = lambda shape: pl.BlockSpec(shape, lambda n, s: (0,) * len(shape))
    return pl.pallas_call(
        update_kernel,
        out_shape=jax.ShapeDtypeStruct((r, c), F32),
        grid_spec=pltpu.PrefetchScalarGridSpec(
            num_scalar_prefetch=1,
            grid=(4,),
            in_specs=[
                pl.BlockSpec((r, w), lambda n, s: (0, n)),
                whole((r, NB)),
                whole((r, NB)),
                pl.BlockSpec((1, NB, w), lambda n, s: ((s[0] - n + 4) % 4, 0, 0)),
                pl.BlockSpec((1, NB, w), lambda n, s: ((s[1] - n + 4) % 4, 0, 0)),
                whole((2 * NB, 2 * NB)),
                whole((2 * NB, 2 * NB)),
            ],
            out_specs=pl.BlockSpec((r, w), lambda n, s: (0, n)),
            scratch_shapes=[
                pltpu.VMEM((r, 2 * NB), F32),
                pltpu.VMEM((r, 2 * NB), BF16),
                pltpu.VMEM((r, 2 * NB), BF16),
            ],
        ),
        compiler_params=pltpu.CompilerParams(
            dimension_semantics=("arbitrary",), vmem_limit_bytes=40 * 1024 * 1024
        ),
        cost_estimate=pl.CostEstimate(flops=7_000_000_000, bytes_accessed=16_000_000, transcendentals=0),
        name="update",
    )(info, kernel, first, second, b0, b1, low, inv)


def place(core, p, q):
    return p * 8 + q * 2 if core == 0 else q * 8 + p * 2 + 1


def local(kernel):
    row = lax.axis_index("row")
    z = lax.axis_index("col")
    y, x, core = row // 8, row // 2 % 4, row % 2
    p = jnp.where(core == 0, y, x)
    q = jnp.where(core == 0, x, y)

    gathered = lax.all_gather(kernel[:, :NB], "col", axis=0, tiled=False)
    first, second = gathered[0], gathered[1]

    own = kernel[:NB, :NB]
    other = lax.ppermute(own, ("row", "col"), [(r * 8 + a, r * 8 + 1 - a) for r in (0, 1) for a in (0, 1)])
    corner = jnp.where(z == 0, jnp.concatenate([own, other], 1), jnp.concatenate([other, own], 1))
    got = [
        lax.ppermute(
            corner, ("row", "col"), [(r * 8 + a, r * 8 + b) for r in (0, 1) for a, b in ((0, 8 - n), (1, 1 + n))]
        )
        for n in (1, 2, 3)
    ]
    corner = jnp.where(z < 2, corner, got[0] + got[1] + got[2])

    w = kernel.shape[1] // 4
    quarters = [kernel[:NB, j * w : (j + 1) * w] for j in range(4)]
    got = [
        lax.ppermute(quarters[j], "row", [(place(c, 0, 0), place(c, j, 0)) for c in (0, 1)]) for j in (1, 2, 3)
    ]
    quarter = jnp.where(p == 0, quarters[0], got[0] + got[1] + got[2])
    packed = jnp.concatenate([quarter, corner], 1)
    got = [
        lax.ppermute(packed, "row", [(place(c, j, 0), place(c, j, n)) for c in (0, 1) for j in range(4)])
        for n in (1, 3, 2)
    ]
    packed = jnp.where(q == 0, packed, got[0] + got[1] + got[2])
    got = [
        lax.ppermute(
            packed,
            "row",
            [(place(c, j, i), place(c, (j + n) % 4, i)) for c in (0, 1) for j in range(4) for i in range(4)],
        )
        for n in (1, 2, 3)
    ]
    corner = packed[:, w:]
    for n in (1, 2, 3):
        corner = jnp.where(p == n, got[n - 1][:, w:], corner)
    swap = lambda v: lax.ppermute(v, "row", [(i, i ^ 1) for i in range(32)])
    corner_other = swap(corner)
    top = jnp.where(core == 0, corner, corner_other)
    bottom = jnp.where(core == 0, corner_other, corner)
    low, inv = factor(top, bottom)
    slots = jnp.stack([packed[:, :w], got[0][:, :w], got[1][:, :w], got[2][:, :w]])
    slots_other = swap(slots)
    b0 = jnp.where(core == 0, slots, slots_other)
    b1 = jnp.where(core == 0, slots_other, slots)
    info = jnp.stack([y, x, row, z]).astype(jnp.int32)
    return update(info, kernel, first, second, b0, b1, low, inv)


def solution(mesh):
    return jax.shard_map(
        local,
        mesh=mesh,
        in_specs=(P("row", "col"),),
        out_specs=P("row", "col"),
        check_vma=False,
    )
```

time: 626 us -> 109 us (0.17)
  waiting for transfers between devices: 486 us -> 25.1 us
  other arithmetic: 52.1 us -> 4.67 us
  local copies, waits for them, and re-layouts: 50.9 us -> 9.31 us
  Pallas kernels: 0 us -> 27.6 us
  starting transfers between devices: 0.39 us -> 27.9 us
  matrix products: 21.2 us -> 0 us
    psum x4 -> x0, waiting for transfers between devices: 349 us -> none  [broadcast(): return lax.psum(kept, axis)]
    all_gather x2 -> x1, waiting for transfers between devices: 137 us -> 0.02 us  [local(): gathered = lax.all_gather(kernel[:, :NB], 'col', axis=0, tiled=False)]
    another operation x10 -> x2, other arithmetic: 45.7 us -> 0.17 us  [the longest x1 0.09 us: local(): jnp.stack([packed[:, :w], got[0][:, :w], got[1][:, :w], got[2][:, :w]])]
    ppermute x0 -> x15, starting transfers between devices: none -> 27.9 us  [the longest x3 8.09 us: local(): lax.ppermute(corner, ('row', 'col'), [(r * 8 + a, r * 8 + b) for r in (0,...]
    pallas_call x0 -> x2, Pallas kernels: none -> 27.6 us  [the longest x1 14.5 us: factor(): pl.pallas_call(factor_kernel, out_shape=[jax.ShapeDtypeStruct((2 * NB, 2...]
    ppermute x0 -> x15, waiting for transfers between devices: none -> 25.1 us  [the longest x3 11.2 us: local(): lax.ppermute(packed, 'row', [(place(c, j, i), place(c, (j + n) % 4, i)) f...]
    all_gather x2 -> x0, local copies, waits for them, and re-layouts: 23.5 us -> none  [factor_panel(): whole = lax.all_gather(rows_side, 'row', axis=0, tiled=True)]
    dot_general x4 -> x0, matrix products: 20.7 us -> none  [the longest x2 16.4 us: product(): return jnp.dot(left, right.T, precision=lax.Precision.HIGHEST)]
  transfers between devices with their start and end apart: 6 -> 16, of which waited for: 6 -> 10; matrix products, arithmetic and copies ran while one was open for 0% -> 7% of each run, Pallas kernels for 0% -> 13%
where the time goes in v1:
time: 109 us; the launch traced here: 108 us
  starting transfers between devices  27.9 us (26%)
  Pallas kernels  27.6 us (25%)
  waiting for transfers between devices  25.1 us (23%)
  between operations  13.7 us (13%)
  local copies, waits for them, and re-layouts  9.31 us (9%)
  other arithmetic  4.67 us (4%)
    pallas_call x1, Pallas kernels, factor(): pl.pallas_call(factor_kernel, out_shape=[jax.ShapeDtypeStruct((2 * NB, 2...  14.5 us
    pallas_call x1, Pallas kernels, update(): pl.pallas_call(update_kernel, out_shape=jax.ShapeDtypeStruct((r, c), F32)...  13.1 us
    ppermute x3, waiting for transfers between devices, local(): lax.ppermute(packed, 'row', [(place(c, j, i), place(c, (j + n) % 4, i)) f...  11.2 us
    ppermute x3, starting transfers between devices, local(): lax.ppermute(corner, ('row', 'col'), [(r * 8 + a, r * 8 + b) for r in (0,...  8.09 us
    ppermute x3, waiting for transfers between devices, local(): lax.ppermute(packed, 'row', [(place(c, j, 0), place(c, j, n)) for c in (0...  7.63 us
    ppermute x1, starting transfers between devices, local(): lax.ppermute(own, ('row', 'col'), [(r * 8 + a, r * 8 + 1 - a) for r in (0...  4.36 us
    unnamed x12, local copies, waits for them, and re-layouts  4.25 us
    ppermute x3, starting transfers between devices, local(): lax.ppermute(packed, 'row', [(place(c, j, i), place(c, (j + n) % 4, i)) f...  4.17 us
  transfers between devices with their start and end apart: 16, of which 10 were waited for; matrix products, arithmetic and copies ran while one was open for 7% of the time, Pallas kernels for 13%

profile of v1, /device:TPU:1, one launch (start us, length us, event | category | flops | bytes accessed | tf_op | source)
XLA Modules:
  0.0 108.4 jit_solution(6519156657919446470)
XLA Ops:
  7.4 4.4 %collective-permute-start.3 = (f32[128,128]{1,0:T(8,128)S(1)}, f32[128,128]{1,0:T(8,128)S(1)}, u32[]{:S(2)}, u32[]{:S(2)}) collective-permute-start(f32[128,128]{1,0:T(8,128)S(1)} %slice.55), channel_id=1, source_target_pairs={{0,1},{1,0},{8,9},{9,8}} | collective-permute-start | bytes 196616 | tf_op jit(solution)/shard_map/ppermute | solution.py:200
  11.8 1.7 %slice.48 = f32[640,128]{1,0:T(8,128)} slice(f32[640,2560]{1,0:T(8,128)} %k_ref.1), slice={[0:640], [0:128]} | slice | bytes 655360 | tf_op jit(solution)/shard_map/slice | solution.py:196
  13.5 5.5 %collective-permute-start.6 = (f32[128,256]{1,0:T(8,128)S(1)}, f32[128,256]{1,0:T(8,128)S(1)}, u32[]{:S(2)}, u32[]{:S(2)}) collective-permute-start(f32[128,256]{1,0:T(8,128)S(1)} %maximum_select_fusion), channel_id=1, source_target_pairs={{0,5},{1,4},{8,13},{9,12}} | collective-permute-start | bytes 393224 | tf_op jit(solution)/shard_map/ppermute | solution.py:203
  19.0 1.3 %collective-permute-start.5 = (f32[128,256]{1,0:T(8,128)S(1)}, f32[128,256]{1,0:T(8,128)S(1)}, u32[]{:S(2)}, u32[]{:S(2)}) collective-permute-start(f32[128,256]{1,0:T(8,128)S(1)} %maximum_select_fusion), channel_id=1, source_target_pairs={{0,6},{1,3},{8,14},{9,11}} | collective-permute-start | bytes 393224 | tf_op jit(solution)/shard_map/ppermute | solution.py:203
  20.3 1.3 %collective-permute-start.4 = (f32[128,256]{1,0:T(8,128)S(1)}, f32[128,256]{1,0:T(8,128)S(1)}, u32[]{:S(2)}, u32[]{:S(2)}) collective-permute-start(f32[128,256]{1,0:T(8,128)S(1)} %maximum_select_fusion), channel_id=1, source_target_pairs={{0,7},{1,2},{8,15},{9,10}} | collective-permute-start | bytes 393224 | tf_op jit(solution)/shard_map/ppermute | solution.py:203
  21.7 1.2 %fusion.2 = (f32[128,640]{1,0:T(8,128)S(1)}, f32[128,640]{1,0:T(8,128)S(1)}, f32[128,640]{1,0:T(8,128)S(1)}) fusion(f32[640,2560]{1,0:T(8,128)} %k_ref.1), kind=kLoop, calls=%fused_computation.18 | loop fusion | bytes 1966080 | tf_op jit(solution)/shard_map/slice | solution.py:211
  22.9 1.3 %collective-permute-start.1 = (f32[128,640]{1,0:T(8,128)S(1)}, f32[128,640]{1,0:T(8,128)S(1)}, u32[]{:S(2)}, u32[]{:S(2)}) collective-permute-start(f32[128,640]{1,0:T(8,128)S(1)} %get-tuple-element.9), channel_id=1, source_target_pairs={{0,128},{8,40},{1,129},{9,41},{2,130},{10,42},{3,131},{11,43},{4,1... | collective-permute-start | bytes 983048 | tf_op jit(solution)/shard_map/ppermute | solution.py:213
  24.2 1.3 %collective-permute-start.2 = (f32[128,640]{1,0:T(8,128)S(1)}, f32[128,640]{1,0:T(8,128)S(1)}, u32[]{:S(2)}, u32[]{:S(2)}) collective-permute-start(f32[128,640]{1,0:T(8,128)S(1)} %get-tuple-element.10), channel_id=1, source_target_pairs={{0,192},{8,56},{1,193},{9,57},{2,194},{10,58},{3,195},{11,59},{4,1... | collective-permute-start | bytes 983048 | tf_op jit(solution)/shard_map/ppermute | solution.py:213
  25.5 1.3 %collective-permute-start = (f32[128,640]{1,0:T(8,128)S(1)}, f32[128,640]{1,0:T(8,128)S(1)}, u32[]{:S(2)}, u32[]{:S(2)}) collective-permute-start(f32[128,640]{1,0:T(8,128)S(1)} %get-tuple-element.11), channel_id=1, source_target_pairs={{0,64},{8,24},{1,65},{9,25},{2,66},{10,26},{3,67},{11,27},{4,68},{... | collective-permute-start | bytes 983048 | tf_op jit(solution)/shard_map/ppermute | solution.py:213
  26.9 1.5 %collective-permute-done.4 = f32[128,256]{1,0:T(8,128)S(1)} collective-permute-done((f32[128,256]{1,0:T(8,128)S(1)}, f32[128,256]{1,0:T(8,128)S(1)}, u32[]{:S(2)}, u32[]{:S(2)}) %collective-permute-start.4) | collective-permute-done | bytes 131104 | tf_op jit(solution)/shard_map/ppermute | solution.py:203
  28.5 1.0 collective-permute-done.2
  29.5 2.2 %collective-permute-done = f32[128,640]{1,0:T(8,128)S(1)} collective-permute-done((f32[128,640]{1,0:T(8,128)S(1)}, f32[128,640]{1,0:T(8,128)S(1)}, u32[]{:S(2)}, u32[]{:S(2)}) %collective-permute-start) | collective-permute-done | bytes 327712 | tf_op jit(solution)/shard_map/ppermute | solution.py:213
  31.7 1.0 add_select_fusion.1
  32.8 1.3 %collective-permute-start.9 = (f32[128,896]{1,0:T(8,128)S(1)}, f32[128,896]{1,0:T(8,128)S(1)}, u32[]{:S(2)}, u32[]{:S(2)}) collective-permute-start(f32[128,896]{1,0:T(8,128)S(1)} %pad_maximum_fusion.1), channel_id=1, source_target_pairs={{0,32},{64,96},{128,160},{192,224},{8,136},{24,152},{40,168},{56,1... | collective-permute-start | bytes 1376264 | tf_op jit(solution)/shard_map/ppermute | solution.py:218
  34.1 1.3 %collective-permute-start.8 = (f32[128,896]{1,0:T(8,128)S(1)}, f32[128,896]{1,0:T(8,128)S(1)}, u32[]{:S(2)}, u32[]{:S(2)}) collective-permute-start(f32[128,896]{1,0:T(8,128)S(1)} %pad_maximum_fusion.1), channel_id=1, source_target_pairs={{0,48},{64,112},{128,176},{192,240},{8,200},{24,216},{40,232},{56,... | collective-permute-start | bytes 1376264 | tf_op jit(solution)/shard_map/ppermute | solution.py:218
  35.4 1.3 %collective-permute-start.7 = (f32[128,896]{1,0:T(8,128)S(1)}, f32[128,896]{1,0:T(8,128)S(1)}, u32[]{:S(2)}, u32[]{:S(2)}) collective-permute-start(f32[128,896]{1,0:T(8,128)S(1)} %pad_maximum_fusion.1), channel_id=1, source_target_pairs={{0,16},{64,80},{128,144},{192,208},{8,72},{24,88},{40,104},{56,120... | collective-permute-start | bytes 1376264 | tf_op jit(solution)/shard_map/ppermute | solution.py:218
  36.8 2.7 %collective-permute-done.9 = f32[128,896]{1,0:T(8,128)S(1)} collective-permute-done((f32[128,896]{1,0:T(8,128)S(1)}, f32[128,896]{1,0:T(8,128)S(1)}, u32[]{:S(2)}, u32[]{:S(2)}) %collective-permute-start.9) | collective-permute-done | bytes 458784 | tf_op jit(solution)/shard_map/ppermute | solution.py:218
  39.5 1.3 %collective-permute-done.8 = f32[128,896]{1,0:T(8,128)S(1)} collective-permute-done((f32[128,896]{1,0:T(8,128)S(1)}, f32[128,896]{1,0:T(8,128)S(1)}, u32[]{:S(2)}, u32[]{:S(2)}) %collective-permute-start.8) | collective-permute-done | bytes 458784 | tf_op jit(solution)/shard_map/ppermute | solution.py:218
  40.8 3.6 %collective-permute-done.7 = f32[128,896]{1,0:T(8,128)S(1)} collective-permute-done((f32[128,896]{1,0:T(8,128)S(1)}, f32[128,896]{1,0:T(8,128)S(1)}, u32[]{:S(2)}, u32[]{:S(2)}) %collective-permute-start.7) | collective-permute-done | bytes 458784 | tf_op jit(solution)/shard_map/ppermute | solution.py:218
  44.5 1.4 %collective-permute-start.12 = (f32[128,896]{1,0:T(8,128)S(1)}, f32[128,896]{1,0:T(8,128)S(1)}, u32[]{:S(2)}, u32[]{:S(2)}) collective-permute-start(f32[128,896]{1,0:T(8,128)S(1)} %add_select_fusion), channel_id=1, source_target_pairs={{0,192},{16,208},{32,224},{48,240},{64,0},{80,16},{96,32},{112,48}... | collective-permute-start | bytes 1376264 | tf_op jit(solution)/shard_map/ppermute | solution.py:223
  45.9 2.8 %collective-permute-start.11 = (f32[128,896]{1,0:T(8,128)S(1)}, f32[128,896]{1,0:T(8,128)S(1)}, u32[]{:S(2)}, u32[]{:S(2)}) collective-permute-start(f32[128,896]{1,0:T(8,128)S(1)} %add_select_fusion), channel_id=1, source_target_pairs={{0,128},{16,144},{32,160},{48,176},{64,192},{80,208},{96,224},{112... | collective-permute-start | bytes 1376264 | tf_op jit(solution)/shard_map/ppermute | solution.py:223
  48.7 4.5 %collective-permute-done.12 = f32[128,896]{1,0:T(8,128)S(1)} collective-permute-done((f32[128,896]{1,0:T(8,128)S(1)}, f32[128,896]{1,0:T(8,128)S(1)}, u32[]{:S(2)}, u32[]{:S(2)}) %collective-permute-start.12) | collective-permute-done | bytes 458784 | tf_op jit(solution)/shard_map/ppermute | solution.py:223
  53.2 1.9 %collective-permute-done.11 = f32[128,896]{1,0:T(8,128)S(1)} collective-permute-done((f32[128,896]{1,0:T(8,128)S(1)}, f32[128,896]{1,0:T(8,128)S(1)}, u32[]{:S(2)}, u32[]{:S(2)}) %collective-permute-start.11) | collective-permute-done | bytes 458784 | tf_op jit(solution)/shard_map/ppermute | solution.py:223
  55.1 4.8 %collective-permute-done.10 = f32[128,896]{1,0:T(8,128)S(1)} collective-permute-done((f32[128,896]{1,0:T(8,128)S(1)}, f32[128,896]{1,0:T(8,128)S(1)}, u32[]{:S(2)}, u32[]{:S(2)}) %collective-permute-start.10) | collective-permute-done | bytes 458784 | tf_op jit(solution)/shard_map/ppermute | solution.py:223
  61.5 3.1 %collective-permute-start.13 = (f32[4,128,640]{2,1,0:T(8,128)S(1)}, f32[4,128,640]{2,1,0:T(8,128)}, u32[]{:S(2)}, u32[]{:S(2)}) collective-permute-start(f32[4,128,640]{2,1,0:T(8,128)S(1)} %pad_maximum_fusion), channel_id=1, source_target_pairs={{0,8},{8,0},{16,24},{24,16},{32,40},{40,32},{48,56},{56,48},{64,72... | collective-permute-start | bytes 3932168 | tf_op jit(solution)/shard_map/ppermute | solution.py:233
  64.6 0.9 fusion.1
  65.9 1.6 %collective-permute-done.14 = f32[128,256]{1,0:T(8,128)S(1)} collective-permute-done((f32[128,256]{1,0:T(8,128)S(1)}, f32[128,256]{1,0:T(8,128)S(1)}, u32[]{:S(2)}, u32[]{:S(2)}) %collective-permute-start.14) | collective-permute-done | bytes 131104 | tf_op jit(solution)/shard_map/ppermute | solution.py:233
  68.2 14.5 %factor.1 = (f32[256,256]{1,0:T(8,128)}, f32[256,256]{1,0:T(8,128)}) custom-call(f32[128,256]{1,0:T(8,128)} %get-tuple-element.17.top, f32[128,256]{1,0:T(8,128)} %get-tuple-element.16.bottom), custom_call_target="tpu_custom_call" | custom-call | tf_op jit(solution)/shard_map/factor/pallas_call | solution.py:102
  82.7 1.6 %broadcast_select_fusion = (f32[4,128,640]{2,1,0:T(8,128)S(1)}, f32[4,128,640]{2,1,0:T(8,128)S(1)}) fusion(f32[4,128,640]{2,1,0:T(8,128)} %collective-permute-done.13, pred[]{:T(512)S(6)} %eq.29, f32[1,128,640]{2,1,0:T(8,128)S(1)} %slice_bitcast_fusion, f32[1,128,640]{2,1,0:T(8,128)} %copy-done.3, f32[1,128,640]{2,1,0:T(8,128)} %copy-done.4, ...), kind=kLoop, calls=%fused_computation.1 | loop fusion | flops 1638400 | bytes 5242881 | tf_op jit(solution)/shard_map/jit(_where)/select_n | solution.py:241
  84.4 1.2 %fusion.3 = (f32[640,128]{1,0:T(8,128)S(1)}, f32[640,128]{1,0:T(8,128)S(1)}) fusion(f32[5120,128]{1,0:T(8,128)} %all-gather.3.cloned.1.call-done), kind=kLoop, calls=%fused_computation.19 | loop fusion | bytes 1310720 | tf_op jit(solution)/shard_map/slice | solution.py:197
  85.6 2.9 %copy-done = f32[640,2560]{1,0:T(8,128)S(1)} copy-done((f32[640,2560]{1,0:T(8,128)S(1)}, f32[640,2560]{1,0:T(8,128)}, u32[]{:S(2)}) %copy-start) | copy-done | bytes 6553624
  88.4 13.1 %update.1 = f32[640,2560]{1,0:T(8,128)} custom-call(s32[4]{0:T(128)S(1)} %pad_add_fusion.info, f32[640,2560]{1,0:T(8,128)S(1)} %copy-done, f32[640,128]{1,0:T(8,128)S(1)} %get-tuple-element.15.first_ref, f32[640,128]{1,0:T(8,128)S(1)} %get-tuple-element.14.second_ref, f32[4,128,640]{2,1,0:T(8,128)S(1)} %get-tuple-element.13.b0_ref, ...), custom_call_target="tpu_custom_call" | custom-call | flops 7000000000 | bytes 16000000 | tf_op jit(solution)/shard_map/update/pallas_call | solution.py:155
  (33 shorter events, 3.7 us)
Async XLA Ops:
  6.5 77.8 %all-gather.3.cloned.1.call-start = ((), (), s32[]{:S(2)}) async-start(), calls=%async_computation | async-start | bytes 2949120 | tf_op jit(solution)/shard_map/all_gather | solution.py:196
  7.4 6.1 %collective-permute-start.3 = (f32[128,128]{1,0:T(8,128)S(1)}, f32[128,128]{1,0:T(8,128)S(1)}, u32[]{:S(2)}, u32[]{:S(2)}) collective-permute-start(f32[128,128]{1,0:T(8,128)S(1)} %slice.55), channel_id=1, source_target_pairs={{0,1},{1,0},{8,9},{9,8}} | collective-permute-start | bytes 196616 | tf_op jit(solution)/shard_map/ppermute | solution.py:200
  13.5 12.0 %collective-permute-start.6 = (f32[128,256]{1,0:T(8,128)S(1)}, f32[128,256]{1,0:T(8,128)S(1)}, u32[]{:S(2)}, u32[]{:S(2)}) collective-permute-start(f32[128,256]{1,0:T(8,128)S(1)} %maximum_select_fusion), channel_id=1, source_target_pairs={{0,5},{1,4},{8,13},{9,12}} | collective-permute-start | bytes 393224 | tf_op jit(solution)/shard_map/ppermute | solution.py:203
  19.0 7.9 %collective-permute-start.5 = (f32[128,256]{1,0:T(8,128)S(1)}, f32[128,256]{1,0:T(8,128)S(1)}, u32[]{:S(2)}, u32[]{:S(2)}) collective-permute-start(f32[128,256]{1,0:T(8,128)S(1)} %maximum_select_fusion), channel_id=1, source_target_pairs={{0,6},{1,3},{8,14},{9,11}} | collective-permute-start | bytes 393224 | tf_op jit(solution)/shard_map/ppermute | solution.py:203
  20.3 8.1 %collective-permute-start.4 = (f32[128,256]{1,0:T(8,128)S(1)}, f32[128,256]{1,0:T(8,128)S(1)}, u32[]{:S(2)}, u32[]{:S(2)}) collective-permute-start(f32[128,256]{1,0:T(8,128)S(1)} %maximum_select_fusion), channel_id=1, source_target_pairs={{0,7},{1,2},{8,15},{9,10}} | collective-permute-start | bytes 393224 | tf_op jit(solution)/shard_map/ppermute | solution.py:203
  22.9 5.6 %collective-permute-start.1 = (f32[128,640]{1,0:T(8,128)S(1)}, f32[128,640]{1,0:T(8,128)S(1)}, u32[]{:S(2)}, u32[]{:S(2)}) collective-permute-start(f32[128,640]{1,0:T(8,128)S(1)} %get-tuple-element.9), channel_id=1, source_target_pairs={{0,128},{8,40},{1,129},{9,41},{2,130},{10,42},{3,131},{11,43},{4,1... | collective-permute-start | bytes 983048 | tf_op jit(solution)/shard_map/ppermute | solution.py:213
  24.2 5.3 %collective-permute-start.2 = (f32[128,640]{1,0:T(8,128)S(1)}, f32[128,640]{1,0:T(8,128)S(1)}, u32[]{:S(2)}, u32[]{:S(2)}) collective-permute-start(f32[128,640]{1,0:T(8,128)S(1)} %get-tuple-element.10), channel_id=1, source_target_pairs={{0,192},{8,56},{1,193},{9,57},{2,194},{10,58},{3,195},{11,59},{4,1... | collective-permute-start | bytes 983048 | tf_op jit(solution)/shard_map/ppermute | solution.py:213
  25.5 6.2 %collective-permute-start = (f32[128,640]{1,0:T(8,128)S(1)}, f32[128,640]{1,0:T(8,128)S(1)}, u32[]{:S(2)}, u32[]{:S(2)}) collective-permute-start(f32[128,640]{1,0:T(8,128)S(1)} %get-tuple-element.11), channel_id=1, source_target_pairs={{0,64},{8,24},{1,65},{9,25},{2,66},{10,26},{3,67},{11,27},{4,68},{... | collective-permute-start | bytes 983048 | tf_op jit(solution)/shard_map/ppermute | solution.py:213
  32.8 6.7 %collective-permute-start.9 = (f32[128,896]{1,0:T(8,128)S(1)}, f32[128,896]{1,0:T(8,128)S(1)}, u32[]{:S(2)}, u32[]{:S(2)}) collective-permute-start(f32[128,896]{1,0:T(8,128)S(1)} %pad_maximum_fusion.1), channel_id=1, source_target_pairs={{0,32},{64,96},{128,160},{192,224},{8,136},{24,152},{40,168},{56,1... | collective-permute-start | bytes 1376264 | tf_op jit(solution)/shard_map/ppermute | solution.py:218
  34.1 6.7 %collective-permute-start.8 = (f32[128,896]{1,0:T(8,128)S(1)}, f32[128,896]{1,0:T(8,128)S(1)}, u32[]{:S(2)}, u32[]{:S(2)}) collective-permute-start(f32[128,896]{1,0:T(8,128)S(1)} %pad_maximum_fusion.1), channel_id=1, source_target_pairs={{0,48},{64,112},{128,176},{192,240},{8,200},{24,216},{40,232},{56,... | collective-permute-start | bytes 1376264 | tf_op jit(solution)/shard_map/ppermute | solution.py:218
  35.4 9.0 %collective-permute-start.7 = (f32[128,896]{1,0:T(8,128)S(1)}, f32[128,896]{1,0:T(8,128)S(1)}, u32[]{:S(2)}, u32[]{:S(2)}) collective-permute-start(f32[128,896]{1,0:T(8,128)S(1)} %pad_maximum_fusion.1), channel_id=1, source_target_pairs={{0,16},{64,80},{128,144},{192,208},{8,72},{24,88},{40,104},{56,120... | collective-permute-start | bytes 1376264 | tf_op jit(solution)/shard_map/ppermute | solution.py:218
  44.5 8.7 %collective-permute-start.12 = (f32[128,896]{1,0:T(8,128)S(1)}, f32[128,896]{1,0:T(8,128)S(1)}, u32[]{:S(2)}, u32[]{:S(2)}) collective-permute-start(f32[128,896]{1,0:T(8,128)S(1)} %add_select_fusion), channel_id=1, source_target_pairs={{0,192},{16,208},{32,224},{48,240},{64,0},{80,16},{96,32},{112,48}... | collective-permute-start | bytes 1376264 | tf_op jit(solution)/shard_map/ppermute | solution.py:223
  45.9 9.2 %collective-permute-start.11 = (f32[128,896]{1,0:T(8,128)S(1)}, f32[128,896]{1,0:T(8,128)S(1)}, u32[]{:S(2)}, u32[]{:S(2)}) collective-permute-start(f32[128,896]{1,0:T(8,128)S(1)} %add_select_fusion), channel_id=1, source_target_pairs={{0,128},{16,144},{32,160},{48,176},{64,192},{80,208},{96,224},{112... | collective-permute-start | bytes 1376264 | tf_op jit(solution)/shard_map/ppermute | solution.py:223
  48.7 11.3 %collective-permute-start.10 = (f32[128,896]{1,0:T(8,128)S(1)}, f32[128,896]{1,0:T(8,128)S(1)}, u32[]{:S(2)}, u32[]{:S(2)}) collective-permute-start(f32[128,896]{1,0:T(8,128)S(1)} %add_select_fusion), channel_id=1, source_target_pairs={{0,64},{16,80},{32,96},{48,112},{64,128},{80,144},{96,160},{112,17... | collective-permute-start | bytes 1376264 | tf_op jit(solution)/shard_map/ppermute | solution.py:223
  55.1 5.7 %copy-start.3 = (f32[1,128,640]{2,1,0:T(8,128)}, f32[1,128,640]{2,1,0:T(8,128)S(1)}, u32[]{:S(2)}) copy-start(f32[1,128,640]{2,1,0:T(8,128)S(1)} %slice_bitcast_fusion.1) | copy-start | bytes 983044
  59.9 0.8 copy-start.5
  60.7 0.7 copy-start.4
  61.5 21.2 %collective-permute-start.13 = (f32[4,128,640]{2,1,0:T(8,128)S(1)}, f32[4,128,640]{2,1,0:T(8,128)}, u32[]{:S(2)}, u32[]{:S(2)}) collective-permute-start(f32[4,128,640]{2,1,0:T(8,128)S(1)} %pad_maximum_fusion), channel_id=1, source_target_pairs={{0,8},{8,0},{16,24},{24,16},{32,40},{40,32},{48,56},{56,48},{64,72... | collective-permute-start | bytes 3932168 | tf_op jit(solution)/shard_map/ppermute | solution.py:233
  65.5 1.9 %collective-permute-start.14 = (f32[128,256]{1,0:T(8,128)S(1)}, f32[128,256]{1,0:T(8,128)S(1)}, u32[]{:S(2)}, u32[]{:S(2)}) collective-permute-start(f32[128,256]{1,0:T(8,128)S(1)} %fusion.1), channel_id=1, source_target_pairs={{0,8},{8,0},{16,24},{24,16},{32,40},{40,32},{48,56},{56,48},{64,72... | collective-permute-start | bytes 393224 | tf_op jit(solution)/shard_map/ppermute | solution.py:233
  84.3 1.2 %copy-start.1 = (f32[256,256]{1,0:T(8,128)S(1)}, f32[256,256]{1,0:T(8,128)}, u32[]{:S(2)}) copy-start(f32[256,256]{1,0:T(8,128)} %get-tuple-element.7.l_ref) | copy-start | bytes 786436
  84.3 1.2 %copy-start.2 = (f32[256,256]{1,0:T(8,128)S(1)}, f32[256,256]{1,0:T(8,128)}, u32[]{:S(2)}) copy-start(f32[256,256]{1,0:T(8,128)} %get-tuple-element.8.w_ref) | copy-start | bytes 786436
  85.6 2.9 %copy-start = (f32[640,2560]{1,0:T(8,128)S(1)}, f32[640,2560]{1,0:T(8,128)}, u32[]{:S(2)}) copy-start(f32[640,2560]{1,0:T(8,128)} %k_ref.1) | copy-start | bytes 19660804
Sparse Core Ops, SparseCore 0:
  13.6 39.8 all-gather.2

commit v2 on v1

v2 whole, which is shorter than its diff:
```python
import jax
import jax.numpy as jnp
from jax import lax
from jax.experimental import pallas as pl
from jax.experimental.pallas import tpu as pltpu
from jax.sharding import PartitionSpec as P

NB = 128
HIGHEST = lax.Precision.HIGHEST
F32 = jnp.float32
BF16 = jnp.bfloat16


def bc(v): return jnp.broadcast_to(v,(8,NB))
def eliminate4(full):
    eye=(lax.broadcasted_iota(jnp.int32,(NB,NB),0)==lax.broadcasted_iota(jnp.int32,(NB,NB),1)).astype(F32)
    G=NB//8
    A=[full[8*g:8*g+8,:] for g in range(G)]
    I=[eye[8*g:8*g+8,:] for g in range(G)]
    sub=lax.broadcasted_iota(jnp.int32,(8,NB),0)
    lane=lax.broadcasted_iota(jnp.int32,(8,NB),1)
    outU=[];outW=[]
    for k in range(0,NB,4):
        g0,s=divmod(k,8)
        C=[bc(A[g0][:,k+a:k+a+1]) for a in range(4)]
        D=[[bc(C[a][s+b:s+b+1,:]) if b<=a else None for b in range(4)] for a in range(4)]
        ra=[bc(A[g0][s+b:s+b+1,:]) for b in range(4)]
        ri=[bc(I[g0][s+b:s+b+1,:]) for b in range(4)]
        p00,p10,p11=D[0][0],D[1][0],D[1][1]
        ip=1.0/(p00*p11-p10*p10)
        i00,i10,i11=p11*ip,-p10*ip,p00*ip
        q20,q21,q30,q31=D[2][0],D[2][1],D[3][0],D[3][1]
        t02=i00*q20+i10*q21; t12=i10*q20+i11*q21
        t03=i00*q30+i10*q31; t13=i10*q30+i11*q31
        s22=D[2][2]-(q20*t02+q21*t12)
        s32=D[3][2]-(q30*t02+q31*t12)
        s33=D[3][3]-(q30*t03+q31*t13)
        isd=1.0/(s22*s33-s32*s32)
        j22,j32,j33=s33*isd,-s32*isd,s22*isd
        def solve(r):
            y2=r[2]-(t02*r[0]+t12*r[1])
            y3=r[3]-(t03*r[0]+t13*r[1])
            x2=j22*y2+j32*y3; x3=j32*y2+j33*y3
            x0=(i00*r[0]+i10*r[1])-(t02*x2+t03*x3)
            x1=(i10*r[0]+i11*r[1])-(t12*x2+t13*x3)
            return [x0,x1,x2,x3],y2,y3
        xa,ya2,ya3=solve(ra)
        xi,yi2,yi3=solve(ri)
        for g in range(g0,G):
            if g==g0:
                if s==4: continue
                c=[jnp.where(sub>=4,v,0.0) for v in C]
            else:
                c=[bc(A[g][:,k+a:k+a+1]) for a in range(4)]
            A[g]=A[g]-((c[0]*xa[0]+c[1]*xa[1])+(c[2]*xa[2]+c[3]*xa[3]))
            I[g]=I[g]-((c[0]*xi[0]+c[1]*xi[1])+(c[2]*xi[2]+c[3]*xi[3]))
        def rsq(x):
            r=lax.rsqrt(x); return r*(1.5-0.5*x*r*r)
        def norm2(d00,d10,d11,r0,r1):
            rs0=rsq(d00); l10=d10*rs0; e=d11-l10*l10; rs1=rsq(e)
            return lambda r0,r1:(r0*rs0,(r1-l10*(r0*rs0))*rs1)
        nP=norm2(p00,p10,p11,None,None); nS=norm2(s22,s32,s33,None,None)
        u=[*nP(ra[0],ra[1]),*nS(ya2,ya3)]
        w=[*nP(ri[0],ri[1]),*nS(yi2,yi3)]
        for b in range(4):
            u[b]=jnp.where(lane>=k+b,u[b],0.0)
        if s==0:
            hu,hw=u,w
        else:
            uu=hu+u; ww=hw+w
            ru=uu[7]; rw=ww[7]
            for b in range(6,-1,-1):
                ru=jnp.where(sub==b,uu[b],ru); rw=jnp.where(sub==b,ww[b],rw)
            outU.append(ru); outW.append(rw)
    return jnp.concatenate(outU,0), jnp.concatenate(outW,0)


def mm(a, b):
    return jnp.dot(a, b, precision=HIGHEST, preferred_element_type=F32)


def mmt(a, b):
    return lax.dot_general(a, b, (((1,), (1,)), ((), ())), precision=HIGHEST, preferred_element_type=F32)


def factor_first(core, mine, other, l_ref, w_ref, s_ref):
    flip = core[0] == 1
    top = jnp.where(flip, other[:, :NB], mine[:, :NB])
    bottom = jnp.where(flip, mine[...], other[...])
    u0, w0 = eliminate4(top)
    l10 = mmt(bottom[:, :NB], w0)
    l_ref[:NB, :] = u0.T
    l_ref[NB:, :] = l10
    w_ref[...] = w0
    s_ref[...] = bottom[:, NB:] - mmt(l10, l10)


def factor_second(l_ref, w0_ref, s_ref, l1_ref, w1_ref):
    u1, w1 = eliminate4(s_ref[...])
    l1_ref[...] = u1.T
    w1_ref[:, :NB] = -mm(mm(w1, l_ref[NB:, :]), w0_ref[...])
    w1_ref[:, NB:] = w1


def sds(*shape):
    return jax.ShapeDtypeStruct(shape, F32)


def vmem(n):
    return [pl.BlockSpec(memory_space=pltpu.VMEM)] * n


def cost(flops, moved):
    return pl.CostEstimate(flops=flops, bytes_accessed=moved, transcendentals=0)


def split(v):
    hi = v.astype(BF16)
    return hi, (v - hi.astype(F32)).astype(BF16)


def update_kernel(info, k_ref, *refs):
    pieces, slots, others = refs[0:8], refs[8:12], refs[12:16]
    l0_ref, w0_ref, l1_ref, w1_ref, out_ref, asm, bs, rows, rhi, rlo = refs[16:]
    step = pl.program_id(0)
    y, x, d, z = info[0], info[1], info[2], info[3]
    core = d % 2
    w = bs.shape[1] // 4
    dot = lambda a, b: jnp.dot(a, b, preferred_element_type=F32)

    @pl.when(step == 0)
    def _():
        for ref, shift in zip(pieces, (0, 4, 7, 3, 1, 5, 2, 6)):
            c = (z + shift) % 8
            asm[c % 2 * 4 + c // 2] = ref[...]
        q = asm.shape[1]
        first = asm[0:4].reshape(4 * q, NB)
        second = asm[4:8].reshape(4 * q, NB)
        w0 = w0_ref[...]
        pan0 = mmt(first, w0)
        pan1 = mmt(first, w1_ref[:, :NB]) + mmt(second, w1_ref[:, NB:])
        rows[:, :NB] = pan0
        rows[:, NB:] = pan1
        for i, v in enumerate((pan0, pan1)):
            hi, lo = split(v)
            rhi[:, i * NB : (i + 1) * NB] = hi
            rlo[:, i * NB : (i + 1) * NB] = lo

        @pl.when(d == 0)
        def _():
            rows[:NB, :NB] = l0_ref[:NB, :]
            rows[:NB, NB:] = jnp.zeros((NB, NB), F32)

        @pl.when(d == 1)
        def _():
            rows[:NB, NB:] = l1_ref[...]

        for s in range(4):
            for group, place_p, block in ((slots, jnp.where(core == 0, y, x), core), (others, jnp.where(core == 0, x, y), 1 - core)):
                n = (place_p - s + 4) % 4
                bs[pl.ds(pl.multiple_of(block * NB, NB), NB), pl.ds(pl.multiple_of(n * w, NB), w)] = group[s][...]

    width = out_ref.shape[1]
    here = pl.ds(pl.multiple_of(step * width, NB), width)
    b0 = bs[:NB, here]
    b1 = bs[NB:, here]
    c0 = mm(w0_ref[...], b0)
    c1 = mm(w1_ref[:, :NB], b0) + mm(w1_ref[:, NB:], b1)
    chi, clo = split(jnp.concatenate([c0, c1], 0))
    prod = dot(rhi[...], chi) + (dot(rlo[...], chi) + dot(rhi[...], clo))
    out_ref[...] = k_ref[...] - prod

    @pl.when(d < 2)
    def _():
        out_ref[:NB, :] = jnp.zeros((NB, width), F32)

    @pl.when((step == 0) & (z == 0))
    def _():
        out_ref[:, :NB] = rows[:, :NB]

    @pl.when((step == 0) & (z == 1))
    def _():
        out_ref[:, :NB] = rows[:, NB:]


def update(info, kernel, pieces, slots, others, l0, w0, l1, w1):
    r, c = kernel.shape
    w = c // STEPS
    operands = [*pieces, *slots, *others, l0, w0, l1, w1]
    whole = [pl.BlockSpec(v.shape, lambda n, s: (0, 0)) for v in operands]
    return pl.pallas_call(
        update_kernel,
        out_shape=sds(r, c),
        grid_spec=pltpu.PrefetchScalarGridSpec(
            num_scalar_prefetch=1,
            grid=(STEPS,),
            in_specs=[pl.BlockSpec((r, w), lambda n, s: (0, n)), *whole],
            out_specs=pl.BlockSpec((r, w), lambda n, s: (0, n)),
            scratch_shapes=[
                pltpu.VMEM((8, r // 4, NB), F32),
                pltpu.VMEM((2 * NB, c), F32),
                pltpu.VMEM((r, 2 * NB), F32),
                pltpu.VMEM((r, 2 * NB), BF16),
                pltpu.VMEM((r, 2 * NB), BF16),
            ],
        ),
        compiler_params=pltpu.CompilerParams(
            dimension_semantics=("arbitrary",), vmem_limit_bytes=40 * 1024 * 1024
        ),
        cost_estimate=cost(5_000_000_000, 18_000_000),
        name="update",
    )(info, kernel, *operands)


STEPS = 5


def place(core, p, q):
    return p * 8 + q * 2 if core == 0 else q * 8 + p * 2 + 1


BOTH = ("row", "col")


def local(kernel):
    row = lax.axis_index("row")
    z = lax.axis_index("col")
    y, x, core = row // 8, row // 2 % 4, row % 2
    p = jnp.where(core == 0, y, x)
    q = jnp.where(core == 0, x, y)
    info = jnp.stack([y, x, row, z]).astype(jnp.int32)

    own = kernel[:NB, :NB]
    other = lax.ppermute(own, BOTH, [(r * 8 + a, r * 8 + 1 - a) for r in (0, 1) for a in (0, 1)])
    corner = jnp.where(z == 0, jnp.concatenate([own, other], 1), jnp.concatenate([other, own], 1))
    got = [
        lax.ppermute(corner, BOTH, [(r * 8 + a, r * 8 + b) for r in (0, 1) for a, b in ((0, 8 - n), (1, 1 + n))])
        for n in (3, 2, 1)
    ]
    corner = jnp.where(z < 2, corner, got[0] + got[1] + got[2])
    got = [
        lax.ppermute(corner, "row", [(place(c, 0, 0), place(c, 0, n)) for c in (0, 1)]) for n in (2, 1, 3)
    ]
    corner = jnp.where(q == 0, corner, got[0] + got[1] + got[2])
    got = [
        lax.ppermute(corner, "row", [(place(c, 0, i), place(c, n, i)) for c in (0, 1) for i in range(4)])
        for n in (2, 1, 3)
    ]
    corner = jnp.where(p == 0, corner, got[0] + got[1] + got[2])
    swap = lambda v: lax.ppermute(v, "row", [(i, i ^ 1) for i in range(32)])
    corner_other = swap(corner)

    first = kernel[:, :NB]
    r4 = kernel.shape[0] // 4
    got = [lax.ppermute(first[j * r4 : (j + 1) * r4], "col", [(0, 2 * j), (1, 2 * j + 1)]) for j in (1, 2, 3)]
    piece = jnp.where(z < 2, first[:r4], got[0] + got[1] + got[2])
    shift = lambda v, n: lax.ppermute(v, "col", [((i + n) % 8, i) for i in range(8)])
    piece4 = shift(piece, 4)
    pair = jnp.concatenate([piece, piece4], 0)
    pairs = [pair] + [shift(pair, n) for n in (7, 1, 2)]
    pieces = [v for a in pairs for v in (a[:r4], a[r4:])]

    w = kernel.shape[1] // 4
    quarters = [kernel[:NB, j * w : (j + 1) * w] for j in range(4)]
    got = [
        lax.ppermute(quarters[j], "row", [(place(c, 0, 0), place(c, j, 0)) for c in (0, 1)]) for j in (2, 1, 3)
    ]
    quarter = jnp.where(p == 0, quarters[0], got[0] + got[1] + got[2])
    got = [
        lax.ppermute(quarter, "row", [(place(c, j, 0), place(c, j, n)) for c in (0, 1) for j in range(4)])
        for n in (2, 1, 3)
    ]
    quarter = jnp.where(q == 0, quarter, got[0] + got[1] + got[2])
    slots = [quarter] + [
        lax.ppermute(
            quarter,
            "row",
            [(place(c, j, i), place(c, (j + n) % 4, i)) for c in (0, 1) for j in range(4) for i in range(4)],
        )
        for n in (1, 2, 3)
    ]

    l0, w0, s = pl.pallas_call(
        factor_first,
        in_specs=[pl.BlockSpec(memory_space=pltpu.SMEM)] + vmem(2),
        out_specs=vmem(3),
        out_shape=[sds(2 * NB, NB), sds(NB, NB), sds(NB, NB)],
        cost_estimate=cost(1_000_000_000, 1_000_000),
        name="factor_first",
    )(core.astype(jnp.int32)[None], corner, corner_other)
    s, slots = lax.optimization_barrier((s, slots))
    others = [swap(v) for v in slots]
    l1, w1 = pl.pallas_call(
        factor_second,
        in_specs=vmem(3),
        out_specs=vmem(2),
        out_shape=[sds(NB, NB), sds(NB, 2 * NB)],
        cost_estimate=cost(1_000_000_000, 1_000_000),
        name="factor_second",
    )(l0, w0, s)
    return update(info, kernel, pieces, slots, others, l0, w0, l1, w1)


def solution(mesh):
    return jax.shard_map(
        local,
        mesh=mesh,
        in_specs=(P("row", "col"),),
        out_specs=P("row", "col"),
        check_vma=False,
    )
```

time: 109 us -> 105 us (0.963)
  the two profiles are of different devices: /device:TPU:1 before, /device:TPU:45 now
where the time goes in v2:
time: 105 us; the launch traced here: 104 us
  starting transfers between devices  60.5 us (58%)
  Pallas kernels  26.7 us (25%)
  local copies, waits for them, and re-layouts  11.3 us (11%)
  waiting for transfers between devices  2.73 us (3%)
  other arithmetic  2.25 us (2%)
    ppermute x4, starting transfers between devices, local(): lax.ppermute(v, 'col', [((i + n) % 8, i) for i in range(8)])  19.4 us
    ppermute x3, starting transfers between devices, local(): lax.ppermute(quarter, 'row', [(place(c, j, i), place(c, (j + n) % 4, i))...  13.4 us
    pallas_call x1, Pallas kernels, update(): pl.pallas_call(update_kernel, out_shape=sds(r, c), grid_spec=pltpu.Prefet...  10.7 us
    ppermute x3, starting transfers between devices, local(): lax.ppermute(first[j * r4:(j + 1) * r4], 'col', [(0, 2 * j), (1, 2 * j +...  10.5 us
    pallas_call x1, Pallas kernels, local(): pl.pallas_call(factor_first, in_specs=[pl.BlockSpec(memory_space=pltpu.SM...  8.11 us
    pallas_call x1, Pallas kernels, local(): pl.pallas_call(factor_second, in_specs=vmem(3), out_specs=vmem(2), out_sh...  7.9 us
    unnamed x14, local copies, waits for them, and re-layouts  6.35 us
    ppermute x5, starting transfers between devices, local(): swap = lambda v: lax.ppermute(v, 'row', [(i, i ^ 1) for i in range(32)])  5.21 us
  transfers between devices with their start and end apart: 31, of which 2 were waited for; matrix products, arithmetic and copies ran while one was open for 6% of the time, Pallas kernels for 15%

profile of v2, /device:TPU:45, one launch (start us, length us, event | category | flops | bytes accessed | tf_op | source)
XLA Modules:
  0.0 104.0 jit_solution(14377670933827302781)
XLA Ops:
  0.0 0.8 slice.60
  1.5 1.0 fusion.1
  2.5 7.9 %collective-permute-start.1 = (f32[160,128]{1,0:T(8,128)S(1)}, f32[160,128]{1,0:T(8,128)S(1)}, u32[]{:S(2)}, u32[]{:S(2)}) collective-permute-start(f32[160,128]{1,0:T(8,128)S(1)} %get-tuple-element.28), channel_id=1, source_target_pairs={{0,4},{1,5},{8,12},{9,13},{16,20},{17,21},{24,28},{25,29},{32,36},... | collective-permute-start | bytes 245768 | tf_op jit(solution)/shard_map/ppermute | solution.py:255
  10.4 1.3 %collective-permute-start.2 = (f32[160,128]{1,0:T(8,128)S(1)}, f32[160,128]{1,0:T(8,128)S(1)}, u32[]{:S(2)}, u32[]{:S(2)}) collective-permute-start(f32[160,128]{1,0:T(8,128)S(1)} %get-tuple-element.29), channel_id=1, source_target_pairs={{0,6},{1,7},{8,14},{9,15},{16,22},{17,23},{24,30},{25,31},{32,38},... | collective-permute-start | bytes 245768 | tf_op jit(solution)/shard_map/ppermute | solution.py:255
  11.7 1.3 %collective-permute-start = (f32[160,128]{1,0:T(8,128)S(1)}, f32[160,128]{1,0:T(8,128)S(1)}, u32[]{:S(2)}, u32[]{:S(2)}) collective-permute-start(f32[160,128]{1,0:T(8,128)S(1)} %get-tuple-element.30), channel_id=1, source_target_pairs={{0,2},{1,3},{8,10},{9,11},{16,18},{17,19},{24,26},{25,27},{32,34},... | collective-permute-start | bytes 245768 | tf_op jit(solution)/shard_map/ppermute | solution.py:255
  13.7 1.2 %fusion = (f32[128,640]{1,0:T(8,128)S(1)}, f32[128,640]{1,0:T(8,128)S(1)}, f32[128,640]{1,0:T(8,128)S(1)}) fusion(f32[640,2560]{1,0:T(8,128)} %k_ref.1), kind=kLoop, calls=%fused_computation.9 | loop fusion | bytes 1966080 | tf_op jit(solution)/shard_map/slice | solution.py:264
  15.0 0.7 collective-permute-start.19
  16.5 0.7 collective-permute-start.20
  18.6 0.9 add_select_fusion.5.refs_0_
  19.5 1.9 %collective-permute-start.3 = (f32[160,128]{1,0:T(8,128)S(1)}, f32[160,128]{1,0:T(8,128)S(1)}, u32[]{:S(2)}, u32[]{:S(2)}) collective-permute-start(f32[160,128]{1,0:T(8,128)S(1)} %add_select_fusion.5.refs_0_), channel_id=1, source_target_pairs={{4,0},{5,1},{6,2},{7,3},{0,4},{1,5},{2,6},{3,7},{12,8},{13,9},{14,... | collective-permute-start | bytes 245768 | tf_op jit(solution)/shard_map/ppermute | solution.py:257
  23.5 1.1 %add_select_fusion.1 = f32[128,640]{1,0:T(8,128)S(1)} fusion(f32[128,640]{1,0:T(8,128)S(1)} %collective-permute-done.20, f32[128,640]{1,0:T(8,128)S(1)} %collective-permute-done.18, f32[128,640]{1,0:T(8,128)S(1)} %collective-permute-done.19, f32[640,2560]{1,0:T(8,128)} %k_ref.1, pred[]{:T(512)S(6)} %eq.19), kind=kLoop, calls=%fused_computation.1 | loop fusion | flops 245760 | bytes 1638401 | tf_op jit(solution)/shard_map/jit(_where)/select_n | solution.py:268
  24.5 0.7 collective-permute-start.23
  25.2 1.6 %collective-permute-done.3.refs_1_ = f32[160,128]{1,0:T(8,128)S(1)} collective-permute-done((f32[160,128]{1,0:T(8,128)S(1)}, f32[160,128]{1,0:T(8,128)S(1)}, u32[]{:S(2)}, u32[]{:S(2)}) %collective-permute-start.3) | collective-permute-done | bytes 81952 | tf_op jit(solution)/shard_map/ppermute | solution.py:257
  26.9 1.3 %collective-permute-start.22 = (f32[128,640]{1,0:T(8,128)S(1)}, f32[128,640]{1,0:T(8,128)S(1)}, u32[]{:S(2)}, u32[]{:S(2)}) collective-permute-start(f32[128,640]{1,0:T(8,128)S(1)} %add_select_fusion.1), channel_id=1, source_target_pairs={{0,16},{64,80},{128,144},{192,208},{8,72},{24,88},{40,104},{56,120... | collective-permute-start | bytes 983048 | tf_op jit(solution)/shard_map/ppermute | solution.py:270
  28.9 2.3 %collective-permute-start.6 = (f32[320,128]{1,0:T(8,128)S(1)}, f32[320,128]{1,0:T(8,128)S(1)}, u32[]{:S(2)}, u32[]{:S(2)}) collective-permute-start(f32[320,128]{1,0:T(8,128)S(1)} %pad_maximum_fusion), channel_id=1, source_target_pairs={{2,0},{3,1},{4,2},{5,3},{6,4},{7,5},{0,6},{1,7},{10,8},{11,9},{12,... | collective-permute-start | bytes 491528 | tf_op jit(solution)/shard_map/ppermute | solution.py:257
  31.2 3.9 %collective-permute-start.5 = (f32[320,128]{1,0:T(8,128)S(1)}, f32[320,128]{1,0:T(8,128)}, u32[]{:S(2)}, u32[]{:S(2)}) collective-permute-start(f32[320,128]{1,0:T(8,128)S(1)} %pad_maximum_fusion), channel_id=1, source_target_pairs={{1,0},{2,1},{3,2},{4,3},{5,4},{6,5},{7,6},{0,7},{9,8},{10,9},{11,1... | collective-permute-start | bytes 491528 | tf_op jit(solution)/shard_map/ppermute | solution.py:257
  36.5 1.3 %collective-permute-start.14 = (f32[128,256]{1,0:T(8,128)S(1)}, f32[128,256]{1,0:T(8,128)S(1)}, u32[]{:S(2)}, u32[]{:S(2)}) collective-permute-start(f32[128,256]{1,0:T(8,128)S(1)} %add_select_fusion.3), channel_id=1, source_target_pairs={{0,128},{16,144},{32,160},{48,176},{8,40},{72,104},{136,168},{200,... | collective-permute-start | bytes 393224 | tf_op jit(solution)/shard_map/ppermute | solution.py:246
  38.2 12.4 %collective-permute-start.25 = (f32[128,640]{1,0:T(8,128)S(1)}, f32[128,640]{1,0:T(8,128)S(1)}, u32[]{:S(2)}, u32[]{:S(2)}) collective-permute-start(f32[128,640]{1,0:T(8,128)S(1)} %add_select_fusion.refs_8_), channel_id=1, source_target_pairs={{0,128},{16,144},{32,160},{48,176},{64,192},{80,208},{96,224},{112... | collective-permute-start | bytes 983048 | tf_op jit(solution)/shard_map/ppermute | solution.py:275
  51.4 3.7 %collective-permute-start.17 = (f32[128,256]{1,0:T(8,128)S(1)}, f32[128,256]{1,0:T(8,128)S(1)}, u32[]{:S(2)}, u32[]{:S(2)}) collective-permute-start(f32[128,256]{1,0:T(8,128)S(1)} %add_select_fusion.2.mine), channel_id=1, source_target_pairs={{0,8},{8,0},{16,24},{24,16},{32,40},{40,32},{48,56},{56,48},{64,72... | collective-permute-start | bytes 393224 | tf_op jit(solution)/shard_map/ppermute | solution.py:250
  55.2 1.0 collective-permute-done.17.other
  56.1 11.3 %collective-permute-start.4 = (f32[320,128]{1,0:T(8,128)S(1)}, f32[320,128]{1,0:T(8,128)}, u32[]{:S(2)}, u32[]{:S(2)}) collective-permute-start(f32[320,128]{1,0:T(8,128)S(1)} %pad_maximum_fusion), channel_id=1, source_target_pairs={{7,0},{0,1},{1,2},{2,3},{3,4},{4,5},{5,6},{6,7},{15,8},{8,9},{9,10... | collective-permute-start | bytes 491528 | tf_op jit(solution)/shard_map/ppermute | solution.py:257
  67.4 8.1 %factor_first.1 = (f32[256,128]{1,0:T(8,128)}, f32[128,128]{1,0:T(8,128)}, f32[128,128]{1,0:T(8,128)}) custom-call(s32[1]{0:T(128)} %bitcast.4.core, f32[128,256]{1,0:T(8,128)} %copy-done.5, f32[128,256]{1,0:T(8,128)} %copy-done.6), custom_call_target="tpu_custom_call" | custom-call | flops 1000000000 | bytes 1000000 | tf_op jit(solution)/shard_map/factor_first/pallas_call | solution.py:283
  75.6 0.7 collective-permute-start.27
  77.1 0.9 fusion.3
  78.0 0.9 fusion.4
  79.0 7.9 %factor_second.1 = (f32[128,128]{1,0:T(8,128)}, f32[128,256]{1,0:T(8,128)}) custom-call(f32[256,128]{1,0:T(8,128)} %get-tuple-element.20.l_ref.refs_16_, f32[128,128]{1,0:T(8,128)} %get-tuple-element.21.w0_ref.refs_17_, f32[128,128]{1,0:T(8,128)} %get-tuple-element.22.s_ref), custom_call_target="tpu_custom_call" | custom-call | flops 1000000000 | bytes 1000000 | tf_op jit(solution)/shard_map/factor_second/pallas_call | solution.py:293
  86.9 2.9 %copy-done = f32[640,2560]{1,0:T(8,128)S(1)} copy-done((f32[640,2560]{1,0:T(8,128)S(1)}, f32[640,2560]{1,0:T(8,128)}, u32[]{:S(2)}) %copy-start) | copy-done | bytes 6553624
  89.8 0.9 copy-done.1
  90.7 0.9 copy-done.2
  91.6 0.8 copy-done.3
  92.4 0.8 copy-done.4
  93.3 10.7 %update.1 = f32[640,2560]{1,0:T(8,128)} custom-call(s32[4]{0:T(128)S(1)} %pad_add_fusion.info, f32[640,2560]{1,0:T(8,128)S(1)} %copy-done, f32[160,128]{1,0:T(8,128)S(1)} %add_select_fusion.5.refs_0_, f32[160,128]{1,0:T(8,128)S(1)} %collective-permute-done.3.refs_1_, f32[160,128]{1,0:T(8,128)S(1)} %get-tuple-element.36.refs_2_, ...), custom_call_target="tpu_custom_call" | custom-call | flops 5000000000 | bytes 18000000 | tf_op jit(solution)/shard_map/update/pallas_call | solution.py:191
  (62 shorter events, 9.6 us)
Async XLA Ops:
  0.8 12.2 %collective-permute-start.7 = (f32[128,128]{1,0:T(8,128)S(1)}, f32[128,128]{1,0:T(8,128)S(1)}, u32[]{:S(2)}, u32[]{:S(2)}) collective-permute-start(f32[128,128]{1,0:T(8,128)S(1)} %slice.60), channel_id=1, source_target_pairs={{0,1},{1,0},{8,9},{9,8}} | collective-permute-start | bytes 196616 | tf_op jit(solution)/shard_map/ppermute | solution.py:234
  2.5 13.3 %collective-permute-start.1 = (f32[160,128]{1,0:T(8,128)S(1)}, f32[160,128]{1,0:T(8,128)S(1)}, u32[]{:S(2)}, u32[]{:S(2)}) collective-permute-start(f32[160,128]{1,0:T(8,128)S(1)} %get-tuple-element.28), channel_id=1, source_target_pairs={{0,4},{1,5},{8,12},{9,13},{16,20},{17,21},{24,28},{25,29},{32,36},... | collective-permute-start | bytes 245768 | tf_op jit(solution)/shard_map/ppermute | solution.py:255
  10.4 6.1 %collective-permute-start.2 = (f32[160,128]{1,0:T(8,128)S(1)}, f32[160,128]{1,0:T(8,128)S(1)}, u32[]{:S(2)}, u32[]{:S(2)}) collective-permute-start(f32[160,128]{1,0:T(8,128)S(1)} %get-tuple-element.29), channel_id=1, source_target_pairs={{0,6},{1,7},{8,14},{9,15},{16,22},{17,23},{24,30},{25,31},{32,38},... | collective-permute-start | bytes 245768 | tf_op jit(solution)/shard_map/ppermute | solution.py:255
  11.7 5.5 %collective-permute-start = (f32[160,128]{1,0:T(8,128)S(1)}, f32[160,128]{1,0:T(8,128)S(1)}, u32[]{:S(2)}, u32[]{:S(2)}) collective-permute-start(f32[160,128]{1,0:T(8,128)S(1)} %get-tuple-element.30), channel_id=1, source_target_pairs={{0,2},{1,3},{8,10},{9,11},{16,18},{17,19},{24,26},{25,27},{32,34},... | collective-permute-start | bytes 245768 | tf_op jit(solution)/shard_map/ppermute | solution.py:255
  13.1 4.8 %collective-permute-start.10 = (f32[128,256]{1,0:T(8,128)S(1)}, f32[128,256]{1,0:T(8,128)S(1)}, u32[]{:S(2)}, u32[]{:S(2)}) collective-permute-start(f32[128,256]{1,0:T(8,128)S(1)} %maximum_select_fusion), channel_id=1, source_target_pairs={{0,7},{1,2},{8,15},{9,10}} | collective-permute-start | bytes 393224 | tf_op jit(solution)/shard_map/ppermute | solution.py:237
  15.0 7.1 %collective-permute-start.19 = (f32[128,640]{1,0:T(8,128)S(1)}, f32[128,640]{1,0:T(8,128)S(1)}, u32[]{:S(2)}, u32[]{:S(2)}) collective-permute-start(f32[128,640]{1,0:T(8,128)S(1)} %get-tuple-element.25), channel_id=1, source_target_pairs={{0,64},{8,24},{1,65},{9,25},{2,66},{10,26},{3,67},{11,27},{4,68},{... | collective-permute-start | bytes 983048 | tf_op jit(solution)/shard_map/ppermute | solution.py:266
  15.8 7.0 %collective-permute-start.18 = (f32[128,640]{1,0:T(8,128)S(1)}, f32[128,640]{1,0:T(8,128)S(1)}, u32[]{:S(2)}, u32[]{:S(2)}) collective-permute-start(f32[128,640]{1,0:T(8,128)S(1)} %get-tuple-element.26), channel_id=1, source_target_pairs={{0,128},{8,40},{1,129},{9,41},{2,130},{10,42},{3,131},{11,43},{4,1... | collective-permute-start | bytes 983048 | tf_op jit(solution)/shard_map/ppermute | solution.py:266
  16.5 7.0 %collective-permute-start.20 = (f32[128,640]{1,0:T(8,128)S(1)}, f32[128,640]{1,0:T(8,128)S(1)}, u32[]{:S(2)}, u32[]{:S(2)}) collective-permute-start(f32[128,640]{1,0:T(8,128)S(1)} %get-tuple-element.27), channel_id=1, source_target_pairs={{0,192},{8,56},{1,193},{9,57},{2,194},{10,58},{3,195},{11,59},{4,1... | collective-permute-start | bytes 983048 | tf_op jit(solution)/shard_map/ppermute | solution.py:266
  17.2 2.3 %collective-permute-start.9 = (f32[128,256]{1,0:T(8,128)S(1)}, f32[128,256]{1,0:T(8,128)S(1)}, u32[]{:S(2)}, u32[]{:S(2)}) collective-permute-start(f32[128,256]{1,0:T(8,128)S(1)} %maximum_select_fusion), channel_id=1, source_target_pairs={{0,6},{1,3},{8,14},{9,11}} | collective-permute-start | bytes 393224 | tf_op jit(solution)/shard_map/ppermute | solution.py:237
  17.9 3.5 %collective-permute-start.8 = (f32[128,256]{1,0:T(8,128)S(1)}, f32[128,256]{1,0:T(8,128)S(1)}, u32[]{:S(2)}, u32[]{:S(2)}) collective-permute-start(f32[128,256]{1,0:T(8,128)S(1)} %maximum_select_fusion), channel_id=1, source_target_pairs={{0,5},{1,4},{8,13},{9,12}} | collective-permute-start | bytes 393224 | tf_op jit(solution)/shard_map/ppermute | solution.py:237
  19.5 7.4 %collective-permute-start.3 = (f32[160,128]{1,0:T(8,128)S(1)}, f32[160,128]{1,0:T(8,128)S(1)}, u32[]{:S(2)}, u32[]{:S(2)}) collective-permute-start(f32[160,128]{1,0:T(8,128)S(1)} %add_select_fusion.5.refs_0_), channel_id=1, source_target_pairs={{4,0},{5,1},{6,2},{7,3},{0,4},{1,5},{2,6},{3,7},{12,8},{13,9},{14,... | collective-permute-start | bytes 245768 | tf_op jit(solution)/shard_map/ppermute | solution.py:257
  21.4 6.8 %collective-permute-start.13 = (f32[128,256]{1,0:T(8,128)S(1)}, f32[128,256]{1,0:T(8,128)S(1)}, u32[]{:S(2)}, u32[]{:S(2)}) collective-permute-start(f32[128,256]{1,0:T(8,128)S(1)} %add_select_fusion.4), channel_id=1, source_target_pairs={{0,48},{8,200},{1,49},{9,201},{2,50},{10,202},{3,51},{11,203},{4,5... | collective-permute-start | bytes 393224 | tf_op jit(solution)/shard_map/ppermute | solution.py:242
  22.1 6.8 %collective-permute-start.12 = (f32[128,256]{1,0:T(8,128)S(1)}, f32[128,256]{1,0:T(8,128)S(1)}, u32[]{:S(2)}, u32[]{:S(2)}) collective-permute-start(f32[128,256]{1,0:T(8,128)S(1)} %add_select_fusion.4), channel_id=1, source_target_pairs={{0,16},{8,72},{1,17},{9,73},{2,18},{10,74},{3,19},{11,75},{4,20},{... | collective-permute-start | bytes 393224 | tf_op jit(solution)/shard_map/ppermute | solution.py:242
  22.8 8.4 %collective-permute-start.11 = (f32[128,256]{1,0:T(8,128)S(1)}, f32[128,256]{1,0:T(8,128)S(1)}, u32[]{:S(2)}, u32[]{:S(2)}) collective-permute-start(f32[128,256]{1,0:T(8,128)S(1)} %add_select_fusion.4), channel_id=1, source_target_pairs={{0,32},{8,136},{1,33},{9,137},{2,34},{10,138},{3,35},{11,139},{4,3... | collective-permute-start | bytes 393224 | tf_op jit(solution)/shard_map/ppermute | solution.py:242
  24.5 10.6 %collective-permute-start.23 = (f32[128,640]{1,0:T(8,128)S(1)}, f32[128,640]{1,0:T(8,128)S(1)}, u32[]{:S(2)}, u32[]{:S(2)}) collective-permute-start(f32[128,640]{1,0:T(8,128)S(1)} %add_select_fusion.1), channel_id=1, source_target_pairs={{0,48},{64,112},{128,176},{192,240},{8,200},{24,216},{40,232},{56,... | collective-permute-start | bytes 983048 | tf_op jit(solution)/shard_map/ppermute | solution.py:270
  26.9 9.0 %collective-permute-start.22 = (f32[128,640]{1,0:T(8,128)S(1)}, f32[128,640]{1,0:T(8,128)S(1)}, u32[]{:S(2)}, u32[]{:S(2)}) collective-permute-start(f32[128,640]{1,0:T(8,128)S(1)} %add_select_fusion.1), channel_id=1, source_target_pairs={{0,16},{64,80},{128,144},{192,208},{8,72},{24,88},{40,104},{56,120... | collective-permute-start | bytes 983048 | tf_op jit(solution)/shard_map/ppermute | solution.py:270
  28.2 8.4 %collective-permute-start.21 = (f32[128,640]{1,0:T(8,128)S(1)}, f32[128,640]{1,0:T(8,128)S(1)}, u32[]{:S(2)}, u32[]{:S(2)}) collective-permute-start(f32[128,640]{1,0:T(8,128)S(1)} %add_select_fusion.1), channel_id=1, source_target_pairs={{0,32},{64,96},{128,160},{192,224},{8,136},{24,152},{40,168},{56,1... | collective-permute-start | bytes 983048 | tf_op jit(solution)/shard_map/ppermute | solution.py:270
  28.9 22.6 %collective-permute-start.6 = (f32[320,128]{1,0:T(8,128)S(1)}, f32[320,128]{1,0:T(8,128)S(1)}, u32[]{:S(2)}, u32[]{:S(2)}) collective-permute-start(f32[320,128]{1,0:T(8,128)S(1)} %pad_maximum_fusion), channel_id=1, source_target_pairs={{2,0},{3,1},{4,2},{5,3},{6,4},{7,5},{0,6},{1,7},{10,8},{11,9},{12,... | collective-permute-start | bytes 491528 | tf_op jit(solution)/shard_map/ppermute | solution.py:257
  31.2 45.6 %collective-permute-start.5 = (f32[320,128]{1,0:T(8,128)S(1)}, f32[320,128]{1,0:T(8,128)}, u32[]{:S(2)}, u32[]{:S(2)}) collective-permute-start(f32[320,128]{1,0:T(8,128)S(1)} %pad_maximum_fusion), channel_id=1, source_target_pairs={{1,0},{2,1},{3,2},{4,3},{5,4},{6,5},{7,6},{0,7},{9,8},{10,9},{11,1... | collective-permute-start | bytes 491528 | tf_op jit(solution)/shard_map/ppermute | solution.py:257
  35.2 2.7 %collective-permute-start.16 = (f32[128,256]{1,0:T(8,128)S(1)}, f32[128,256]{1,0:T(8,128)S(1)}, u32[]{:S(2)}, u32[]{:S(2)}) collective-permute-start(f32[128,256]{1,0:T(8,128)S(1)} %add_select_fusion.3), channel_id=1, source_target_pairs={{0,192},{16,208},{32,224},{48,240},{8,56},{72,120},{136,184},{200,... | collective-permute-start | bytes 393224 | tf_op jit(solution)/shard_map/ppermute | solution.py:246
  35.8 2.4 %collective-permute-start.15 = (f32[128,256]{1,0:T(8,128)S(1)}, f32[128,256]{1,0:T(8,128)S(1)}, u32[]{:S(2)}, u32[]{:S(2)}) collective-permute-start(f32[128,256]{1,0:T(8,128)S(1)} %add_select_fusion.3), channel_id=1, source_target_pairs={{0,64},{16,80},{32,96},{48,112},{8,24},{72,88},{136,152},{200,216}... | collective-permute-start | bytes 393224 | tf_op jit(solution)/shard_map/ppermute | solution.py:246
  36.5 14.2 %collective-permute-start.14 = (f32[128,256]{1,0:T(8,128)S(1)}, f32[128,256]{1,0:T(8,128)S(1)}, u32[]{:S(2)}, u32[]{:S(2)}) collective-permute-start(f32[128,256]{1,0:T(8,128)S(1)} %add_select_fusion.3), channel_id=1, source_target_pairs={{0,128},{16,144},{32,160},{48,176},{8,40},{72,104},{136,168},{200,... | collective-permute-start | bytes 393224 | tf_op jit(solution)/shard_map/ppermute | solution.py:246
  37.9 37.6 %collective-permute-start.26 = (f32[128,640]{1,0:T(8,128)S(1)}, f32[128,640]{1,0:T(8,128)S(1)}, u32[]{:S(2)}, u32[]{:S(2)}) collective-permute-start(f32[128,640]{1,0:T(8,128)S(1)} %add_select_fusion.refs_8_), channel_id=1, source_target_pairs={{0,192},{16,208},{32,224},{48,240},{64,0},{80,16},{96,32},{112,48}... | collective-permute-start | bytes 983048 | tf_op jit(solution)/shard_map/ppermute | solution.py:275
  38.2 37.3 %collective-permute-start.25 = (f32[128,640]{1,0:T(8,128)S(1)}, f32[128,640]{1,0:T(8,128)S(1)}, u32[]{:S(2)}, u32[]{:S(2)}) collective-permute-start(f32[128,640]{1,0:T(8,128)S(1)} %add_select_fusion.refs_8_), channel_id=1, source_target_pairs={{0,128},{16,144},{32,160},{48,176},{64,192},{80,208},{96,224},{112... | collective-permute-start | bytes 983048 | tf_op jit(solution)/shard_map/ppermute | solution.py:275
  50.7 24.8 %collective-permute-start.24 = (f32[128,640]{1,0:T(8,128)S(1)}, f32[128,640]{1,0:T(8,128)S(1)}, u32[]{:S(2)}, u32[]{:S(2)}) collective-permute-start(f32[128,640]{1,0:T(8,128)S(1)} %add_select_fusion.refs_8_), channel_id=1, source_target_pairs={{0,64},{16,80},{32,96},{48,112},{64,128},{80,144},{96,160},{112,17... | collective-permute-start | bytes 983048 | tf_op jit(solution)/shard_map/ppermute | solution.py:275
  51.4 16.0 %copy-start.5 = (f32[128,256]{1,0:T(8,128)}, f32[128,256]{1,0:T(8,128)S(1)}, u32[]{:S(2)}) copy-start(f32[128,256]{1,0:T(8,128)S(1)} %add_select_fusion.2.mine) | copy-start | bytes 393220
  51.4 4.7 %collective-permute-start.17 = (f32[128,256]{1,0:T(8,128)S(1)}, f32[128,256]{1,0:T(8,128)S(1)}, u32[]{:S(2)}, u32[]{:S(2)}) collective-permute-start(f32[128,256]{1,0:T(8,128)S(1)} %add_select_fusion.2.mine), channel_id=1, source_target_pairs={{0,8},{8,0},{16,24},{24,16},{32,40},{40,32},{48,56},{56,48},{64,72... | collective-permute-start | bytes 393224 | tf_op jit(solution)/shard_map/ppermute | solution.py:250
  56.1 21.9 %collective-permute-start.4 = (f32[320,128]{1,0:T(8,128)S(1)}, f32[320,128]{1,0:T(8,128)}, u32[]{:S(2)}, u32[]{:S(2)}) collective-permute-start(f32[320,128]{1,0:T(8,128)S(1)} %pad_maximum_fusion), channel_id=1, source_target_pairs={{7,0},{0,1},{1,2},{2,3},{3,4},{4,5},{5,6},{6,7},{15,8},{8,9},{9,10... | collective-permute-start | bytes 491528 | tf_op jit(solution)/shard_map/ppermute | solution.py:257
  75.6 11.3 %collective-permute-start.27 = (f32[128,640]{1,0:T(8,128)S(1)}, f32[128,640]{1,0:T(8,128)S(1)}, u32[]{:S(2)}, u32[]{:S(2)}) collective-permute-start(f32[128,640]{1,0:T(8,128)S(1)} %add_select_fusion.refs_8_), channel_id=1, source_target_pairs={{0,8},{8,0},{16,24},{24,16},{32,40},{40,32},{48,56},{56,48},{64,72... | collective-permute-start | bytes 983048 | tf_op jit(solution)/shard_map/ppermute | solution.py:250
  76.3 10.6 %collective-permute-start.28 = (f32[128,640]{1,0:T(8,128)S(1)}, f32[128,640]{1,0:T(8,128)S(1)}, u32[]{:S(2)}, u32[]{:S(2)}) collective-permute-start(f32[128,640]{1,0:T(8,128)S(1)} %collective-permute-done.24.refs_9_), channel_id=1, source_target_pairs={{0,8},{8,0},{16,24},{24,16},{32,40},{40,32},{48,56},{56,48},{64,72... | collective-permute-start | bytes 983048 | tf_op jit(solution)/shard_map/ppermute | solution.py:250
  76.6 10.3 %collective-permute-start.29 = (f32[128,640]{1,0:T(8,128)S(1)}, f32[128,640]{1,0:T(8,128)S(1)}, u32[]{:S(2)}, u32[]{:S(2)}) collective-permute-start(f32[128,640]{1,0:T(8,128)S(1)} %collective-permute-done.25.refs_10_), channel_id=1, source_target_pairs={{0,8},{8,0},{16,24},{24,16},{32,40},{40,32},{48,56},{56,48},{64,72... | collective-permute-start | bytes 983048 | tf_op jit(solution)/shard_map/ppermute | solution.py:250
  76.8 10.1 %collective-permute-start.30 = (f32[128,640]{1,0:T(8,128)S(1)}, f32[128,640]{1,0:T(8,128)S(1)}, u32[]{:S(2)}, u32[]{:S(2)}) collective-permute-start(f32[128,640]{1,0:T(8,128)S(1)} %collective-permute-done.26.refs_11_), channel_id=1, source_target_pairs={{0,8},{8,0},{16,24},{24,16},{32,40},{40,32},{48,56},{56,48},{64,72... | collective-permute-start | bytes 983048 | tf_op jit(solution)/shard_map/ppermute | solution.py:250
  (6 other events, 17.7 us)

commit v3 on v2

--- a/solution.py
+++ b/solution.py
@@ -120,8 +120,8 @@
 
 
 def update_kernel(info, k_ref, *refs):
-    pieces, slots, others = refs[0:8], refs[8:12], refs[12:16]
-    l0_ref, w0_ref, l1_ref, w1_ref, out_ref, asm, bs, rows, rhi, rlo = refs[16:]
+    halves, slots, others = refs[0:2], refs[2:6], refs[6:10]
+    l0_ref, w0_ref, l1_ref, w1_ref, out_ref, asm, bs, rows, rhi, rlo = refs[10:]
     step = pl.program_id(0)
     y, x, d, z = info[0], info[1], info[2], info[3]
     core = d % 2
@@ -130,12 +130,10 @@
 
     @pl.when(step == 0)
     def _():
-        for ref, shift in zip(pieces, (0, 4, 7, 3, 1, 5, 2, 6)):
-            c = (z + shift) % 8
-            asm[c % 2 * 4 + c // 2] = ref[...]
-        q = asm.shape[1]
-        first = asm[0:4].reshape(4 * q, NB)
-        second = asm[4:8].reshape(4 * q, NB)
+        asm[z % 2] = halves[0][...]
+        asm[1 - z % 2] = halves[1][...]
+        first = asm[0]
+        second = asm[1]
         w0 = w0_ref[...]
         pan0 = mmt(first, w0)
         pan1 = mmt(first, w1_ref[:, :NB]) + mmt(second, w1_ref[:, NB:])
@@ -183,10 +181,10 @@
         out_ref[:, :NB] = rows[:, NB:]
 
 
-def update(info, kernel, pieces, slots, others, l0, w0, l1, w1):
+def update(info, kernel, halves, slots, others, l0, w0, l1, w1):
     r, c = kernel.shape
     w = c // STEPS
-    operands = [*pieces, *slots, *others, l0, w0, l1, w1]
+    operands = [*halves, *slots, *others, l0, w0, l1, w1]
     whole = [pl.BlockSpec(v.shape, lambda n, s: (0, 0)) for v in operands]
     return pl.pallas_call(
         update_kernel,
@@ -197,7 +195,7 @@
             in_specs=[pl.BlockSpec((r, w), lambda n, s: (0, n)), *whole],
             out_specs=pl.BlockSpec((r, w), lambda n, s: (0, n)),
             scratch_shapes=[
-                pltpu.VMEM((8, r // 4, NB), F32),
+                pltpu.VMEM((2, r, NB), F32),
                 pltpu.VMEM((2 * NB, c), F32),
                 pltpu.VMEM((r, 2 * NB), F32),
                 pltpu.VMEM((r, 2 * NB), BF16),
@@ -205,7 +203,7 @@
             ],
         ),
         compiler_params=pltpu.CompilerParams(
-            dimension_semantics=("arbitrary",), vmem_limit_bytes=40 * 1024 * 1024
+            dimension_semantics=("arbitrary",), vmem_limit_bytes=28 * 1024 * 1024
         ),
         cost_estimate=cost(5_000_000_000, 18_000_000),
         name="update",
@@ -220,6 +218,39 @@
 
 
 BOTH = ("row", "col")
+
+
+def whole_permute(v, axis, pairs):
+    stride, size = (8, 256) if axis == BOTH else (1, 32)
+    to = dict(pairs)
+    back = {b: a for a, b in pairs}
+    for b in list(back):
+        if b not in to:
+            a = b
+            while a in back:
+                a = back[a]
+            to[b] = a
+    real = dict(pairs)
+    for i in range(size):
+        j = i ^ stride
+        if i in to:
+            continue
+        if j not in to:
+            to[i], to[j] = j, i
+        elif j not in real:
+            to[i], to[j] = to[j], i
+        else:
+            k = next(a for a, b in to.items() if b == j)
+            assert k not in real
+            to[i], to[k] = j, i
+    return lax.ppermute(v, axis, sorted(to.items()))
+
+
+def pick(i, *values):
+    out = values[-1]
+    for n in range(len(values) - 2, -1, -1):
+        out = jnp.where(i == n, values[n], out)
+    return out
 
 
 def local(kernel):
@@ -231,46 +262,45 @@
     info = jnp.stack([y, x, row, z]).astype(jnp.int32)
 
     own = kernel[:NB, :NB]
-    other = lax.ppermute(own, BOTH, [(r * 8 + a, r * 8 + 1 - a) for r in (0, 1) for a in (0, 1)])
+    other = whole_permute(own, BOTH, [(r * 8 + a, r * 8 + 1 - a) for r in (0, 1) for a in (0, 1)])
     corner = jnp.where(z == 0, jnp.concatenate([own, other], 1), jnp.concatenate([other, own], 1))
     got = [
-        lax.ppermute(corner, BOTH, [(r * 8 + a, r * 8 + b) for r in (0, 1) for a, b in ((0, 8 - n), (1, 1 + n))])
+        whole_permute(corner, BOTH, [(r * 8 + a, r * 8 + b) for r in (0, 1) for a, b in ((0, 8 - n), (1, 1 + n))])
         for n in (3, 2, 1)
     ]
-    corner = jnp.where(z < 2, corner, got[0] + got[1] + got[2])
-    got = [
-        lax.ppermute(corner, "row", [(place(c, 0, 0), place(c, 0, n)) for c in (0, 1)]) for n in (2, 1, 3)
-    ]
-    corner = jnp.where(q == 0, corner, got[0] + got[1] + got[2])
-    got = [
-        lax.ppermute(corner, "row", [(place(c, 0, i), place(c, n, i)) for c in (0, 1) for i in range(4)])
+    corner = pick(z, corner, corner, got[2], got[1], got[0], got[0], got[1], got[2])
+    first = kernel[:, :NB]
+    corner, first = lax.optimization_barrier((corner, first))
+    got = [
+        whole_permute(corner, "row", [(place(c, 0, 0), place(c, 0, n)) for c in (0, 1)]) for n in (2, 1, 3)
+    ]
+    corner = pick(q, corner, got[1], got[0], got[2])
+    got = [
+        whole_permute(corner, "row", [(place(c, 0, i), place(c, n, i)) for c in (0, 1) for i in range(4)])
         for n in (2, 1, 3)
     ]
-    corner = jnp.where(p == 0, corner, got[0] + got[1] + got[2])
+    corner = pick(p, corner, got[1], got[0], got[2])
     swap = lambda v: lax.ppermute(v, "row", [(i, i ^ 1) for i in range(32)])
     corner_other = swap(corner)
 
-    first = kernel[:, :NB]
-    r4 = kernel.shape[0] // 4
-    got = [lax.ppermute(first[j * r4 : (j + 1) * r4], "col", [(0, 2 * j), (1, 2 * j + 1)]) for j in (1, 2, 3)]
-    piece = jnp.where(z < 2, first[:r4], got[0] + got[1] + got[2])
-    shift = lambda v, n: lax.ppermute(v, "col", [((i + n) % 8, i) for i in range(8)])
-    piece4 = shift(piece, 4)
-    pair = jnp.concatenate([piece, piece4], 0)
-    pairs = [pair] + [shift(pair, n) for n in (7, 1, 2)]
-    pieces = [v for a in pairs for v in (a[:r4], a[r4:])]
+    mesh_line = lambda pairs: [(r * 8 + a, r * 8 + b) for r in range(32) for a, b in pairs]
+    far = whole_permute(first, BOTH, mesh_line(((0, 4), (1, 5))))
+    half = jnp.where((z == 4) | (z == 5), far, first)
+    near = whole_permute(half, BOTH, mesh_line(((0, 2), (1, 3), (4, 6), (5, 7))))
+    half = jnp.where((z % 4) < 2, half, near)
+    half_other = whole_permute(half, BOTH, mesh_line([(i, i ^ 1) for i in range(8)]))
 
     w = kernel.shape[1] // 4
     quarters = [kernel[:NB, j * w : (j + 1) * w] for j in range(4)]
     got = [
-        lax.ppermute(quarters[j], "row", [(place(c, 0, 0), place(c, j, 0)) for c in (0, 1)]) for j in (2, 1, 3)
-    ]
-    quarter = jnp.where(p == 0, quarters[0], got[0] + got[1] + got[2])
-    got = [
-        lax.ppermute(quarter, "row", [(place(c, j, 0), place(c, j, n)) for c in (0, 1) for j in range(4)])
+        whole_permute(quarters[j], "row", [(place(c, 0, 0), place(c, j, 0)) for c in (0, 1)]) for j in (2, 1, 3)
+    ]
+    quarter = pick(p, quarters[0], got[1], got[0], got[2])
+    got = [
+        whole_permute(quarter, "row", [(place(c, j, 0), place(c, j, n)) for c in (0, 1) for j in range(4)])
         for n in (2, 1, 3)
     ]
-    quarter = jnp.where(q == 0, quarter, got[0] + got[1] + got[2])
+    quarter = pick(q, quarter, got[1], got[0], got[2])
     slots = [quarter] + [
         lax.ppermute(
             quarter,
@@ -285,6 +315,7 @@
         in_specs=[pl.BlockSpec(memory_space=pltpu.SMEM)] + vmem(2),
         out_specs=vmem(3),
         out_shape=[sds(2 * NB, NB), sds(NB, NB), sds(NB, NB)],
+        compiler_params=pltpu.CompilerParams(vmem_limit_bytes=4 * 1024 * 1024),
         cost_estimate=cost(1_000_000_000, 1_000_000),
         name="factor_first",
     )(core.astype(jnp.int32)[None], corner, corner_other)
@@ -295,10 +326,11 @@
         in_specs=vmem(3),
         out_specs=vmem(2),
         out_shape=[sds(NB, NB), sds(NB, 2 * NB)],
+        compiler_params=pltpu.CompilerParams(vmem_limit_bytes=4 * 1024 * 1024),
         cost_estimate=cost(1_000_000_000, 1_000_000),
         name="factor_second",
     )(l0, w0, s)
-    return update(info, kernel, pieces, slots, others, l0, w0, l1, w1)
+    return update(info, kernel, [half, half_other], slots, others, l0, w0, l1, w1)
 
 
 def solution(mesh):

time: 105 us -> 79.7 us (0.76)
  the two profiles are of different devices: /device:TPU:45 before, /device:TPU:1 now
where the time goes in v3:
time: 79.7 us; the launch traced here: 79.1 us
  waiting for transfers between devices  28.5 us (36%)
  Pallas kernels  23.6 us (30%)
  starting transfers between devices  22.3 us (28%)
  local copies, waits for them, and re-layouts  3.09 us (4%)
  other arithmetic  1.36 us (2%)
    ppermute x19, waiting for transfers between devices, whole_permute(): return lax.ppermute(v, axis, sorted(to.items()))  28.2 us
    ppermute x19, starting transfers between devices, whole_permute(): return lax.ppermute(v, axis, sorted(to.items()))  17 us
    pallas_call x1, Pallas kernels, update(): pl.pallas_call(update_kernel, out_shape=sds(r, c), grid_spec=pltpu.Prefet...  10.8 us
    pallas_call x1, Pallas kernels, local(): pl.pallas_call(factor_first, in_specs=[pl.BlockSpec(memory_space=pltpu.SM...  6.52 us
    pallas_call x1, Pallas kernels, local(): pl.pallas_call(factor_second, in_specs=vmem(3), out_specs=vmem(2), out_sh...  6.29 us
    ppermute x5, starting transfers between devices, local(): swap = lambda v: lax.ppermute(v, 'row', [(i, i ^ 1) for i in range(32)])  2.81 us
    ppermute x3, starting transfers between devices, local(): lax.ppermute(quarter, 'row', [(place(c, j, i), place(c, (j + n) % 4, i))...  2.44 us
  transfers between devices with their start and end apart: 27, of which 10 were waited for; matrix products, arithmetic and copies ran while one was open for 4% of the time, Pallas kernels for 16%

profile of v3, /device:TPU:1, one launch (start us, length us, event | category | flops | bytes accessed | tf_op | source)
XLA Modules:
  0.0 79.1 jit_solution(8110395611500211519)
XLA Ops:
  0.0 0.8 %slice.18 = f32[128,128]{1,0:T(8,128)S(1)} slice(f32[640,2560]{1,0:T(8,128)} %k_ref.1), slice={[0:128], [0:128]} | slice | bytes 131072 | tf_op jit(solution)/shard_map/slice | solution.py:264
  0.8 2.5 %collective-permute-start = (f32[128,128]{1,0:T(8,128)S(1)}, f32[128,128]{1,0:T(8,128)S(1)}, u32[]{:S(2)}, u32[]{:S(2)}) collective-permute-start(f32[128,128]{1,0:T(8,128)S(1)} %slice.18), channel_id=1, source_target_pairs={{0,1},{1,0},{2,10},{3,11},{4,12},{5,13},{6,14},{7,15},{8,9},{9,8},... | collective-permute-start | bytes 196616 | tf_op jit(solution)/shard_map/ppermute | solution.py:246
  3.3 1.7 %collective-permute-done = f32[128,128]{1,0:T(8,128)S(1)} collective-permute-done((f32[128,128]{1,0:T(8,128)S(1)}, f32[128,128]{1,0:T(8,128)S(1)}, u32[]{:S(2)}, u32[]{:S(2)}) %collective-permute-start) | collective-permute-done | bytes 65568 | tf_op jit(solution)/shard_map/ppermute | solution.py:246
  5.0 4.8 %collective-permute-start.3 = (f32[128,256]{1,0:T(8,128)S(1)}, f32[128,256]{1,0:T(8,128)S(1)}, u32[]{:S(2)}, u32[]{:S(2)}) collective-permute-start(f32[128,256]{1,0:T(8,128)S(1)} %maximum_select_fusion), channel_id=1, source_target_pairs={{0,5},{1,4},{2,10},{3,11},{4,1},{5,0},{6,14},{7,15},{8,13},{9,12},... | collective-permute-start | bytes 393224 | tf_op jit(solution)/shard_map/ppermute | solution.py:246
  9.8 1.0 %slice.19 = f32[640,128]{1,0:T(8,128)S(1)} slice(f32[640,2560]{1,0:T(8,128)} %k_ref.1), slice={[0:640], [0:128]} | slice | bytes 655360 | tf_op jit(solution)/shard_map/slice | solution.py:272
  10.8 1.5 %collective-permute-done.3 = f32[128,256]{1,0:T(8,128)S(1)} collective-permute-done((f32[128,256]{1,0:T(8,128)S(1)}, f32[128,256]{1,0:T(8,128)S(1)}, u32[]{:S(2)}, u32[]{:S(2)}) %collective-permute-start.3) | collective-permute-done | bytes 131104 | tf_op jit(solution)/shard_map/ppermute | solution.py:246
  12.3 6.4 %collective-permute-done.2 = f32[128,256]{1,0:T(8,128)S(1)} collective-permute-done((f32[128,256]{1,0:T(8,128)S(1)}, f32[128,256]{1,0:T(8,128)S(1)}, u32[]{:S(2)}, u32[]{:S(2)}) %collective-permute-start.2) | collective-permute-done | bytes 131104 | tf_op jit(solution)/shard_map/ppermute | solution.py:246
  18.8 1.0 %collective-permute-done.1 = f32[128,256]{1,0:T(8,128)S(1)} collective-permute-done((f32[128,256]{1,0:T(8,128)S(1)}, f32[128,256]{1,0:T(8,128)S(1)}, u32[]{:S(2)}, u32[]{:S(2)}) %collective-permute-start.1) | collective-permute-done | bytes 131104 | tf_op jit(solution)/shard_map/ppermute | solution.py:246
  20.0 0.1 collective-permute-start.7
  20.1 1.2 %fusion.2 = (f32[128,640]{1,0:T(8,128)S(1)}, f32[128,640]{1,0:T(8,128)S(1)}, f32[128,640]{1,0:T(8,128)S(1)}) fusion(f32[640,2560]{1,0:T(8,128)} %k_ref.1), kind=kLoop, calls=%fused_computation.12 | loop fusion | bytes 1966080 | tf_op jit(solution)/shard_map/slice | solution.py:294
  21.3 4.3 %collective-permute-start.16 = (f32[128,640]{1,0:T(8,128)S(1)}, f32[128,640]{1,0:T(8,128)S(1)}, u32[]{:S(2)}, u32[]{:S(2)}) collective-permute-start(f32[128,640]{1,0:T(8,128)S(1)} %get-tuple-element.29), channel_id=1, source_target_pairs={{0,192},{8,56},{16,24},{24,16},{32,40},{40,32},{48,8},{56,48},{64,... | collective-permute-start | bytes 983048 | tf_op jit(solution)/shard_map/ppermute | solution.py:246
  25.7 0.4 collective-permute-start.15
  26.0 1.6 %collective-permute-done.9 = f32[128,256]{1,0:T(8,128)S(1)} collective-permute-done((f32[128,256]{1,0:T(8,128)S(1)}, f32[128,256]{1,0:T(8,128)S(1)}, u32[]{:S(2)}, u32[]{:S(2)}) %collective-permute-start.9) | collective-permute-done | bytes 131104 | tf_op jit(solution)/shard_map/ppermute | solution.py:246
  27.8 0.3 collective-permute-start.12
  28.0 7.6 %collective-permute-done.16 = f32[128,640]{1,0:T(8,128)S(1)} collective-permute-done((f32[128,640]{1,0:T(8,128)S(1)}, f32[128,640]{1,0:T(8,128)S(1)}, u32[]{:S(2)}, u32[]{:S(2)}) %collective-permute-start.16) | collective-permute-done | bytes 327712 | tf_op jit(solution)/shard_map/ppermute | solution.py:246
  35.6 1.0 %select_select_fusion.1 = f32[128,640]{1,0:T(8,128)S(1)} fusion(f32[128,640]{1,0:T(8,128)S(1)} %collective-permute-done.14, f32[128,640]{1,0:T(8,128)S(1)} %collective-permute-done.15, f32[128,640]{1,0:T(8,128)S(1)} %collective-permute-done.16, f32[640,2560]{1,0:T(8,128)} %k_ref.1, pred[]{:T(512)S(6)} %eq.69, pred[]{:T(512)S(6)} %eq.68, pred[]{:T(512)S(6)} %eq.64), kind=kLoop, calls=%fused_computation.1 | loop fusion | flops 245760 | bytes 1638403 | tf_op jit(solution)/shard_map/jit(_where)/select_n | solution.py:252
  36.7 0.1 collective-permute-start.19
  36.8 2.8 %collective-permute-start.18 = (f32[128,640]{1,0:T(8,128)S(1)}, f32[128,640]{1,0:T(8,128)S(1)}, u32[]{:S(2)}, u32[]{:S(2)}) collective-permute-start(f32[128,640]{1,0:T(8,128)S(1)} %select_select_fusion.1), channel_id=1, source_target_pairs={{0,32},{8,136},{16,24},{24,152},{32,0},{40,168},{48,56},{56,184},{... | collective-permute-start | bytes 983048 | tf_op jit(solution)/shard_map/ppermute | solution.py:246
  39.6 1.7 %collective-permute-done.11 = f32[128,256]{1,0:T(8,128)S(1)} collective-permute-done((f32[128,256]{1,0:T(8,128)S(1)}, f32[128,256]{1,0:T(8,128)S(1)}, u32[]{:S(2)}, u32[]{:S(2)}) %collective-permute-start.11) | collective-permute-done | bytes 131104 | tf_op jit(solution)/shard_map/ppermute | solution.py:246
  41.3 0.7 collective-permute-start.13
  42.1 1.5 %collective-permute-start.5 = (f32[640,128]{1,0:T(8,128)S(1)}, f32[640,128]{1,0:T(8,128)S(1)}, u32[]{:S(2)}, u32[]{:S(2)}) collective-permute-start(f32[640,128]{1,0:T(8,128)S(1)} %broadcast_select_fusion), channel_id=1, source_target_pairs={{0,2},{1,3},{2,0},{3,1},{4,6},{5,7},{6,4},{7,5},{8,10},{9,11},{10,... | collective-permute-start | bytes 983048 | tf_op jit(solution)/shard_map/ppermute | solution.py:246
  43.5 4.7 %collective-permute-done.19 = f32[128,640]{1,0:T(8,128)S(1)} collective-permute-done((f32[128,640]{1,0:T(8,128)S(1)}, f32[128,640]{1,0:T(8,128)S(1)}, u32[]{:S(2)}, u32[]{:S(2)}) %collective-permute-start.19) | collective-permute-done | bytes 327712 | tf_op jit(solution)/shard_map/ppermute | solution.py:246
  48.3 0.1 collective-permute-start.22
  48.4 2.4 %collective-permute-start.21 = (f32[128,640]{1,0:T(8,128)S(1)}, f32[128,640]{1,0:T(8,128)S(1)}, u32[]{:S(2)}, u32[]{:S(2)}) collective-permute-start(f32[128,640]{1,0:T(8,128)S(1)} %select_select_fusion.refs_2_), channel_id=1, source_target_pairs={{0,128},{16,144},{32,160},{48,176},{64,192},{80,208},{96,224},{112... | collective-permute-start | bytes 983048 | tf_op jit(solution)/shard_map/ppermute | solution.py:305
  50.8 6.5 %factor_first.1 = (f32[256,128]{1,0:T(8,128)S(1)}, f32[128,128]{1,0:T(8,128)S(1)}, f32[128,128]{1,0:T(8,128)S(1)}) custom-call(s32[1]{0:T(128)} %bitcast.4.core, f32[128,256]{1,0:T(8,128)S(1)} %select_select_fusion.4.mine, f32[128,256]{1,0:T(8,128)S(1)} %collective-permute-done.13.other), custom_call_target="tpu_custom_call" | custom-call | flops 1000000000 | bytes 1000000 | tf_op jit(solution)/shard_map/factor_first/pallas_call | solution.py:313
  57.3 2.1 %collective-permute-done.5 = f32[640,128]{1,0:T(8,128)S(1)} collective-permute-done((f32[640,128]{1,0:T(8,128)S(1)}, f32[640,128]{1,0:T(8,128)S(1)}, u32[]{:S(2)}, u32[]{:S(2)}) %collective-permute-start.5) | collective-permute-done | bytes 327712 | tf_op jit(solution)/shard_map/ppermute | solution.py:246
  59.4 0.1 collective-permute-start.6
  59.5 0.2 collective-permute-done.20.refs_3_
  59.7 1.6 %collective-permute-start.23 = (f32[128,640]{1,0:T(8,128)S(1)}, f32[128,640]{1,0:T(8,128)S(1)}, u32[]{:S(2)}, u32[]{:S(2)}) collective-permute-start(f32[128,640]{1,0:T(8,128)S(1)} %select_select_fusion.refs_2_), channel_id=1, source_target_pairs={{0,8},{8,0},{16,24},{24,16},{32,40},{40,32},{48,56},{56,48},{64,72... | collective-permute-start | bytes 983048 | tf_op jit(solution)/shard_map/ppermute | solution.py:283
  61.3 0.5 collective-permute-start.25
  61.9 6.3 %factor_second.1 = (f32[128,128]{1,0:T(8,128)S(1)}, f32[128,256]{1,0:T(8,128)S(1)}) custom-call(f32[256,128]{1,0:T(8,128)S(1)} %get-tuple-element.24.l_ref.refs_10_, f32[128,128]{1,0:T(8,128)S(1)} %get-tuple-element.25.w0_ref.refs_11_, f32[128,128]{1,0:T(8,128)S(1)} %get-tuple-element.26.s_ref), custom_call_target="tpu_custom_call" | custom-call | flops 1000000000 | bytes 1000000 | tf_op jit(solution)/shard_map/factor_second/pallas_call | solution.py:324
  68.3 10.8 %update.1 = f32[640,2560]{1,0:T(8,128)} custom-call(s32[4]{0:T(128)S(1)} %pad_add_fusion.info, f32[640,2560]{1,0:T(8,128)S(1)} %bitcast.6, f32[640,128]{1,0:T(8,128)S(1)} %broadcast_select_fusion.1.refs_0_, f32[640,128]{1,0:T(8,128)S(1)} %collective-permute-done.6.refs_1_, f32[128,640]{1,0:T(8,128)S(1)} %select_select_fusion.refs_2_, ...), custom_call_target="tpu_custom_call" | custom-call | flops 5000000000 | bytes 18000000 | tf_op jit(solution)/shard_map/update/pallas_call | solution.py:189
  (42 shorter events, 0.6 us)
Async XLA Ops:
  0.8 4.1 %collective-permute-start = (f32[128,128]{1,0:T(8,128)S(1)}, f32[128,128]{1,0:T(8,128)S(1)}, u32[]{:S(2)}, u32[]{:S(2)}) collective-permute-start(f32[128,128]{1,0:T(8,128)S(1)} %slice.18), channel_id=1, source_target_pairs={{0,1},{1,0},{2,10},{3,11},{4,12},{5,13},{6,14},{7,15},{8,9},{9,8},... | collective-permute-start | bytes 196616 | tf_op jit(solution)/shard_map/ppermute | solution.py:246
  5.0 7.4 %collective-permute-start.3 = (f32[128,256]{1,0:T(8,128)S(1)}, f32[128,256]{1,0:T(8,128)S(1)}, u32[]{:S(2)}, u32[]{:S(2)}) collective-permute-start(f32[128,256]{1,0:T(8,128)S(1)} %maximum_select_fusion), channel_id=1, source_target_pairs={{0,5},{1,4},{2,10},{3,11},{4,1},{5,0},{6,14},{7,15},{8,13},{9,12},... | collective-permute-start | bytes 393224 | tf_op jit(solution)/shard_map/ppermute | solution.py:246
  9.8 9.0 %collective-permute-start.2 = (f32[128,256]{1,0:T(8,128)S(1)}, f32[128,256]{1,0:T(8,128)S(1)}, u32[]{:S(2)}, u32[]{:S(2)}) collective-permute-start(f32[128,256]{1,0:T(8,128)S(1)} %maximum_select_fusion), channel_id=1, source_target_pairs={{0,6},{1,3},{2,10},{3,1},{4,12},{5,13},{6,0},{7,15},{8,14},{9,11},... | collective-permute-start | bytes 393224 | tf_op jit(solution)/shard_map/ppermute | solution.py:246
  9.8 9.9 %collective-permute-start.1 = (f32[128,256]{1,0:T(8,128)S(1)}, f32[128,256]{1,0:T(8,128)S(1)}, u32[]{:S(2)}, u32[]{:S(2)}) collective-permute-start(f32[128,256]{1,0:T(8,128)S(1)} %maximum_select_fusion), channel_id=1, source_target_pairs={{0,7},{1,2},{2,1},{3,11},{4,12},{5,13},{6,14},{7,0},{8,15},{9,10},... | collective-permute-start | bytes 393224 | tf_op jit(solution)/shard_map/ppermute | solution.py:246
  19.8 7.9 %collective-permute-start.9 = (f32[128,256]{1,0:T(8,128)S(1)}, f32[128,256]{1,0:T(8,128)S(1)}, u32[]{:S(2)}, u32[]{:S(2)}) collective-permute-start(f32[128,256]{1,0:T(8,128)S(1)} %select_select_fusion.2), channel_id=1, source_target_pairs={{0,48},{8,200},{16,24},{24,16},{32,40},{40,32},{48,56},{56,0},{64,... | collective-permute-start | bytes 393224 | tf_op jit(solution)/shard_map/ppermute | solution.py:246
  19.9 7.8 %collective-permute-start.8 = (f32[128,256]{1,0:T(8,128)S(1)}, f32[128,256]{1,0:T(8,128)S(1)}, u32[]{:S(2)}, u32[]{:S(2)}) collective-permute-start(f32[128,256]{1,0:T(8,128)S(1)} %select_select_fusion.2), channel_id=1, source_target_pairs={{0,32},{8,136},{16,24},{24,16},{32,40},{40,0},{48,56},{56,48},{64,... | collective-permute-start | bytes 393224 | tf_op jit(solution)/shard_map/ppermute | solution.py:246
  20.0 7.7 %collective-permute-start.7 = (f32[128,256]{1,0:T(8,128)S(1)}, f32[128,256]{1,0:T(8,128)S(1)}, u32[]{:S(2)}, u32[]{:S(2)}) collective-permute-start(f32[128,256]{1,0:T(8,128)S(1)} %select_select_fusion.2), channel_id=1, source_target_pairs={{0,16},{8,72},{16,24},{24,0},{32,40},{40,32},{48,56},{56,48},{64,8... | collective-permute-start | bytes 393224 | tf_op jit(solution)/shard_map/ppermute | solution.py:246
  21.3 14.3 %collective-permute-start.16 = (f32[128,640]{1,0:T(8,128)S(1)}, f32[128,640]{1,0:T(8,128)S(1)}, u32[]{:S(2)}, u32[]{:S(2)}) collective-permute-start(f32[128,640]{1,0:T(8,128)S(1)} %get-tuple-element.29), channel_id=1, source_target_pairs={{0,192},{8,56},{16,24},{24,16},{32,40},{40,32},{48,8},{56,48},{64,... | collective-permute-start | bytes 983048 | tf_op jit(solution)/shard_map/ppermute | solution.py:246
  25.7 9.9 %collective-permute-start.15 = (f32[128,640]{1,0:T(8,128)S(1)}, f32[128,640]{1,0:T(8,128)S(1)}, u32[]{:S(2)}, u32[]{:S(2)}) collective-permute-start(f32[128,640]{1,0:T(8,128)S(1)} %get-tuple-element.30), channel_id=1, source_target_pairs={{0,128},{8,40},{16,24},{24,16},{32,8},{40,32},{48,56},{56,48},{64,... | collective-permute-start | bytes 983048 | tf_op jit(solution)/shard_map/ppermute | solution.py:246
  27.7 8.0 %collective-permute-start.14 = (f32[128,640]{1,0:T(8,128)S(1)}, f32[128,640]{1,0:T(8,128)S(1)}, u32[]{:S(2)}, u32[]{:S(2)}) collective-permute-start(f32[128,640]{1,0:T(8,128)S(1)} %get-tuple-element.31), channel_id=1, source_target_pairs={{0,64},{8,24},{16,8},{24,16},{32,40},{40,32},{48,56},{56,48},{64,7... | collective-permute-start | bytes 983048 | tf_op jit(solution)/shard_map/ppermute | solution.py:246
  27.7 14.3 %collective-permute-start.4 = (f32[640,128]{1,0:T(8,128)S(1)}, f32[640,128]{1,0:T(8,128)S(1)}, u32[]{:S(2)}, u32[]{:S(2)}) collective-permute-start(f32[640,128]{1,0:T(8,128)S(1)} %slice.19), channel_id=1, source_target_pairs={{0,4},{1,5},{2,10},{3,11},{4,0},{5,1},{6,14},{7,15},{8,12},{9,13},... | collective-permute-start | bytes 983048 | tf_op jit(solution)/shard_map/ppermute | solution.py:246
  27.7 40.5 %slice-start = ((s8[6553600]{0:T(1024)(128)(4,1)}), s8[4194304]{0:T(1024)(128)(4,1)S(1)}, s32[]{:S(2)}) async-start(s8[6553600]{0:T(1024)(128)(4,1)} %bitcast.5), calls=%async_computation | async-start | bytes 8388608
  27.8 9.0 %collective-permute-start.12 = (f32[128,256]{1,0:T(8,128)S(1)}, f32[128,256]{1,0:T(8,128)S(1)}, u32[]{:S(2)}, u32[]{:S(2)}) collective-permute-start(f32[128,256]{1,0:T(8,128)S(1)} %select_select_fusion.5), channel_id=1, source_target_pairs={{0,192},{8,56},{16,208},{24,16},{32,224},{40,32},{48,240},{56,8},{... | collective-permute-start | bytes 393224 | tf_op jit(solution)/shard_map/ppermute | solution.py:246
  35.6 5.6 %collective-permute-start.11 = (f32[128,256]{1,0:T(8,128)S(1)}, f32[128,256]{1,0:T(8,128)S(1)}, u32[]{:S(2)}, u32[]{:S(2)}) collective-permute-start(f32[128,256]{1,0:T(8,128)S(1)} %select_select_fusion.5), channel_id=1, source_target_pairs={{0,128},{8,40},{16,144},{24,16},{32,160},{40,8},{48,176},{56,48},{... | collective-permute-start | bytes 393224 | tf_op jit(solution)/shard_map/ppermute | solution.py:246
  35.6 5.6 %collective-permute-start.10 = (f32[128,256]{1,0:T(8,128)S(1)}, f32[128,256]{1,0:T(8,128)S(1)}, u32[]{:S(2)}, u32[]{:S(2)}) collective-permute-start(f32[128,256]{1,0:T(8,128)S(1)} %select_select_fusion.5), channel_id=1, source_target_pairs={{0,64},{8,24},{16,80},{24,8},{32,96},{40,32},{48,112},{56,48},{64,... | collective-permute-start | bytes 393224 | tf_op jit(solution)/shard_map/ppermute | solution.py:246
  36.7 11.6 %collective-permute-start.19 = (f32[128,640]{1,0:T(8,128)S(1)}, f32[128,640]{1,0:T(8,128)S(1)}, u32[]{:S(2)}, u32[]{:S(2)}) collective-permute-start(f32[128,640]{1,0:T(8,128)S(1)} %select_select_fusion.1), channel_id=1, source_target_pairs={{0,48},{8,200},{16,24},{24,216},{32,40},{40,232},{48,0},{56,248},{... | collective-permute-start | bytes 983048 | tf_op jit(solution)/shard_map/ppermute | solution.py:246
  36.8 11.5 %collective-permute-start.18 = (f32[128,640]{1,0:T(8,128)S(1)}, f32[128,640]{1,0:T(8,128)S(1)}, u32[]{:S(2)}, u32[]{:S(2)}) collective-permute-start(f32[128,640]{1,0:T(8,128)S(1)} %select_select_fusion.1), channel_id=1, source_target_pairs={{0,32},{8,136},{16,24},{24,152},{32,0},{40,168},{48,56},{56,184},{... | collective-permute-start | bytes 983048 | tf_op jit(solution)/shard_map/ppermute | solution.py:246
  41.2 7.0 %collective-permute-start.17 = (f32[128,640]{1,0:T(8,128)S(1)}, f32[128,640]{1,0:T(8,128)S(1)}, u32[]{:S(2)}, u32[]{:S(2)}) collective-permute-start(f32[128,640]{1,0:T(8,128)S(1)} %select_select_fusion.1), channel_id=1, source_target_pairs={{0,16},{8,72},{16,0},{24,88},{32,40},{40,104},{48,56},{56,120},{64... | collective-permute-start | bytes 983048 | tf_op jit(solution)/shard_map/ppermute | solution.py:246
  41.3 9.5 %collective-permute-start.13 = (f32[128,256]{1,0:T(8,128)S(1)}, f32[128,256]{1,0:T(8,128)S(1)}, u32[]{:S(2)}, u32[]{:S(2)}) collective-permute-start(f32[128,256]{1,0:T(8,128)S(1)} %select_select_fusion.4.mine), channel_id=1, source_target_pairs={{0,8},{8,0},{16,24},{24,16},{32,40},{40,32},{48,56},{56,48},{64,72... | collective-permute-start | bytes 393224 | tf_op jit(solution)/shard_map/ppermute | solution.py:283
  42.1 17.3 %collective-permute-start.5 = (f32[640,128]{1,0:T(8,128)S(1)}, f32[640,128]{1,0:T(8,128)S(1)}, u32[]{:S(2)}, u32[]{:S(2)}) collective-permute-start(f32[640,128]{1,0:T(8,128)S(1)} %broadcast_select_fusion), channel_id=1, source_target_pairs={{0,2},{1,3},{2,0},{3,1},{4,6},{5,7},{6,4},{7,5},{8,10},{9,11},{10,... | collective-permute-start | bytes 983048 | tf_op jit(solution)/shard_map/ppermute | solution.py:246
  48.3 11.2 %collective-permute-start.22 = (f32[128,640]{1,0:T(8,128)S(1)}, f32[128,640]{1,0:T(8,128)S(1)}, u32[]{:S(2)}, u32[]{:S(2)}) collective-permute-start(f32[128,640]{1,0:T(8,128)S(1)} %select_select_fusion.refs_2_), channel_id=1, source_target_pairs={{0,192},{16,208},{32,224},{48,240},{64,0},{80,16},{96,32},{112,48}... | collective-permute-start | bytes 983048 | tf_op jit(solution)/shard_map/ppermute | solution.py:305
  48.4 11.1 %collective-permute-start.21 = (f32[128,640]{1,0:T(8,128)S(1)}, f32[128,640]{1,0:T(8,128)S(1)}, u32[]{:S(2)}, u32[]{:S(2)}) collective-permute-start(f32[128,640]{1,0:T(8,128)S(1)} %select_select_fusion.refs_2_), channel_id=1, source_target_pairs={{0,128},{16,144},{32,160},{48,176},{64,192},{80,208},{96,224},{112... | collective-permute-start | bytes 983048 | tf_op jit(solution)/shard_map/ppermute | solution.py:305
  50.8 9.0 %collective-permute-start.20 = (f32[128,640]{1,0:T(8,128)S(1)}, f32[128,640]{1,0:T(8,128)S(1)}, u32[]{:S(2)}, u32[]{:S(2)}) collective-permute-start(f32[128,640]{1,0:T(8,128)S(1)} %select_select_fusion.refs_2_), channel_id=1, source_target_pairs={{0,64},{16,80},{32,96},{48,112},{64,128},{80,144},{96,160},{112,17... | collective-permute-start | bytes 983048 | tf_op jit(solution)/shard_map/ppermute | solution.py:305
  50.8 17.5 %slice-start.1 = ((s8[6553600]{0:T(1024)(128)(4,1)}), s8[2359296]{0:T(1024)(128)(4,1)S(1)}, s32[]{:S(2)}) async-start(s8[6553600]{0:T(1024)(128)(4,1)} %bitcast.5), calls=%async_computation.1 | async-start | bytes 4718592
  59.4 8.8 %collective-permute-start.6 = (f32[640,128]{1,0:T(8,128)S(1)}, f32[640,128]{1,0:T(8,128)S(1)}, u32[]{:S(2)}, u32[]{:S(2)}) collective-permute-start(f32[640,128]{1,0:T(8,128)S(1)} %broadcast_select_fusion.1.refs_0_), channel_id=1, source_target_pairs={{0,1},{1,0},{2,3},{3,2},{4,5},{5,4},{6,7},{7,6},{8,9},{9,8},{10,11... | collective-permute-start | bytes 983048 | tf_op jit(solution)/shard_map/ppermute | solution.py:246
  59.7 8.5 %collective-permute-start.23 = (f32[128,640]{1,0:T(8,128)S(1)}, f32[128,640]{1,0:T(8,128)S(1)}, u32[]{:S(2)}, u32[]{:S(2)}) collective-permute-start(f32[128,640]{1,0:T(8,128)S(1)} %select_select_fusion.refs_2_), channel_id=1, source_target_pairs={{0,8},{8,0},{16,24},{24,16},{32,40},{40,32},{48,56},{56,48},{64,72... | collective-permute-start | bytes 983048 | tf_op jit(solution)/shard_map/ppermute | solution.py:283
  61.3 6.9 %collective-permute-start.24 = (f32[128,640]{1,0:T(8,128)S(1)}, f32[128,640]{1,0:T(8,128)S(1)}, u32[]{:S(2)}, u32[]{:S(2)}) collective-permute-start(f32[128,640]{1,0:T(8,128)S(1)} %collective-permute-done.20.refs_3_), channel_id=1, source_target_pairs={{0,8},{8,0},{16,24},{24,16},{32,40},{40,32},{48,56},{56,48},{64,72... | collective-permute-start | bytes 983048 | tf_op jit(solution)/shard_map/ppermute | solution.py:283
  61.3 6.9 %collective-permute-start.25 = (f32[128,640]{1,0:T(8,128)S(1)}, f32[128,640]{1,0:T(8,128)S(1)}, u32[]{:S(2)}, u32[]{:S(2)}) collective-permute-start(f32[128,640]{1,0:T(8,128)S(1)} %collective-permute-done.21.refs_4_), channel_id=1, source_target_pairs={{0,8},{8,0},{16,24},{24,16},{32,40},{40,32},{48,56},{56,48},{64,72... | collective-permute-start | bytes 983048 | tf_op jit(solution)/shard_map/ppermute | solution.py:283
  61.8 6.4 %collective-permute-start.26 = (f32[128,640]{1,0:T(8,128)S(1)}, f32[128,640]{1,0:T(8,128)S(1)}, u32[]{:S(2)}, u32[]{:S(2)}) collective-permute-start(f32[128,640]{1,0:T(8,128)S(1)} %collective-permute-done.22.refs_5_), channel_id=1, source_target_pairs={{0,8},{8,0},{16,24},{24,16},{32,40},{40,32},{48,56},{56,48},{64,72... | collective-permute-start | bytes 983048 | tf_op jit(solution)/shard_map/ppermute | solution.py:283

commit v4 on v0

v4 whole, which is shorter than its diff:
```python
import jax
import jax.numpy as jnp
from jax import lax
from jax.experimental import pallas as pl
from jax.experimental.pallas import tpu as pltpu
from jax.sharding import PartitionSpec as P

NB = 128
HIGHEST = lax.Precision.HIGHEST
F32 = jnp.float32
BF16 = jnp.bfloat16


def bc(v):
    return jnp.broadcast_to(v, (8, NB))


def identity():
    r=lax.broadcasted_iota(jnp.int32,(NB,NB),0)
    c=lax.broadcasted_iota(jnp.int32,(NB,NB),1)
    return (r==c).astype(F32)


def eliminate(left,right,lo,hi):
    G=NB//8
    A=[left[8*g:8*g+8,:] for g in range(G)]
    I=[right[8*g:8*g+8,:] for g in range(G)]
    sub=lax.broadcasted_iota(jnp.int32,(8,NB),0)
    lane=lax.broadcasted_iota(jnp.int32,(8,NB),1)
    outU=[];outW=[]
    def rsq(x):
        r=lax.rsqrt(x); return r*(1.5-0.5*x*r*r)
    for g0 in range(lo,hi):
        k=8*g0
        C=[bc(A[g0][:,k+a:k+a+1]) for a in range(8)]
        D=[[bc(C[a][b:b+1,:]) for b in range(a+1)] for a in range(8)]
        T=[[None]*8 for _ in range(8)]
        inv=[]
        for j in range(0,8,2):
            p00,p10,p11=D[j][j],D[j+1][j],D[j+1][j+1]
            ip=1.0/(p00*p11-p10*p10)
            i00,i10,i11=p11*ip,-p10*ip,p00*ip
            inv.append((i00,i10,i11,p00,p10,p11))
            for r in range(j+2,8):
                T[r][j]=i00*D[r][j]+i10*D[r][j+1]
                T[r][j+1]=i10*D[r][j]+i11*D[r][j+1]
            for r in range(j+2,8):
                for c in range(j+2,r+1):
                    D[r][c]=D[r][c]-(D[r][j]*T[c][j]+D[r][j+1]*T[c][j+1])
        def solve(x):
            y=[bc(x[b:b+1,:]) for b in range(8)]
            for j in range(0,8,2):
                for r in range(j+2,8):
                    y[r]=y[r]-(T[r][j]*y[j]+T[r][j+1]*y[j+1])
            X=[None]*8
            for j in (6,4,2,0):
                i00,i10,i11=inv[j//2][:3]
                a=i00*y[j]+i10*y[j+1]; b=i10*y[j]+i11*y[j+1]
                for r in range(j+2,8):
                    a=a-T[r][j]*X[r]; b=b-T[r][j+1]*X[r]
                X[j],X[j+1]=a,b
            return y,X
        ya,xa=solve(A[g0])
        yi,xi=solve(I[g0])
        for g in range(g0+1,G):
            c=[bc(A[g][:,k+a:k+a+1]) for a in range(8)]
            def acc(x):
                t=[c[a]*x[a] for a in range(8)]
                return ((t[0]+t[1])+(t[2]+t[3]))+((t[4]+t[5])+(t[6]+t[7]))
            A[g]=A[g]-acc(xa)
            I[g]=I[g]-acc(xi)
        u=[];w=[]
        for j in range(0,8,2):
            p00,p10,p11=inv[j//2][3:]
            rs0=rsq(p00); l10=p10*rs0; rs1=rsq(p11-l10*l10)
            for y,o in ((ya,u),(yi,w)):
                o.append(y[j]*rs0); o.append((y[j+1]-l10*o[-1])*rs1)
        ru,rw=u[7],w[7]
        for b in range(6,-1,-1):
            ru=jnp.where(sub==b,u[b],ru); rw=jnp.where(sub==b,w[b],rw)
        outU.append(jnp.where(lane>=sub+k,ru,0.0)); outW.append(rw)
    rest = (jnp.concatenate(A[hi:],0),jnp.concatenate(I[hi:],0)) if hi<G else None
    return jnp.concatenate(outU,0), jnp.concatenate(outW,0), rest


def mm(a, b):
    return jnp.dot(a, b, precision=HIGHEST, preferred_element_type=F32)


def mmt(a, b):
    return lax.dot_general(a, b, (((1,), (1,)), ((), ())), precision=HIGHEST, preferred_element_type=F32)


def factor_first(core, mine, other, l_ref, w_ref, s_ref):
    flip = core[0] == 1
    top = jnp.where(flip, other[:, :NB], mine[:, :NB])
    bottom = jnp.where(flip, mine[...], other[...])
    u0, w0, _ = eliminate(top, identity(), 0, NB // 8)
    l10 = mmt(bottom[:, :NB], w0)
    l_ref[:NB, :] = u0.T
    l_ref[NB:, :] = l10
    w_ref[...] = w0
    s_ref[...] = bottom[:, NB:] - mmt(l10, l10)


def factor_second(s_ref, a_ref, i_ref):
    u, w, (a, i) = eliminate(s_ref[...], identity(), 0, NB // 16)
    a_ref[: NB // 2] = u
    a_ref[NB // 2 :] = a
    i_ref[: NB // 2] = w
    i_ref[NB // 2 :] = i


def factor_third(a_ref, i_ref, l_ref, w0_ref, l1_ref, w1_ref):
    u, w, _ = eliminate(a_ref[...], i_ref[...], NB // 16, NB // 8)
    u = jnp.concatenate([a_ref[: NB // 2], u], 0)
    w = jnp.concatenate([i_ref[: NB // 2], w], 0)
    l1_ref[...] = u.T
    w1_ref[:, :NB] = -mm(mm(w, l_ref[NB:, :]), w0_ref[...])
    w1_ref[:, NB:] = w


def sds(*shape):
    return jax.ShapeDtypeStruct(shape, F32)


def vmem(n):
    return [pl.BlockSpec(memory_space=pltpu.VMEM)] * n


def cost(flops, moved):
    return pl.CostEstimate(flops=flops, bytes_accessed=moved, transcendentals=0)


def split(v):
    hi = v.astype(BF16)
    return hi, (v - hi.astype(F32)).astype(BF16)


def update_kernel(info, k_ref, h0, h1, s0, s1, s2, s3, o0, o1, o2, o3, l0_ref, w0_ref, l1_ref, w1_ref, out_ref, bs, wf, rows, r3, c3, buf, sems):
    y, x, d, z = info[0], info[1], info[2], info[3]
    core = d % 2
    w = bs.shape[1] // 4
    dot = lambda a, b: jnp.dot(a, b, preferred_element_type=F32)

    for group, p, block in (
        ((s0, s1, s2, s3), jnp.where(core == 0, y, x), core),
        ((o0, o1, o2, o3), jnp.where(core == 0, x, y), 1 - core),
    ):
        for s in range(4):
            n = (p - s + 4) % 4
            bs[pl.ds(pl.multiple_of(block * NB, NB), NB), pl.ds(pl.multiple_of(n * w, NB), w)] = group[s][...]

    wf[:NB, :NB] = w0_ref[...]
    wf[:NB, NB:] = jnp.zeros((NB, NB), F32)
    wf[NB:, :] = w1_ref[...]
    even = z % 2 == 0
    first = jnp.where(even, h0[...], h1[...])
    second = jnp.where(even, h1[...], h0[...])
    pan = mmt(jnp.concatenate([first, second], 1), wf[...])
    rows[...] = pan
    hi, lo = split(pan)
    r3[:, : 2 * NB] = hi
    r3[:, 2 * NB : 4 * NB] = lo
    r3[:, 4 * NB :] = hi

    @pl.when(d == 0)
    def _():
        rows[:NB, :NB] = l0_ref[:NB, :]
        rows[:NB, NB:] = jnp.zeros((NB, NB), F32)

    @pl.when(d == 1)
    def _():
        rows[:NB, NB:] = l1_ref[...]

    whi, wlo = split(wf[...])
    w3 = jnp.concatenate([whi, wlo, whi], 1)
    r, c = buf.shape
    width = c // STEPS
    copies = []

    for n in range(5):
        here = slice(n * c // 5, (n + 1) * c // 5)
        bhi, blo = split(bs[:, here])
        chi, clo = split(dot(w3, jnp.concatenate([bhi, bhi, blo], 0)))
        c3[: 2 * NB, here] = chi
        c3[2 * NB : 4 * NB, here] = chi
        c3[4 * NB :, here] = clo

    for n in range(STEPS):
        here = slice(n * width, (n + 1) * width)
        buf[:, here] = k_ref[:, here] - dot(r3[...], c3[:, here])

        @pl.when(d < 2)
        def _():
            buf[:NB, here] = jnp.zeros((NB, width), F32)

        if n == 0:

            @pl.when(z == 0)
            def _():
                buf[:, :NB] = rows[:, :NB]

            @pl.when(z == 1)
            def _():
                buf[:, :NB] = rows[:, NB:]

        copy = pltpu.make_async_copy(buf.at[:, here], out_ref.at[:, here], sems.at[n])
        copy.start()
        copies.append(copy)
    for copy in copies:
        copy.wait()


def update(info, kernel, halves, slots, others, l0, w0, l1, w1):
    r, c = kernel.shape
    operands = [kernel, *halves, *slots, *others, l0, w0, l1, w1]
    return pl.pallas_call(
        update_kernel,
        out_shape=sds(r, c),
        in_specs=[pl.BlockSpec(memory_space=pltpu.SMEM)] + vmem(len(operands)),
        out_specs=pl.BlockSpec(memory_space=pl.ANY),
        scratch_shapes=[
            pltpu.VMEM((2 * NB, c), F32),
            pltpu.VMEM((2 * NB, 2 * NB), F32),
            pltpu.VMEM((r, 2 * NB), F32),
            pltpu.VMEM((r, 6 * NB), BF16),
            pltpu.VMEM((6 * NB, c), BF16),
            pltpu.VMEM((r, c), F32),
            pltpu.SemaphoreType.DMA((STEPS,)),
        ],
        compiler_params=pltpu.CompilerParams(vmem_limit_bytes=32 * 1024 * 1024),
        cost_estimate=cost(5_000_000_000, 18_000_000),
        name="update",
    )(info, *operands)


STEPS = 5


def place(core, p, q):
    return p * 8 + q * 2 if core == 0 else q * 8 + p * 2 + 1


BOTH = ("row", "col")


def whole_permute(v, axis, pairs):
    stride, size = (8, 256) if axis == BOTH else (1, 32)
    to = dict(pairs)
    back = {b: a for a, b in pairs}
    for b in list(back):
        if b not in to:
            a = b
            while a in back:
                a = back[a]
            to[b] = a
    real = dict(pairs)
    for i in range(size):
        j = i ^ stride
        if i in to:
            continue
        if j not in to:
            to[i], to[j] = j, i
        elif j not in real:
            to[i], to[j] = to[j], i
        else:
            k = next(a for a, b in to.items() if b == j)
            assert k not in real
            to[i], to[k] = j, i
    return lax.ppermute(v, axis, sorted(to.items()))


def pick(i, *values):
    out = values[-1]
    for n in range(len(values) - 2, -1, -1):
        out = jnp.where(i == n, values[n], out)
    return out


def local(kernel):
    row = lax.axis_index("row")
    z = lax.axis_index("col")
    y, x, core = row // 8, row // 2 % 4, row % 2
    p = jnp.where(core == 0, y, x)
    q = jnp.where(core == 0, x, y)
    info = jnp.stack([y, x, row, z]).astype(jnp.int32)

    swap = lambda v: lax.ppermute(v, "row", [(i, i ^ 1) for i in range(32)])
    in_line = lambda pairs: [(r * 8 + a, r * 8 + b) for r in (0, 1) for a, b in pairs]
    in_lines = lambda pairs: [(r * 8 + a, r * 8 + b) for r in range(32) for a, b in pairs]
    w = kernel.shape[1] // 4

    own = kernel[:NB, :NB]
    quarters = [kernel[:NB, j * w : (j + 1) * w] for j in range(4)]
    other = whole_permute(own, BOTH, in_line(((0, 1), (1, 0))))
    scattered = [
        whole_permute(quarters[j], "row", [(place(c, 0, 0), place(c, j, 0)) for c in (0, 1)]) for j in (2, 1, 3)
    ]
    corner = jnp.where(z == 0, jnp.concatenate([own, other], 1), jnp.concatenate([other, own], 1))
    two = whole_permute(corner, BOTH, in_line(((0, 6), (1, 3))))
    one = whole_permute(corner, BOTH, in_line(((0, 7), (1, 2))))
    corner = pick(z, corner, corner, one, two, two, two, two, one)
    quarter = pick(p, quarters[0], scattered[1], scattered[0], scattered[2])
    first = kernel[:, :NB]
    corner, quarter, first = lax.optimization_barrier((corner, quarter, first))
    last = whole_permute(corner, BOTH, in_line(((6, 5), (3, 4))))
    corner = jnp.where((z == 4) | (z == 5), last, corner)

    far = whole_permute(first, BOTH, in_lines(((0, 4), (1, 5))))

    spread = [
        whole_permute(quarter, "row", [(place(c, j, 0), place(c, j, n)) for c in (0, 1) for j in range(4)])
        for n in (2, 1, 3)
    ]
    got = [whole_permute(corner, "row", [(place(c, 0, 0), place(c, 0, n)) for c in (0, 1)]) for n in (2, 1, 3)]
    corner = pick(q, corner, got[1], got[0], got[2])
    got = [
        whole_permute(corner, "row", [(place(c, 0, i), place(c, n, i)) for c in (0, 1) for i in range(4)])
        for n in (2, 1, 3)
    ]
    corner = pick(p, corner, got[1], got[0], got[2])
    quarter = pick(q, quarter, spread[1], spread[0], spread[2])
    half = jnp.where((z == 4) | (z == 5), far, first)
    corner, quarter, half = lax.optimization_barrier((corner, quarter, half))

    corner_other = swap(corner)
    slots = [
        lax.ppermute(
            quarter,
            "row",
            [(place(c, j, i), place(c, (j + n) % 4, i)) for c in (0, 1) for j in range(4) for i in range(4)],
        )
        for n in (1, 2, 3)
    ]
    near = whole_permute(half, BOTH, in_lines(((0, 2), (1, 3), (4, 6), (5, 7))))
    l0, w0, s = kernel_call(factor_first, "factor_first", [(2 * NB, NB), (NB, NB), (NB, NB)], 1)(
        core.astype(jnp.int32)[None], corner, corner_other
    )
    half = jnp.where((z % 4) < 2, half, near)
    s, half = lax.optimization_barrier((s, half))
    half_other = whole_permute(half, BOTH, in_lines([(i, i ^ 1) for i in range(8)]))
    left, right = kernel_call(factor_second, "factor_second", [(NB, NB), (NB, NB)])(s)
    left, right, quarter, slots = lax.optimization_barrier((left, right, quarter, slots))
    slots = [quarter, *slots]
    others = [swap(v) for v in slots]
    l1, w1 = kernel_call(factor_third, "factor_third", [(NB, NB), (NB, 2 * NB)])(left, right, l0, w0)
    return update(info, kernel, [half, half_other], slots, others, l0, w0, l1, w1)


def kernel_call(body, name, shapes, scalars=0):
    def call(*operands):
        return pl.pallas_call(
            body,
            in_specs=[pl.BlockSpec(memory_space=pltpu.SMEM)] * scalars + vmem(len(operands) - scalars),
            out_specs=vmem(len(shapes)),
            out_shape=[sds(*shape) for shape in shapes],
            compiler_params=pltpu.CompilerParams(vmem_limit_bytes=4 * 1024 * 1024),
            cost_estimate=cost(1_000_000_000, 1_000_000),
            name=name,
        )(*operands)

    return call


def solution(mesh):
    return jax.shard_map(
        local,
        mesh=mesh,
        in_specs=(P("row", "col"),),
        out_specs=P("row", "col"),
        check_vma=False,
    )
```

time: 626 us -> 83.3 us (0.13)
  waiting for transfers between devices: 486 us -> 37 us
  other arithmetic: 52.1 us -> 2.51 us
  local copies, waits for them, and re-layouts: 50.9 us -> 3.54 us
  matrix products: 21.2 us -> 0 us
  starting transfers between devices: 0.39 us -> 21.4 us
  Pallas kernels: 0 us -> 18.1 us
  between operations: 13.7 us -> 0.53 us
    psum x4 -> x0, waiting for transfers between devices: 349 us -> none  [broadcast(): return lax.psum(kept, axis)]
    all_gather x2 -> x0, waiting for transfers between devices: 137 us -> none  [factor_panel(): whole = lax.all_gather(rows_side, 'row', axis=0, tiled=True)]
    another operation x10 -> x1, other arithmetic: 45.7 us -> 0.08 us  [local(): info = jnp.stack([y, x, row, z]).astype(jnp.int32)]
    ppermute x0 -> x27, waiting for transfers between devices: none -> 37 us  [the longest x19 37 us: whole_permute(): return lax.ppermute(v, axis, sorted(to.items()))]
    all_gather x2 -> x0, local copies, waits for them, and re-layouts: 23.5 us -> none  [factor_panel(): whole = lax.all_gather(rows_side, 'row', axis=0, tiled=True)]
    ppermute x0 -> x27, starting transfers between devices: none -> 21.4 us  [the longest x19 17.2 us: whole_permute(): return lax.ppermute(v, axis, sorted(to.items()))]
    dot_general x4 -> x0, matrix products: 20.7 us -> none  [the longest x2 16.4 us: product(): return jnp.dot(left, right.T, precision=lax.Precision.HIGHEST)]
    pallas_call x0 -> x4, Pallas kernels: none -> 18.1 us  [the longest x3 9.98 us: call(): pl.pallas_call(body, in_specs=[pl.BlockSpec(memory_space=pltpu.SMEM)] * s...]
  transfers between devices with their start and end apart: 6 -> 27, of which waited for: 6 -> 9; matrix products, arithmetic and copies ran while one was open for 0% -> 4% of each run, Pallas kernels for 0% -> 12%
where the time goes in v4:
time: 83.3 us; the launch traced here: 83.1 us
  waiting for transfers between devices  37 us (44%)
  starting transfers between devices  21.4 us (26%)
  Pallas kernels  18.1 us (22%)
  local copies, waits for them, and re-layouts  3.54 us (4%)
  other arithmetic  2.51 us (3%)
    ppermute x19, waiting for transfers between devices, whole_permute(): return lax.ppermute(v, axis, sorted(to.items()))  37 us
    ppermute x19, starting transfers between devices, whole_permute(): return lax.ppermute(v, axis, sorted(to.items()))  17.2 us
    pallas_call x3, Pallas kernels, call(): pl.pallas_call(body, in_specs=[pl.BlockSpec(memory_space=pltpu.SMEM)] * s...  9.98 us
    pallas_call x1, Pallas kernels, update(): pl.pallas_call(update_kernel, out_shape=sds(r, c), in_specs=[pl.BlockSpec...  8.1 us
    ppermute x3, starting transfers between devices, local(): lax.ppermute(quarter, 'row', [(place(c, j, i), place(c, (j + n) % 4, i))...  2.34 us
    select_n x5, other arithmetic, pick(): out = jnp.where(i == n, values[n], out)  2.33 us
    ppermute x5, starting transfers between devices, local(): swap = lambda v: lax.ppermute(v, 'row', [(i, i ^ 1) for i in range(32)])  1.85 us
  transfers between devices with their start and end apart: 27, of which 9 were waited for; matrix products, arithmetic and copies ran while one was open for 4% of the time, Pallas kernels for 12%

profile of v4, /device:TPU:1, one launch (start us, length us, event | category | flops | bytes accessed | tf_op | source)
XLA Modules:
  0.0 83.1 jit_solution(8113686190469260942)
XLA Ops:
  0.0 0.8 %slice.18 = f32[128,128]{1,0:T(8,128)S(1)} slice(f32[640,2560]{1,0:T(8,128)} %k_ref.1), slice={[0:128], [0:128]} | slice | bytes 131072 | tf_op jit(solution)/shard_map/slice | solution.py:294
  0.8 2.5 %collective-permute-start = (f32[128,128]{1,0:T(8,128)S(1)}, f32[128,128]{1,0:T(8,128)S(1)}, u32[]{:S(2)}, u32[]{:S(2)}) collective-permute-start(f32[128,128]{1,0:T(8,128)S(1)} %slice.18), channel_id=1, source_target_pairs={{0,1},{1,0},{2,10},{3,11},{4,12},{5,13},{6,14},{7,15},{8,9},{9,8},... | collective-permute-start | bytes 196616 | tf_op jit(solution)/shard_map/ppermute | solution.py:271
  3.3 1.7 %collective-permute-done = f32[128,128]{1,0:T(8,128)S(1)} collective-permute-done((f32[128,128]{1,0:T(8,128)S(1)}, f32[128,128]{1,0:T(8,128)S(1)}, u32[]{:S(2)}, u32[]{:S(2)}) %collective-permute-start) | collective-permute-done | bytes 65568 | tf_op jit(solution)/shard_map/ppermute | solution.py:271
  5.0 4.4 %collective-permute-start.2 = (f32[128,256]{1,0:T(8,128)S(1)}, f32[128,256]{1,0:T(8,128)S(1)}, u32[]{:S(2)}, u32[]{:S(2)}) collective-permute-start(f32[128,256]{1,0:T(8,128)S(1)} %maximum_select_fusion), channel_id=1, source_target_pairs={{0,6},{1,3},{2,10},{3,1},{4,12},{5,13},{6,0},{7,15},{8,14},{9,11},... | collective-permute-start | bytes 393224 | tf_op jit(solution)/shard_map/ppermute | solution.py:271
  9.4 1.2 %fusion.1 = (f32[128,640]{1,0:T(8,128)S(1)}, f32[128,640]{1,0:T(8,128)S(1)}, f32[128,640]{1,0:T(8,128)S(1)}) fusion(f32[640,2560]{1,0:T(8,128)} %k_ref.1), kind=kLoop, calls=%fused_computation.12 | loop fusion | bytes 1966080 | tf_op jit(solution)/shard_map/slice | solution.py:295
  10.8 0.1 collective-permute-start.3
  11.0 1.0 %slice.23 = f32[640,128]{1,0:T(8,128)S(1)} slice(f32[640,2560]{1,0:T(8,128)} %k_ref.1), slice={[0:640], [0:128]} | slice | bytes 655360 | tf_op jit(solution)/shard_map/slice | solution.py:305
  12.0 5.0 %collective-permute-done.1 = f32[128,256]{1,0:T(8,128)S(1)} collective-permute-done((f32[128,256]{1,0:T(8,128)S(1)}, f32[128,256]{1,0:T(8,128)S(1)}, u32[]{:S(2)}, u32[]{:S(2)}) %collective-permute-start.1) | collective-permute-done | bytes 131104 | tf_op jit(solution)/shard_map/ppermute | solution.py:271
  17.0 5.1 %collective-permute-done.5 = f32[128,640]{1,0:T(8,128)S(1)} collective-permute-done((f32[128,640]{1,0:T(8,128)S(1)}, f32[128,640]{1,0:T(8,128)S(1)}, u32[]{:S(2)}, u32[]{:S(2)}) %collective-permute-start.5) | collective-permute-done | bytes 327712 | tf_op jit(solution)/shard_map/ppermute | solution.py:271
  22.2 1.0 %select_select_fusion.1 = f32[128,640]{1,0:T(8,128)S(1)} fusion(f32[128,640]{1,0:T(8,128)S(1)} %collective-permute-done.3, f32[128,640]{1,0:T(8,128)S(1)} %collective-permute-done.4, f32[128,640]{1,0:T(8,128)S(1)} %collective-permute-done.5, f32[640,2560]{1,0:T(8,128)} %k_ref.1, pred[]{:T(512)S(6)} %eq.69, pred[]{:T(512)S(6)} %eq.68, pred[]{:T(512)S(6)} %eq.59), kind=kLoop, calls=%fused_computation.1 | loop fusion | flops 245760 | bytes 1638403 | tf_op jit(solution)/shard_map/jit(_where)/select_n | solution.py:277
  23.2 0.5 collective-permute-start.6
  23.7 1.0 %collective-permute-done.6 = f32[128,256]{1,0:T(8,128)S(1)} collective-permute-done((f32[128,256]{1,0:T(8,128)S(1)}, f32[128,256]{1,0:T(8,128)S(1)}, u32[]{:S(2)}, u32[]{:S(2)}) %collective-permute-start.6) | collective-permute-done | bytes 131104 | tf_op jit(solution)/shard_map/ppermute | solution.py:271
  25.0 2.9 %collective-permute-start.15 = (f32[128,640]{1,0:T(8,128)S(1)}, f32[128,640]{1,0:T(8,128)S(1)}, u32[]{:S(2)}, u32[]{:S(2)}) collective-permute-start(f32[128,640]{1,0:T(8,128)S(1)} %select_select_fusion.1), channel_id=1, source_target_pairs={{0,48},{8,200},{16,24},{24,216},{32,40},{40,232},{48,0},{56,248},{... | collective-permute-start | bytes 983048 | tf_op jit(solution)/shard_map/ppermute | solution.py:271
  27.8 0.4 collective-permute-start.14
  28.2 8.8 %collective-permute-done.9 = f32[128,256]{1,0:T(8,128)S(1)} collective-permute-done((f32[128,256]{1,0:T(8,128)S(1)}, f32[128,256]{1,0:T(8,128)S(1)}, u32[]{:S(2)}, u32[]{:S(2)}) %collective-permute-start.9) | collective-permute-done | bytes 131104 | tf_op jit(solution)/shard_map/ppermute | solution.py:271
  37.0 5.5 %collective-permute-start.16 = (f32[640,128]{1,0:T(8,128)S(1)}, f32[640,128]{1,0:T(8,128)S(1)}, u32[]{:S(2)}, u32[]{:S(2)}) collective-permute-start(f32[640,128]{1,0:T(8,128)S(1)} %slice.23), channel_id=1, source_target_pairs={{0,4},{1,5},{2,10},{3,11},{4,0},{5,1},{6,14},{7,15},{8,12},{9,13},... | collective-permute-start | bytes 983048 | tf_op jit(solution)/shard_map/ppermute | solution.py:271
  42.7 0.3 collective-permute-start.10
  43.0 0.3 copy-done
  43.4 1.2 %select_select_fusion.s0 = f32[128,640]{1,0:T(8,128)S(1)} fusion(f32[128,640]{1,0:T(8,128)S(1)} %select_select_fusion.1, f32[128,640]{1,0:T(8,128)} %collective-permute-done.13, f32[128,640]{1,0:T(8,128)} %copy-done.1, f32[128,640]{1,0:T(8,128)} %copy-done, pred[]{:T(512)S(6)} %eq.71, pred[]{:T(512)S(6)} %eq.70, pred[]{:T(512)S(6)} %eq.60), kind=kLoop, calls=%fused_computation | loop fusion | flops 245760 | bytes 1638403 | tf_op jit(solution)/shard_map/jit(_where)/select_n | solution.py:277
  44.6 3.1 %collective-permute-done.16 = f32[640,128]{1,0:T(8,128)S(1)} collective-permute-done((f32[640,128]{1,0:T(8,128)S(1)}, f32[640,128]{1,0:T(8,128)S(1)}, u32[]{:S(2)}, u32[]{:S(2)}) %collective-permute-start.16) | collective-permute-done | bytes 327712 | tf_op jit(solution)/shard_map/ppermute | solution.py:271
  47.8 1.2 %collective-permute-done.12 = f32[128,256]{1,0:T(8,128)S(1)} collective-permute-done((f32[128,256]{1,0:T(8,128)S(1)}, f32[128,256]{1,0:T(8,128)S(1)}, u32[]{:S(2)}, u32[]{:S(2)}) %collective-permute-start.12) | collective-permute-done | bytes 131104 | tf_op jit(solution)/shard_map/ppermute | solution.py:271
  49.1 0.2 collective-permute-start.17
  49.3 1.6 %collective-permute-start.22 = (f32[128,640]{1,0:T(8,128)S(1)}, f32[128,640]{1,0:T(8,128)S(1)}, u32[]{:S(2)}, u32[]{:S(2)}) collective-permute-start(f32[128,640]{1,0:T(8,128)S(1)} %select_select_fusion.s0), channel_id=1, source_target_pairs={{0,192},{16,208},{32,224},{48,240},{64,0},{80,16},{96,32},{112,48}... | collective-permute-start | bytes 983048 | tf_op jit(solution)/shard_map/ppermute | solution.py:329
  50.9 0.8 collective-permute-start.20
  51.7 5.5 %factor_first.1 = (f32[256,128]{1,0:T(8,128)S(1)}, f32[128,128]{1,0:T(8,128)S(1)}, f32[128,128]{1,0:T(8,128)S(1)}) custom-call(s32[1]{0:T(128)} %bitcast.4.core, f32[128,256]{1,0:T(8,128)S(1)} %select_select_fusion.4.mine, f32[128,256]{1,0:T(8,128)S(1)} %collective-permute-done.17.other), custom_call_target="tpu_custom_call" | custom-call | flops 1000000000 | bytes 1000000 | tf_op jit(solution)/shard_map/factor_first/pallas_call | solution.py:353
  57.2 9.1 %collective-permute-done.18 = f32[640,128]{1,0:T(8,128)} collective-permute-done((f32[640,128]{1,0:T(8,128)S(1)}, f32[640,128]{1,0:T(8,128)}, u32[]{:S(2)}, u32[]{:S(2)}) %collective-permute-start.18) | collective-permute-done | bytes 327712 | tf_op jit(solution)/shard_map/ppermute | solution.py:271
  66.5 1.9 %factor_second.1 = (f32[128,128]{1,0:T(8,128)S(1)}, f32[128,128]{1,0:T(8,128)S(1)}) custom-call(f32[128,128]{1,0:T(8,128)S(1)} %get-tuple-element.33.s_ref), custom_call_target="tpu_custom_call" | custom-call | flops 1000000000 | bytes 1000000 | tf_op jit(solution)/shard_map/factor_second/pallas_call | solution.py:353
  68.4 1.0 %collective-permute-start.23 = (f32[128,640]{1,0:T(8,128)S(1)}, f32[128,640]{1,0:T(8,128)S(1)}, u32[]{:S(2)}, u32[]{:S(2)}) collective-permute-start(f32[128,640]{1,0:T(8,128)S(1)} %select_select_fusion.s0), channel_id=1, source_target_pairs={{0,8},{8,0},{16,24},{24,16},{32,40},{40,32},{48,56},{56,48},{64,72... | collective-permute-start | bytes 983048 | tf_op jit(solution)/shard_map/ppermute | solution.py:289
  69.6 0.4 collective-permute-start.25
  70.1 2.6 %factor_third.1 = (f32[128,128]{1,0:T(8,128)S(1)}, f32[128,256]{1,0:T(8,128)S(1)}) custom-call(f32[128,128]{1,0:T(8,128)S(1)} %get-tuple-element.43.a_ref, f32[128,128]{1,0:T(8,128)S(1)} %get-tuple-element.44.i_ref, f32[256,128]{1,0:T(8,128)S(1)} %get-tuple-element.41.l_ref.l0_ref, f32[128,128]{1,0:T(8,128)S(1)} %get-tuple-element.42.w0_ref), custom_call_target="tpu_custom_call" | custom-call | flops 1000000000 | bytes 1000000 | tf_op jit(solution)/shard_map/factor_third/pallas_call | solution.py:353
  72.7 2.0 %collective-permute-done.19.h1 = f32[640,128]{1,0:T(8,128)S(1)} collective-permute-done((f32[640,128]{1,0:T(8,128)S(1)}, f32[640,128]{1,0:T(8,128)S(1)}, u32[]{:S(2)}, u32[]{:S(2)}) %collective-permute-start.19) | collective-permute-done | bytes 327712 | tf_op jit(solution)/shard_map/ppermute | solution.py:271
  74.8 8.1 %update.1 = f32[640,2560]{1,0:T(8,128)} custom-call(s32[4]{0:T(128)S(1)} %pad_add_fusion.info, f32[640,2560]{1,0:T(8,128)S(1)} %bitcast.6, f32[640,128]{1,0:T(8,128)S(1)} %broadcast_select_fusion.h0, f32[640,128]{1,0:T(8,128)S(1)} %collective-permute-done.19.h1, f32[128,640]{1,0:T(8,128)S(1)} %select_select_fusion.s0, ...), custom_call_target="tpu_custom_call" | custom-call | flops 5000000000 | bytes 18000000 | tf_op jit(solution)/shard_map/update/pallas_call | solution.py:218
  (48 shorter events, 1.5 us)
Async XLA Ops:
  0.8 4.1 %collective-permute-start = (f32[128,128]{1,0:T(8,128)S(1)}, f32[128,128]{1,0:T(8,128)S(1)}, u32[]{:S(2)}, u32[]{:S(2)}) collective-permute-start(f32[128,128]{1,0:T(8,128)S(1)} %slice.18), channel_id=1, source_target_pairs={{0,1},{1,0},{2,10},{3,11},{4,12},{5,13},{6,14},{7,15},{8,9},{9,8},... | collective-permute-start | bytes 196616 | tf_op jit(solution)/shard_map/ppermute | solution.py:271
  5.0 7.0 %collective-permute-start.2 = (f32[128,256]{1,0:T(8,128)S(1)}, f32[128,256]{1,0:T(8,128)S(1)}, u32[]{:S(2)}, u32[]{:S(2)}) collective-permute-start(f32[128,256]{1,0:T(8,128)S(1)} %maximum_select_fusion), channel_id=1, source_target_pairs={{0,6},{1,3},{2,10},{3,1},{4,12},{5,13},{6,0},{7,15},{8,14},{9,11},... | collective-permute-start | bytes 393224 | tf_op jit(solution)/shard_map/ppermute | solution.py:271
  9.4 7.6 %collective-permute-start.1 = (f32[128,256]{1,0:T(8,128)S(1)}, f32[128,256]{1,0:T(8,128)S(1)}, u32[]{:S(2)}, u32[]{:S(2)}) collective-permute-start(f32[128,256]{1,0:T(8,128)S(1)} %maximum_select_fusion), channel_id=1, source_target_pairs={{0,7},{1,2},{2,1},{3,11},{4,12},{5,13},{6,14},{7,0},{8,15},{9,10},... | collective-permute-start | bytes 393224 | tf_op jit(solution)/shard_map/ppermute | solution.py:271
  10.6 11.5 %collective-permute-start.5 = (f32[128,640]{1,0:T(8,128)S(1)}, f32[128,640]{1,0:T(8,128)S(1)}, u32[]{:S(2)}, u32[]{:S(2)}) collective-permute-start(f32[128,640]{1,0:T(8,128)S(1)} %get-tuple-element.47), channel_id=1, source_target_pairs={{0,192},{8,56},{16,24},{24,16},{32,40},{40,32},{48,8},{56,48},{64,... | collective-permute-start | bytes 983048 | tf_op jit(solution)/shard_map/ppermute | solution.py:271
  10.7 11.4 %collective-permute-start.4 = (f32[128,640]{1,0:T(8,128)S(1)}, f32[128,640]{1,0:T(8,128)S(1)}, u32[]{:S(2)}, u32[]{:S(2)}) collective-permute-start(f32[128,640]{1,0:T(8,128)S(1)} %get-tuple-element.48), channel_id=1, source_target_pairs={{0,128},{8,40},{16,24},{24,16},{32,8},{40,32},{48,56},{56,48},{64,... | collective-permute-start | bytes 983048 | tf_op jit(solution)/shard_map/ppermute | solution.py:271
  10.8 11.4 %collective-permute-start.3 = (f32[128,640]{1,0:T(8,128)S(1)}, f32[128,640]{1,0:T(8,128)S(1)}, u32[]{:S(2)}, u32[]{:S(2)}) collective-permute-start(f32[128,640]{1,0:T(8,128)S(1)} %get-tuple-element.49), channel_id=1, source_target_pairs={{0,64},{8,24},{16,8},{24,16},{32,40},{40,32},{48,56},{56,48},{64,7... | collective-permute-start | bytes 983048 | tf_op jit(solution)/shard_map/ppermute | solution.py:271
  23.2 1.5 %collective-permute-start.6 = (f32[128,256]{1,0:T(8,128)S(1)}, f32[128,256]{1,0:T(8,128)S(1)}, u32[]{:S(2)}, u32[]{:S(2)}) collective-permute-start(f32[128,256]{1,0:T(8,128)S(1)} %select_select_fusion.2), channel_id=1, source_target_pairs={{0,8},{1,9},{2,10},{3,4},{4,3},{5,6},{6,5},{7,15},{8,0},{9,1},{10,... | collective-permute-start | bytes 393224 | tf_op jit(solution)/shard_map/ppermute | solution.py:271
  24.7 12.3 %collective-permute-start.9 = (f32[128,256]{1,0:T(8,128)S(1)}, f32[128,256]{1,0:T(8,128)S(1)}, u32[]{:S(2)}, u32[]{:S(2)}) collective-permute-start(f32[128,256]{1,0:T(8,128)S(1)} %broadcast_select_fusion.2), channel_id=1, source_target_pairs={{0,48},{8,200},{16,24},{24,16},{32,40},{40,32},{48,56},{56,0},{64,... | collective-permute-start | bytes 393224 | tf_op jit(solution)/shard_map/ppermute | solution.py:271
  24.8 12.2 %collective-permute-start.8 = (f32[128,256]{1,0:T(8,128)S(1)}, f32[128,256]{1,0:T(8,128)S(1)}, u32[]{:S(2)}, u32[]{:S(2)}) collective-permute-start(f32[128,256]{1,0:T(8,128)S(1)} %broadcast_select_fusion.2), channel_id=1, source_target_pairs={{0,32},{8,136},{16,24},{24,16},{32,40},{40,0},{48,56},{56,48},{64,... | collective-permute-start | bytes 393224 | tf_op jit(solution)/shard_map/ppermute | solution.py:271
  24.9 17.6 %collective-permute-start.7 = (f32[128,256]{1,0:T(8,128)S(1)}, f32[128,256]{1,0:T(8,128)S(1)}, u32[]{:S(2)}, u32[]{:S(2)}) collective-permute-start(f32[128,256]{1,0:T(8,128)S(1)} %broadcast_select_fusion.2), channel_id=1, source_target_pairs={{0,16},{8,72},{16,24},{24,0},{32,40},{40,32},{48,56},{56,48},{64,8... | collective-permute-start | bytes 393224 | tf_op jit(solution)/shard_map/ppermute | solution.py:271
  25.0 17.6 %collective-permute-start.15 = (f32[128,640]{1,0:T(8,128)S(1)}, f32[128,640]{1,0:T(8,128)S(1)}, u32[]{:S(2)}, u32[]{:S(2)}) collective-permute-start(f32[128,640]{1,0:T(8,128)S(1)} %select_select_fusion.1), channel_id=1, source_target_pairs={{0,48},{8,200},{16,24},{24,216},{32,40},{40,232},{48,0},{56,248},{... | collective-permute-start | bytes 983048 | tf_op jit(solution)/shard_map/ppermute | solution.py:271
  27.8 14.9 %collective-permute-start.14 = (f32[128,640]{1,0:T(8,128)S(1)}, f32[128,640]{1,0:T(8,128)S(1)}, u32[]{:S(2)}, u32[]{:S(2)}) collective-permute-start(f32[128,640]{1,0:T(8,128)S(1)} %select_select_fusion.1), channel_id=1, source_target_pairs={{0,32},{8,136},{16,24},{24,152},{32,0},{40,168},{48,56},{56,184},{... | collective-permute-start | bytes 983048 | tf_op jit(solution)/shard_map/ppermute | solution.py:271
  37.0 6.5 %collective-permute-start.13 = (f32[128,640]{1,0:T(8,128)S(1)}, f32[128,640]{1,0:T(8,128)}, u32[]{:S(2)}, u32[]{:S(2)}) collective-permute-start(f32[128,640]{1,0:T(8,128)S(1)} %select_select_fusion.1), channel_id=1, source_target_pairs={{0,16},{8,72},{16,0},{24,88},{32,40},{40,104},{48,56},{56,120},{64... | collective-permute-start | bytes 983048 | tf_op jit(solution)/shard_map/ppermute | solution.py:271
  37.0 10.8 %collective-permute-start.16 = (f32[640,128]{1,0:T(8,128)S(1)}, f32[640,128]{1,0:T(8,128)S(1)}, u32[]{:S(2)}, u32[]{:S(2)}) collective-permute-start(f32[640,128]{1,0:T(8,128)S(1)} %slice.23), channel_id=1, source_target_pairs={{0,4},{1,5},{2,10},{3,11},{4,0},{5,1},{6,14},{7,15},{8,12},{9,13},... | collective-permute-start | bytes 983048 | tf_op jit(solution)/shard_map/ppermute | solution.py:271
  42.5 6.5 %collective-permute-start.12 = (f32[128,256]{1,0:T(8,128)S(1)}, f32[128,256]{1,0:T(8,128)S(1)}, u32[]{:S(2)}, u32[]{:S(2)}) collective-permute-start(f32[128,256]{1,0:T(8,128)S(1)} %select_select_fusion.5), channel_id=1, source_target_pairs={{0,192},{8,56},{16,208},{24,16},{32,224},{40,32},{48,240},{56,8},{... | collective-permute-start | bytes 393224 | tf_op jit(solution)/shard_map/ppermute | solution.py:271
  42.6 0.7 copy-start
  42.6 6.4 %collective-permute-start.11 = (f32[128,256]{1,0:T(8,128)S(1)}, f32[128,256]{1,0:T(8,128)S(1)}, u32[]{:S(2)}, u32[]{:S(2)}) collective-permute-start(f32[128,256]{1,0:T(8,128)S(1)} %select_select_fusion.5), channel_id=1, source_target_pairs={{0,128},{8,40},{16,144},{24,16},{32,160},{40,8},{48,176},{56,48},{... | collective-permute-start | bytes 393224 | tf_op jit(solution)/shard_map/ppermute | solution.py:271
  42.7 0.7 copy-start.1
  42.7 6.3 %collective-permute-start.10 = (f32[128,256]{1,0:T(8,128)S(1)}, f32[128,256]{1,0:T(8,128)S(1)}, u32[]{:S(2)}, u32[]{:S(2)}) collective-permute-start(f32[128,256]{1,0:T(8,128)S(1)} %select_select_fusion.5), channel_id=1, source_target_pairs={{0,64},{8,24},{16,80},{24,8},{32,96},{40,32},{48,112},{56,48},{64,... | collective-permute-start | bytes 393224 | tf_op jit(solution)/shard_map/ppermute | solution.py:271
  43.4 31.3 %slice-start = ((s8[6553600]{0:T(1024)(128)(4,1)}), s8[2359296]{0:T(1024)(128)(4,1)S(1)}, s32[]{:S(2)}) async-start(s8[6553600]{0:T(1024)(128)(4,1)} %bitcast.5), calls=%async_computation | async-start | bytes 4718592
  49.0 17.3 %collective-permute-start.18 = (f32[640,128]{1,0:T(8,128)S(1)}, f32[640,128]{1,0:T(8,128)}, u32[]{:S(2)}, u32[]{:S(2)}) collective-permute-start(f32[640,128]{1,0:T(8,128)S(1)} %broadcast_select_fusion.1), channel_id=1, source_target_pairs={{0,2},{1,3},{2,0},{3,1},{4,6},{5,7},{6,4},{7,5},{8,10},{9,11},{10,... | collective-permute-start | bytes 983048 | tf_op jit(solution)/shard_map/ppermute | solution.py:271
  49.1 2.5 %collective-permute-start.17 = (f32[128,256]{1,0:T(8,128)S(1)}, f32[128,256]{1,0:T(8,128)S(1)}, u32[]{:S(2)}, u32[]{:S(2)}) collective-permute-start(f32[128,256]{1,0:T(8,128)S(1)} %select_select_fusion.4.mine), channel_id=1, source_target_pairs={{0,8},{8,0},{16,24},{24,16},{32,40},{40,32},{48,56},{56,48},{64,72... | collective-permute-start | bytes 393224 | tf_op jit(solution)/shard_map/ppermute | solution.py:289
  49.3 19.0 %collective-permute-start.22 = (f32[128,640]{1,0:T(8,128)S(1)}, f32[128,640]{1,0:T(8,128)S(1)}, u32[]{:S(2)}, u32[]{:S(2)}) collective-permute-start(f32[128,640]{1,0:T(8,128)S(1)} %select_select_fusion.s0), channel_id=1, source_target_pairs={{0,192},{16,208},{32,224},{48,240},{64,0},{80,16},{96,32},{112,48}... | collective-permute-start | bytes 983048 | tf_op jit(solution)/shard_map/ppermute | solution.py:329
  50.9 17.5 %collective-permute-start.21 = (f32[128,640]{1,0:T(8,128)S(1)}, f32[128,640]{1,0:T(8,128)S(1)}, u32[]{:S(2)}, u32[]{:S(2)}) collective-permute-start(f32[128,640]{1,0:T(8,128)S(1)} %select_select_fusion.s0), channel_id=1, source_target_pairs={{0,128},{16,144},{32,160},{48,176},{64,192},{80,208},{96,224},{112... | collective-permute-start | bytes 983048 | tf_op jit(solution)/shard_map/ppermute | solution.py:329
  50.9 17.5 %collective-permute-start.20 = (f32[128,640]{1,0:T(8,128)S(1)}, f32[128,640]{1,0:T(8,128)S(1)}, u32[]{:S(2)}, u32[]{:S(2)}) collective-permute-start(f32[128,640]{1,0:T(8,128)S(1)} %select_select_fusion.s0), channel_id=1, source_target_pairs={{0,64},{16,80},{32,96},{48,112},{64,128},{80,144},{96,160},{112,17... | collective-permute-start | bytes 983048 | tf_op jit(solution)/shard_map/ppermute | solution.py:329
  57.2 17.6 %slice-start.1 = ((s8[6553600]{0:T(1024)(128)(4,1)}), s8[4194304]{0:T(1024)(128)(4,1)S(1)}, s32[]{:S(2)}) async-start(s8[6553600]{0:T(1024)(128)(4,1)} %bitcast.5), calls=%async_computation.1 | async-start | bytes 8388608
  66.4 8.4 %collective-permute-start.19 = (f32[640,128]{1,0:T(8,128)S(1)}, f32[640,128]{1,0:T(8,128)S(1)}, u32[]{:S(2)}, u32[]{:S(2)}) collective-permute-start(f32[640,128]{1,0:T(8,128)S(1)} %broadcast_select_fusion.h0), channel_id=1, source_target_pairs={{0,1},{1,0},{2,3},{3,2},{4,5},{5,4},{6,7},{7,6},{8,9},{9,8},{10,11... | collective-permute-start | bytes 983048 | tf_op jit(solution)/shard_map/ppermute | solution.py:271
  68.4 6.3 %collective-permute-start.23 = (f32[128,640]{1,0:T(8,128)S(1)}, f32[128,640]{1,0:T(8,128)S(1)}, u32[]{:S(2)}, u32[]{:S(2)}) collective-permute-start(f32[128,640]{1,0:T(8,128)S(1)} %select_select_fusion.s0), channel_id=1, source_target_pairs={{0,8},{8,0},{16,24},{24,16},{32,40},{40,32},{48,56},{56,48},{64,72... | collective-permute-start | bytes 983048 | tf_op jit(solution)/shard_map/ppermute | solution.py:289
  69.5 5.3 %collective-permute-start.24 = (f32[128,640]{1,0:T(8,128)S(1)}, f32[128,640]{1,0:T(8,128)S(1)}, u32[]{:S(2)}, u32[]{:S(2)}) collective-permute-start(f32[128,640]{1,0:T(8,128)S(1)} %collective-permute-done.20.s1), channel_id=1, source_target_pairs={{0,8},{8,0},{16,24},{24,16},{32,40},{40,32},{48,56},{56,48},{64,72... | collective-permute-start | bytes 983048 | tf_op jit(solution)/shard_map/ppermute | solution.py:289
  69.6 5.2 %collective-permute-start.25 = (f32[128,640]{1,0:T(8,128)S(1)}, f32[128,640]{1,0:T(8,128)S(1)}, u32[]{:S(2)}, u32[]{:S(2)}) collective-permute-start(f32[128,640]{1,0:T(8,128)S(1)} %collective-permute-done.21.s2), channel_id=1, source_target_pairs={{0,8},{8,0},{16,24},{24,16},{32,40},{40,32},{48,56},{56,48},{64,72... | collective-permute-start | bytes 983048 | tf_op jit(solution)/shard_map/ppermute | solution.py:289
  70.0 4.8 %collective-permute-start.26 = (f32[128,640]{1,0:T(8,128)S(1)}, f32[128,640]{1,0:T(8,128)S(1)}, u32[]{:S(2)}, u32[]{:S(2)}) collective-permute-start(f32[128,640]{1,0:T(8,128)S(1)} %collective-permute-done.22.s3), channel_id=1, source_target_pairs={{0,8},{8,0},{16,24},{24,16},{32,40},{40,32},{48,56},{56,48},{64,72... | collective-permute-start | bytes 983048 | tf_op jit(solution)/shard_map/ppermute | solution.py:289

commit v5 on v4

--- a/solution.py
+++ b/solution.py
@@ -278,6 +278,31 @@
     return out
 
 
+def fetch_kernel(k_ref, *refs):
+    outs, sems = refs[:-1], refs[-1]
+    w = k_ref.shape[1] // 4
+    views = [k_ref.at[:NB, :NB], k_ref.at[:, :NB]] + [k_ref.at[:NB, j * w : (j + 1) * w] for j in range(4)]
+    copies = [pltpu.make_async_copy(v, o, sems.at[i]) for i, (v, o) in enumerate(zip(views, outs))]
+    for copy in copies:
+        copy.start()
+    for copy in copies:
+        copy.wait()
+
+
+def fetch(kernel):
+    r, c = kernel.shape
+    shapes = [(NB, NB), (r, NB)] + [(NB, c // 4)] * 4
+    return pl.pallas_call(
+        fetch_kernel,
+        in_specs=[pl.BlockSpec(memory_space=pl.ANY)],
+        out_specs=vmem(len(shapes)),
+        out_shape=[sds(*shape) for shape in shapes],
+        scratch_shapes=[pltpu.SemaphoreType.DMA((len(shapes),))],
+        compiler_params=pltpu.CompilerParams(vmem_limit_bytes=56 * 1024 * 1024),
+        name="fetch",
+    )(kernel)
+
+
 def local(kernel):
     row = lax.axis_index("row")
     z = lax.axis_index("col")
@@ -291,39 +316,38 @@
     in_lines = lambda pairs: [(r * 8 + a, r * 8 + b) for r in range(32) for a, b in pairs]
     w = kernel.shape[1] // 4
 
-    own = kernel[:NB, :NB]
-    quarters = [kernel[:NB, j * w : (j + 1) * w] for j in range(4)]
+    own, first, *quarters = fetch(kernel)
+
     other = whole_permute(own, BOTH, in_line(((0, 1), (1, 0))))
     scattered = [
         whole_permute(quarters[j], "row", [(place(c, 0, 0), place(c, j, 0)) for c in (0, 1)]) for j in (2, 1, 3)
     ]
+    far = whole_permute(first, BOTH, in_lines(((0, 4), (1, 5))))
+    other, scattered = lax.optimization_barrier((other, scattered))
+
     corner = jnp.where(z == 0, jnp.concatenate([own, other], 1), jnp.concatenate([other, own], 1))
-    two = whole_permute(corner, BOTH, in_line(((0, 6), (1, 3))))
-    one = whole_permute(corner, BOTH, in_line(((0, 7), (1, 2))))
-    corner = pick(z, corner, corner, one, two, two, two, two, one)
+    got = [whole_permute(corner, BOTH, in_line(((0, 8 - n), (1, 1 + n)))) for n in (3, 2, 1)]
+    corner = pick(z, corner, corner, got[2], got[1], got[0], got[0], got[1], got[2])
     quarter = pick(p, quarters[0], scattered[1], scattered[0], scattered[2])
-    first = kernel[:, :NB]
-    corner, quarter, first = lax.optimization_barrier((corner, quarter, first))
-    last = whole_permute(corner, BOTH, in_line(((6, 5), (3, 4))))
-    corner = jnp.where((z == 4) | (z == 5), last, corner)
-
-    far = whole_permute(first, BOTH, in_lines(((0, 4), (1, 5))))
-
-    spread = [
-        whole_permute(quarter, "row", [(place(c, j, 0), place(c, j, n)) for c in (0, 1) for j in range(4)])
+    packed = jnp.concatenate([quarter, corner], 1)
+    half = jnp.where((z == 4) | (z == 5), far, first)
+    packed, half = lax.optimization_barrier((packed, half))
+
+    got = [
+        whole_permute(packed, "row", [(place(c, j, 0), place(c, j, n)) for c in (0, 1) for j in range(4)])
         for n in (2, 1, 3)
     ]
-    got = [whole_permute(corner, "row", [(place(c, 0, 0), place(c, 0, n)) for c in (0, 1)]) for n in (2, 1, 3)]
-    corner = pick(q, corner, got[1], got[0], got[2])
+    near = whole_permute(half, BOTH, in_lines(((0, 2), (1, 3), (4, 6), (5, 7))))
+    packed = pick(q, packed, got[1], got[0], got[2])
+    half = jnp.where((z % 4) < 2, half, near)
+    packed, half = lax.optimization_barrier((packed, half))
+    corner, quarter = packed[:, w:], packed[:, :w]
+
     got = [
         whole_permute(corner, "row", [(place(c, 0, i), place(c, n, i)) for c in (0, 1) for i in range(4)])
         for n in (2, 1, 3)
     ]
     corner = pick(p, corner, got[1], got[0], got[2])
-    quarter = pick(q, quarter, spread[1], spread[0], spread[2])
-    half = jnp.where((z == 4) | (z == 5), far, first)
-    corner, quarter, half = lax.optimization_barrier((corner, quarter, half))
-
     corner_other = swap(corner)
     slots = [
         lax.ppermute(
@@ -333,13 +357,10 @@
         )
         for n in (1, 2, 3)
     ]
-    near = whole_permute(half, BOTH, in_lines(((0, 2), (1, 3), (4, 6), (5, 7))))
+    half_other = whole_permute(half, BOTH, in_lines([(i, i ^ 1) for i in range(8)]))
     l0, w0, s = kernel_call(factor_first, "factor_first", [(2 * NB, NB), (NB, NB), (NB, NB)], 1)(
         core.astype(jnp.int32)[None], corner, corner_other
     )
-    half = jnp.where((z % 4) < 2, half, near)
-    s, half = lax.optimization_barrier((s, half))
-    half_other = whole_permute(half, BOTH, in_lines([(i, i ^ 1) for i in range(8)]))
     left, right = kernel_call(factor_second, "factor_second", [(NB, NB), (NB, NB)])(s)
     left, right, quarter, slots = lax.optimization_barrier((left, right, quarter, slots))
     slots = [quarter, *slots]

time: 83.3 us -> 80 us (0.960)
  waiting for transfers between devices: 37 us -> 26.4 us
  starting transfers between devices: 21.4 us -> 27.9 us
  local copies, waits for them, and re-layouts: 3.54 us -> 0.04 us
  Pallas kernels: 18.1 us -> 20.7 us
  other arithmetic: 2.51 us -> 4.2 us
    ppermute x19 -> x16, waiting for transfers between devices: 37 us -> 25.4 us  [whole_permute(): return lax.ppermute(v, axis, sorted(to.items()))]
    ppermute x19 -> x16, starting transfers between devices: 17.2 us -> 20.9 us  [whole_permute(): return lax.ppermute(v, axis, sorted(to.items()))]
    slice x3 -> x2, local copies, waits for them, and re-layouts: 3.08 us -> 0.03 us  [local(): corner, quarter = (packed[:, w:], packed[:, :w])]
    pallas_call x0 -> x1, Pallas kernels: none -> 2.65 us  [fetch(): pl.pallas_call(fetch_kernel, in_specs=[pl.BlockSpec(memory_space=pl.ANY)]...]
    ppermute x5, starting transfers between devices: 1.85 us -> 3.74 us  [local(): swap = lambda v: lax.ppermute(v, 'row', [(i, i ^ 1) for i in range(32)])]
    select_n x1, other arithmetic: 0.04 us -> 1.02 us  [local(): half = jnp.where((z == 4) | (z == 5), far, first)]
    ppermute x5, waiting for transfers between devices: 0.01 us -> 0.99 us  [local(): swap = lambda v: lax.ppermute(v, 'row', [(i, i ^ 1) for i in range(32)])]
    ppermute x3, starting transfers between devices: 2.34 us -> 3.31 us  [local(): lax.ppermute(quarter, 'row', [(place(c, j, i), place(c, (j + n) % 4, i))...]
  transfers between devices with their start and end apart: 27 -> 24, of which waited for: 9 -> 7; matrix products, arithmetic and copies ran while one was open for 4% -> 4% of each run, Pallas kernels for 12% -> 13%
where the time goes in v5:
time: 80 us; the launch traced here: 79.7 us
  starting transfers between devices  27.9 us (35%)
  waiting for transfers between devices  26.4 us (33%)
  Pallas kernels  20.7 us (26%)
  other arithmetic  4.2 us (5%)
    ppermute x16, waiting for transfers between devices, whole_permute(): return lax.ppermute(v, axis, sorted(to.items()))  25.4 us
    ppermute x16, starting transfers between devices, whole_permute(): return lax.ppermute(v, axis, sorted(to.items()))  20.9 us
    pallas_call x3, Pallas kernels, call(): pl.pallas_call(body, in_specs=[pl.BlockSpec(memory_space=pltpu.SMEM)] * s...  9.98 us
    pallas_call x1, Pallas kernels, update(): pl.pallas_call(update_kernel, out_shape=sds(r, c), in_specs=[pl.BlockSpec...  8.1 us
    ppermute x5, starting transfers between devices, local(): swap = lambda v: lax.ppermute(v, 'row', [(i, i ^ 1) for i in range(32)])  3.74 us
    ppermute x3, starting transfers between devices, local(): lax.ppermute(quarter, 'row', [(place(c, j, i), place(c, (j + n) % 4, i))...  3.31 us
    pallas_call x1, Pallas kernels, fetch(): pl.pallas_call(fetch_kernel, in_specs=[pl.BlockSpec(memory_space=pl.ANY)]...  2.65 us
    select_n x4, other arithmetic, pick(): out = jnp.where(i == n, values[n], out)  2.11 us
  transfers between devices with their start and end apart: 24, of which 7 were waited for; matrix products, arithmetic and copies ran while one was open for 4% of the time, Pallas kernels for 13%

profile of v5, /device:TPU:1, one launch (start us, length us, event | category | flops | bytes accessed | tf_op | source)
XLA Modules:
  0.0 79.7 jit_solution(14718867276675716318)
XLA Ops:
  0.0 2.6 %fetch.1 = (f32[128,128]{1,0:T(8,128)}, f32[640,128]{1,0:T(8,128)}, f32[128,640]{1,0:T(8,128)}, f32[128,640]{1,0:T(8,128)}, f32[128,640]{1,0:T(8,128)}, /*index=5*/f32[128,640]{1,0:T(8,128)}) custom-call(f32[640,2560]{1,0:T(8,128)} %k_ref.3), custom_call_target="tpu_custom_call" | custom-call | tf_op jit(solution)/shard_map/fetch/pallas_call | solution.py:295
  2.7 3.6 %collective-permute-start.1 = (f32[128,640]{1,0:T(8,128)}, f32[128,640]{1,0:T(8,128)S(1)}, u32[]{:S(2)}, u32[]{:S(2)}) collective-permute-start(f32[128,640]{1,0:T(8,128)} %get-tuple-element.34), channel_id=1, source_target_pairs={{0,128},{8,40},{16,24},{24,16},{32,8},{40,32},{48,56},{56,48},{64,... | collective-permute-start | bytes 983048 | tf_op jit(solution)/shard_map/ppermute | solution.py:271
  6.3 0.5 collective-permute-start.3
  6.8 1.6 %collective-permute-start = (f32[128,128]{1,0:T(8,128)}, f32[128,128]{1,0:T(8,128)S(1)}, u32[]{:S(2)}, u32[]{:S(2)}) collective-permute-start(f32[128,128]{1,0:T(8,128)} %get-tuple-element.33), channel_id=1, source_target_pairs={{0,1},{1,0},{2,10},{3,11},{4,12},{5,13},{6,14},{7,15},{8,9},{9,8},... | collective-permute-start | bytes 196616 | tf_op jit(solution)/shard_map/ppermute | solution.py:271
  8.5 6.2 %collective-permute-start.7 = (f32[640,128]{1,0:T(8,128)}, f32[640,128]{1,0:T(8,128)S(1)}, u32[]{:S(2)}, u32[]{:S(2)}) collective-permute-start(f32[640,128]{1,0:T(8,128)} %get-tuple-element.41), channel_id=1, source_target_pairs={{0,4},{1,5},{2,10},{3,11},{4,0},{5,1},{6,14},{7,15},{8,12},{9,13},... | collective-permute-start | bytes 983048 | tf_op jit(solution)/shard_map/ppermute | solution.py:271
  14.7 1.0 %collective-permute-done.3 = f32[128,640]{1,0:T(8,128)S(1)} collective-permute-done((f32[128,640]{1,0:T(8,128)}, f32[128,640]{1,0:T(8,128)S(1)}, u32[]{:S(2)}, u32[]{:S(2)}) %collective-permute-start.3) | collective-permute-done | bytes 327712 | tf_op jit(solution)/shard_map/ppermute | solution.py:271
  15.6 0.9 %maximum_select_fusion = f32[128,256]{1,0:T(8,128)S(1)} fusion(f32[128,128]{1,0:T(8,128)S(1)} %collective-permute-done, f32[128,128]{1,0:T(8,128)} %get-tuple-element.33, pred[]{:T(512)S(6)} %eq.58), kind=kLoop, calls=%fused_computation.9 | loop fusion | flops 98304 | bytes 262145 | tf_op jit(solution)/shard_map/jit(_where)/select_n | solution.py:328
  16.6 6.6 %collective-permute-start.6 = (f32[128,256]{1,0:T(8,128)S(1)}, f32[128,256]{1,0:T(8,128)S(1)}, u32[]{:S(2)}, u32[]{:S(2)}) collective-permute-start(f32[128,256]{1,0:T(8,128)S(1)} %maximum_select_fusion), channel_id=1, source_target_pairs={{0,5},{1,4},{2,10},{3,11},{4,1},{5,0},{6,14},{7,15},{8,13},{9,12},... | collective-permute-start | bytes 393224 | tf_op jit(solution)/shard_map/ppermute | solution.py:271
  23.1 1.0 %select_select_fusion.1 = f32[128,640]{1,0:T(8,128)S(1)} fusion(f32[128,640]{1,0:T(8,128)} %get-tuple-element.32, f32[128,640]{1,0:T(8,128)S(1)} %collective-permute-done.2, f32[128,640]{1,0:T(8,128)S(1)} %collective-permute-done.1, f32[128,640]{1,0:T(8,128)S(1)} %collective-permute-done.3, pred[]{:T(512)S(6)} %eq.57, pred[]{:T(512)S(6)} %eq.56, pred[]{:T(512)S(6)} %eq.55), kind=kLoop, calls=%fused_computation.2 | loop fusion | flops 245760 | bytes 1638403 | tf_op jit(solution)/shard_map/jit(_where)/select_n | solution.py:277
  24.2 1.0 %broadcast_select_fusion.1 = f32[640,128]{1,0:T(8,128)S(1)} fusion(f32[640,128]{1,0:T(8,128)S(1)} %collective-permute-done.7, f32[640,128]{1,0:T(8,128)} %get-tuple-element.41, pred[]{:T(512)S(6)} %or.3), kind=kLoop, calls=%fused_computation.6 | loop fusion | flops 81920 | bytes 983041 | tf_op jit(solution)/shard_map/jit(_where)/select_n | solution.py:333
  25.2 1.5 %collective-permute-done.6 = f32[128,256]{1,0:T(8,128)S(1)} collective-permute-done((f32[128,256]{1,0:T(8,128)S(1)}, f32[128,256]{1,0:T(8,128)S(1)}, u32[]{:S(2)}, u32[]{:S(2)}) %collective-permute-start.6) | collective-permute-done | bytes 131104 | tf_op jit(solution)/shard_map/ppermute | solution.py:271
  26.7 2.9 %collective-permute-done.5 = f32[128,256]{1,0:T(8,128)S(1)} collective-permute-done((f32[128,256]{1,0:T(8,128)S(1)}, f32[128,256]{1,0:T(8,128)S(1)}, u32[]{:S(2)}, u32[]{:S(2)}) %collective-permute-start.5) | collective-permute-done | bytes 131104 | tf_op jit(solution)/shard_map/ppermute | solution.py:271
  29.7 2.3 %collective-permute-done.4 = f32[128,256]{1,0:T(8,128)S(1)} collective-permute-done((f32[128,256]{1,0:T(8,128)S(1)}, f32[128,256]{1,0:T(8,128)S(1)}, u32[]{:S(2)}, u32[]{:S(2)}) %collective-permute-start.4) | collective-permute-done | bytes 131104 | tf_op jit(solution)/shard_map/ppermute | solution.py:271
  32.0 1.0 %select_select_fusion.2 = f32[128,256]{1,0:T(8,128)S(1)} fusion(f32[128,256]{1,0:T(8,128)S(1)} %collective-permute-done.4, f32[128,256]{1,0:T(8,128)S(1)} %collective-permute-done.5, f32[128,256]{1,0:T(8,128)S(1)} %collective-permute-done.6, pred[]{:T(512)S(6)} %eq.64, pred[]{:T(512)S(6)} %eq.63, pred[]{:T(512)S(6)} %eq.62, pred[]{:T(512)S(6)} %eq.61, ...), kind=kLoop, calls=%fused_computation.3 | loop fusion | flops 327680 | bytes 655367 | tf_op jit(solution)/shard_map/jit(_where)/select_n | solution.py:277
  33.0 2.0 %collective-permute-start.11 = (f32[640,128]{1,0:T(8,128)S(1)}, f32[640,128]{1,0:T(8,128)S(1)}, u32[]{:S(2)}, u32[]{:S(2)}) collective-permute-start(f32[640,128]{1,0:T(8,128)S(1)} %broadcast_select_fusion.1), channel_id=1, source_target_pairs={{0,2},{1,3},{2,0},{3,1},{4,6},{5,7},{6,4},{7,5},{8,10},{9,11},{10,... | collective-permute-start | bytes 983048 | tf_op jit(solution)/shard_map/ppermute | solution.py:271
  35.1 14.4 %collective-permute-done.11 = f32[640,128]{1,0:T(8,128)S(1)} collective-permute-done((f32[640,128]{1,0:T(8,128)S(1)}, f32[640,128]{1,0:T(8,128)S(1)}, u32[]{:S(2)}, u32[]{:S(2)}) %collective-permute-start.11) | collective-permute-done | bytes 327712 | tf_op jit(solution)/shard_map/ppermute | solution.py:271
  49.5 0.1 select_select_fusion
  49.6 0.1 collective-permute-start.15
  49.7 0.1 collective-permute-start.14
  50.0 2.6 %collective-permute-start.19 = (f32[128,640]{1,0:T(8,128)S(1)}, f32[128,640]{1,0:T(8,128)S(1)}, u32[]{:S(2)}, u32[]{:S(2)}) collective-permute-start(f32[128,640]{1,0:T(8,128)S(1)} %slice.7.s0), channel_id=1, source_target_pairs={{0,192},{16,208},{32,224},{48,240},{64,0},{80,16},{96,32},{112,48}... | collective-permute-start | bytes 983048 | tf_op jit(solution)/shard_map/ppermute | solution.py:353
  52.5 0.8 collective-permute-start.18
  53.3 3.2 %collective-permute-done.15 = f32[128,256]{1,0:T(8,128)S(1)} collective-permute-done((f32[128,256]{1,0:T(8,128)S(1)}, f32[128,256]{1,0:T(8,128)S(1)}, u32[]{:S(2)}, u32[]{:S(2)}) %collective-permute-start.15) | collective-permute-done | bytes 131104 | tf_op jit(solution)/shard_map/ppermute | solution.py:271
  56.5 2.6 %collective-permute-start.16 = (f32[128,256]{1,0:T(8,128)S(1)}, f32[128,256]{1,0:T(8,128)S(1)}, u32[]{:S(2)}, u32[]{:S(2)}) collective-permute-start(f32[128,256]{1,0:T(8,128)S(1)} %select_select_fusion.4.mine), channel_id=1, source_target_pairs={{0,8},{8,0},{16,24},{24,16},{32,40},{40,32},{48,56},{56,48},{64,72... | collective-permute-start | bytes 393224 | tf_op jit(solution)/shard_map/ppermute | solution.py:314
  59.2 1.0 %collective-permute-done.16.other = f32[128,256]{1,0:T(8,128)S(1)} collective-permute-done((f32[128,256]{1,0:T(8,128)S(1)}, f32[128,256]{1,0:T(8,128)S(1)}, u32[]{:S(2)}, u32[]{:S(2)}) %collective-permute-start.16) | collective-permute-done | bytes 131104 | tf_op jit(solution)/shard_map/ppermute | solution.py:314
  60.1 5.5 %factor_first.1 = (f32[256,128]{1,0:T(8,128)S(1)}, f32[128,128]{1,0:T(8,128)S(1)}, f32[128,128]{1,0:T(8,128)S(1)}) custom-call(s32[1]{0:T(128)} %bitcast.4.core, f32[128,256]{1,0:T(8,128)S(1)} %select_select_fusion.4.mine, f32[128,256]{1,0:T(8,128)S(1)} %collective-permute-done.16.other), custom_call_target="tpu_custom_call" | custom-call | flops 1000000000 | bytes 1000000 | tf_op jit(solution)/shard_map/factor_first/pallas_call | solution.py:374
  65.6 1.9 %factor_second.1 = (f32[128,128]{1,0:T(8,128)S(1)}, f32[128,128]{1,0:T(8,128)S(1)}) custom-call(f32[128,128]{1,0:T(8,128)S(1)} %get-tuple-element.46.s_ref), custom_call_target="tpu_custom_call" | custom-call | flops 1000000000 | bytes 1000000 | tf_op jit(solution)/shard_map/factor_second/pallas_call | solution.py:374
  67.6 0.4 collective-permute-start.20
  68.0 0.1 collective-permute-start.21
  68.2 0.4 collective-permute-start.22
  68.6 0.1 collective-permute-start.23
  68.8 2.6 %factor_third.1 = (f32[128,128]{1,0:T(8,128)S(1)}, f32[128,256]{1,0:T(8,128)S(1)}) custom-call(f32[128,128]{1,0:T(8,128)S(1)} %get-tuple-element.55.a_ref, f32[128,128]{1,0:T(8,128)S(1)} %get-tuple-element.56.i_ref, f32[256,128]{1,0:T(8,128)S(1)} %get-tuple-element.53.l_ref.l0_ref, f32[128,128]{1,0:T(8,128)S(1)} %get-tuple-element.54.w0_ref), custom_call_target="tpu_custom_call" | custom-call | flops 1000000000 | bytes 1000000 | tf_op jit(solution)/shard_map/factor_third/pallas_call | solution.py:374
  71.4 8.1 %update.1 = f32[640,2560]{1,0:T(8,128)} custom-call(s32[4]{0:T(128)S(1)} %pad_add_fusion.info, f32[640,2560]{1,0:T(8,128)S(1)} %bitcast.6, f32[640,128]{1,0:T(8,128)S(1)} %broadcast_select_fusion.h0, f32[640,128]{1,0:T(8,128)S(1)} %collective-permute-done.12.h1, f32[128,640]{1,0:T(8,128)S(1)} %slice.7.s0, f32[128,640]{1,0:T(8,128)S(1)} %collective-permute-done.17.s1, ...), custom_call_target="tpu_custom_call" | custom-call | flops 5000000000 | bytes 18000000 | tf_op jit(solution)/shard_map/update/pallas_call | solution.py:218
  (37 shorter events, 0.4 us)
Async XLA Ops:
  2.7 12.0 %collective-permute-start.1 = (f32[128,640]{1,0:T(8,128)}, f32[128,640]{1,0:T(8,128)S(1)}, u32[]{:S(2)}, u32[]{:S(2)}) collective-permute-start(f32[128,640]{1,0:T(8,128)} %get-tuple-element.34), channel_id=1, source_target_pairs={{0,128},{8,40},{16,24},{24,16},{32,8},{40,32},{48,56},{56,48},{64,... | collective-permute-start | bytes 983048 | tf_op jit(solution)/shard_map/ppermute | solution.py:271
  6.3 8.4 %collective-permute-start.2 = (f32[128,640]{1,0:T(8,128)}, f32[128,640]{1,0:T(8,128)S(1)}, u32[]{:S(2)}, u32[]{:S(2)}) collective-permute-start(f32[128,640]{1,0:T(8,128)} %get-tuple-element.35), channel_id=1, source_target_pairs={{0,64},{8,24},{16,8},{24,16},{32,40},{40,32},{48,56},{56,48},{64,7... | collective-permute-start | bytes 983048 | tf_op jit(solution)/shard_map/ppermute | solution.py:271
  6.3 9.3 %collective-permute-start.3 = (f32[128,640]{1,0:T(8,128)}, f32[128,640]{1,0:T(8,128)S(1)}, u32[]{:S(2)}, u32[]{:S(2)}) collective-permute-start(f32[128,640]{1,0:T(8,128)} %get-tuple-element.36), channel_id=1, source_target_pairs={{0,192},{8,56},{16,24},{24,16},{32,40},{40,32},{48,8},{56,48},{64,... | collective-permute-start | bytes 983048 | tf_op jit(solution)/shard_map/ppermute | solution.py:271
  6.8 7.8 %collective-permute-start = (f32[128,128]{1,0:T(8,128)}, f32[128,128]{1,0:T(8,128)S(1)}, u32[]{:S(2)}, u32[]{:S(2)}) collective-permute-start(f32[128,128]{1,0:T(8,128)} %get-tuple-element.33), channel_id=1, source_target_pairs={{0,1},{1,0},{2,10},{3,11},{4,12},{5,13},{6,14},{7,15},{8,9},{9,8},... | collective-permute-start | bytes 196616 | tf_op jit(solution)/shard_map/ppermute | solution.py:271
  8.5 15.7 %collective-permute-start.7 = (f32[640,128]{1,0:T(8,128)}, f32[640,128]{1,0:T(8,128)S(1)}, u32[]{:S(2)}, u32[]{:S(2)}) collective-permute-start(f32[640,128]{1,0:T(8,128)} %get-tuple-element.41), channel_id=1, source_target_pairs={{0,4},{1,5},{2,10},{3,11},{4,0},{5,1},{6,14},{7,15},{8,12},{9,13},... | collective-permute-start | bytes 983048 | tf_op jit(solution)/shard_map/ppermute | solution.py:271
  16.6 10.2 %collective-permute-start.6 = (f32[128,256]{1,0:T(8,128)S(1)}, f32[128,256]{1,0:T(8,128)S(1)}, u32[]{:S(2)}, u32[]{:S(2)}) collective-permute-start(f32[128,256]{1,0:T(8,128)S(1)} %maximum_select_fusion), channel_id=1, source_target_pairs={{0,5},{1,4},{2,10},{3,11},{4,1},{5,0},{6,14},{7,15},{8,13},{9,12},... | collective-permute-start | bytes 393224 | tf_op jit(solution)/shard_map/ppermute | solution.py:271
  23.1 6.6 %collective-permute-start.5 = (f32[128,256]{1,0:T(8,128)S(1)}, f32[128,256]{1,0:T(8,128)S(1)}, u32[]{:S(2)}, u32[]{:S(2)}) collective-permute-start(f32[128,256]{1,0:T(8,128)S(1)} %maximum_select_fusion), channel_id=1, source_target_pairs={{0,6},{1,3},{2,10},{3,1},{4,12},{5,13},{6,0},{7,15},{8,14},{9,11},... | collective-permute-start | bytes 393224 | tf_op jit(solution)/shard_map/ppermute | solution.py:271
  23.1 8.9 %collective-permute-start.4 = (f32[128,256]{1,0:T(8,128)S(1)}, f32[128,256]{1,0:T(8,128)S(1)}, u32[]{:S(2)}, u32[]{:S(2)}) collective-permute-start(f32[128,256]{1,0:T(8,128)S(1)} %maximum_select_fusion), channel_id=1, source_target_pairs={{0,7},{1,2},{2,1},{3,11},{4,12},{5,13},{6,14},{7,0},{8,15},{9,10},... | collective-permute-start | bytes 393224 | tf_op jit(solution)/shard_map/ppermute | solution.py:271
  33.0 16.4 %collective-permute-start.11 = (f32[640,128]{1,0:T(8,128)S(1)}, f32[640,128]{1,0:T(8,128)S(1)}, u32[]{:S(2)}, u32[]{:S(2)}) collective-permute-start(f32[640,128]{1,0:T(8,128)S(1)} %broadcast_select_fusion.1), channel_id=1, source_target_pairs={{0,2},{1,3},{2,0},{3,1},{4,6},{5,7},{6,4},{7,5},{8,10},{9,11},{10,... | collective-permute-start | bytes 983048 | tf_op jit(solution)/shard_map/ppermute | solution.py:271
  35.0 14.5 %collective-permute-start.10 = (f32[128,896]{1,0:T(8,128)S(1)}, f32[128,896]{1,0:T(8,128)S(1)}, u32[]{:S(2)}, u32[]{:S(2)}) collective-permute-start(f32[128,896]{1,0:T(8,128)S(1)} %pad_maximum_fusion), channel_id=1, source_target_pairs={{0,48},{8,200},{16,24},{24,216},{32,40},{40,232},{48,0},{56,248},{... | collective-permute-start | bytes 1376264 | tf_op jit(solution)/shard_map/ppermute | solution.py:271
  35.0 14.5 %collective-permute-start.9 = (f32[128,896]{1,0:T(8,128)S(1)}, f32[128,896]{1,0:T(8,128)S(1)}, u32[]{:S(2)}, u32[]{:S(2)}) collective-permute-start(f32[128,896]{1,0:T(8,128)S(1)} %pad_maximum_fusion), channel_id=1, source_target_pairs={{0,32},{8,136},{16,24},{24,152},{32,0},{40,168},{48,56},{56,184},{... | collective-permute-start | bytes 1376264 | tf_op jit(solution)/shard_map/ppermute | solution.py:271
  35.0 14.5 %collective-permute-start.8 = (f32[128,896]{1,0:T(8,128)S(1)}, f32[128,896]{1,0:T(8,128)S(1)}, u32[]{:S(2)}, u32[]{:S(2)}) collective-permute-start(f32[128,896]{1,0:T(8,128)S(1)} %pad_maximum_fusion), channel_id=1, source_target_pairs={{0,16},{8,72},{16,0},{24,88},{32,40},{40,104},{48,56},{56,120},{64... | collective-permute-start | bytes 1376264 | tf_op jit(solution)/shard_map/ppermute | solution.py:271
  49.5 21.9 %slice-start = ((s8[6553600]{0:T(1024)(128)(4,1)}), s8[4194304]{0:T(1024)(128)(4,1)S(1)}, s32[]{:S(2)}) async-start(s8[6553600]{0:T(1024)(128)(4,1)} %bitcast.5), calls=%async_computation | async-start | bytes 8388608
  49.6 6.8 %collective-permute-start.15 = (f32[128,256]{1,0:T(8,128)S(1)}, f32[128,256]{1,0:T(8,128)S(1)}, u32[]{:S(2)}, u32[]{:S(2)}) collective-permute-start(f32[128,256]{1,0:T(8,128)S(1)} %slice.6), channel_id=1, source_target_pairs={{0,192},{8,56},{16,208},{24,16},{32,224},{40,32},{48,240},{56,8},{... | collective-permute-start | bytes 393224 | tf_op jit(solution)/shard_map/ppermute | solution.py:271
  49.7 6.7 %collective-permute-start.14 = (f32[128,256]{1,0:T(8,128)S(1)}, f32[128,256]{1,0:T(8,128)S(1)}, u32[]{:S(2)}, u32[]{:S(2)}) collective-permute-start(f32[128,256]{1,0:T(8,128)S(1)} %slice.6), channel_id=1, source_target_pairs={{0,128},{8,40},{16,144},{24,16},{32,160},{40,8},{48,176},{56,48},{... | collective-permute-start | bytes 393224 | tf_op jit(solution)/shard_map/ppermute | solution.py:271
  49.8 6.6 %collective-permute-start.13 = (f32[128,256]{1,0:T(8,128)S(1)}, f32[128,256]{1,0:T(8,128)S(1)}, u32[]{:S(2)}, u32[]{:S(2)}) collective-permute-start(f32[128,256]{1,0:T(8,128)S(1)} %slice.6), channel_id=1, source_target_pairs={{0,64},{8,24},{16,80},{24,8},{32,96},{40,32},{48,112},{56,48},{64,... | collective-permute-start | bytes 393224 | tf_op jit(solution)/shard_map/ppermute | solution.py:271
  50.0 17.6 %collective-permute-start.19 = (f32[128,640]{1,0:T(8,128)S(1)}, f32[128,640]{1,0:T(8,128)S(1)}, u32[]{:S(2)}, u32[]{:S(2)}) collective-permute-start(f32[128,640]{1,0:T(8,128)S(1)} %slice.7.s0), channel_id=1, source_target_pairs={{0,192},{16,208},{32,224},{48,240},{64,0},{80,16},{96,32},{112,48}... | collective-permute-start | bytes 983048 | tf_op jit(solution)/shard_map/ppermute | solution.py:353
  52.5 15.1 %collective-permute-start.18 = (f32[128,640]{1,0:T(8,128)S(1)}, f32[128,640]{1,0:T(8,128)S(1)}, u32[]{:S(2)}, u32[]{:S(2)}) collective-permute-start(f32[128,640]{1,0:T(8,128)S(1)} %slice.7.s0), channel_id=1, source_target_pairs={{0,128},{16,144},{32,160},{48,176},{64,192},{80,208},{96,224},{112... | collective-permute-start | bytes 983048 | tf_op jit(solution)/shard_map/ppermute | solution.py:353
  56.5 11.1 %collective-permute-start.17 = (f32[128,640]{1,0:T(8,128)S(1)}, f32[128,640]{1,0:T(8,128)S(1)}, u32[]{:S(2)}, u32[]{:S(2)}) collective-permute-start(f32[128,640]{1,0:T(8,128)S(1)} %slice.7.s0), channel_id=1, source_target_pairs={{0,64},{16,80},{32,96},{48,112},{64,128},{80,144},{96,160},{112,17... | collective-permute-start | bytes 983048 | tf_op jit(solution)/shard_map/ppermute | solution.py:353
  56.5 3.6 %collective-permute-start.16 = (f32[128,256]{1,0:T(8,128)S(1)}, f32[128,256]{1,0:T(8,128)S(1)}, u32[]{:S(2)}, u32[]{:S(2)}) collective-permute-start(f32[128,256]{1,0:T(8,128)S(1)} %select_select_fusion.4.mine), channel_id=1, source_target_pairs={{0,8},{8,0},{16,24},{24,16},{32,40},{40,32},{48,56},{56,48},{64,72... | collective-permute-start | bytes 393224 | tf_op jit(solution)/shard_map/ppermute | solution.py:314
  59.2 12.2 %collective-permute-start.12 = (f32[640,128]{1,0:T(8,128)S(1)}, f32[640,128]{1,0:T(8,128)S(1)}, u32[]{:S(2)}, u32[]{:S(2)}) collective-permute-start(f32[640,128]{1,0:T(8,128)S(1)} %broadcast_select_fusion.h0), channel_id=1, source_target_pairs={{0,1},{1,0},{2,3},{3,2},{4,5},{5,4},{6,7},{7,6},{8,9},{9,8},{10,11... | collective-permute-start | bytes 983048 | tf_op jit(solution)/shard_map/ppermute | solution.py:271
  60.1 11.3 %slice-start.1 = ((s8[6553600]{0:T(1024)(128)(4,1)}), s8[2359296]{0:T(1024)(128)(4,1)S(1)}, s32[]{:S(2)}) async-start(s8[6553600]{0:T(1024)(128)(4,1)} %bitcast.5), calls=%async_computation.1 | async-start | bytes 4718592
  67.6 3.8 %collective-permute-start.20 = (f32[128,640]{1,0:T(8,128)S(1)}, f32[128,640]{1,0:T(8,128)S(1)}, u32[]{:S(2)}, u32[]{:S(2)}) collective-permute-start(f32[128,640]{1,0:T(8,128)S(1)} %slice.7.s0), channel_id=1, source_target_pairs={{0,8},{8,0},{16,24},{24,16},{32,40},{40,32},{48,56},{56,48},{64,72... | collective-permute-start | bytes 983048 | tf_op jit(solution)/shard_map/ppermute | solution.py:314
  68.0 3.3 %collective-permute-start.21 = (f32[128,640]{1,0:T(8,128)S(1)}, f32[128,640]{1,0:T(8,128)S(1)}, u32[]{:S(2)}, u32[]{:S(2)}) collective-permute-start(f32[128,640]{1,0:T(8,128)S(1)} %collective-permute-done.17.s1), channel_id=1, source_target_pairs={{0,8},{8,0},{16,24},{24,16},{32,40},{40,32},{48,56},{56,48},{64,72... | collective-permute-start | bytes 983048 | tf_op jit(solution)/shard_map/ppermute | solution.py:314
  68.2 3.2 %collective-permute-start.22 = (f32[128,640]{1,0:T(8,128)S(1)}, f32[128,640]{1,0:T(8,128)S(1)}, u32[]{:S(2)}, u32[]{:S(2)}) collective-permute-start(f32[128,640]{1,0:T(8,128)S(1)} %collective-permute-done.18.s2), channel_id=1, source_target_pairs={{0,8},{8,0},{16,24},{24,16},{32,40},{40,32},{48,56},{56,48},{64,72... | collective-permute-start | bytes 983048 | tf_op jit(solution)/shard_map/ppermute | solution.py:314
  68.6 2.8 %collective-permute-start.23 = (f32[128,640]{1,0:T(8,128)S(1)}, f32[128,640]{1,0:T(8,128)S(1)}, u32[]{:S(2)}, u32[]{:S(2)}) collective-permute-start(f32[128,640]{1,0:T(8,128)S(1)} %collective-permute-done.19.s3), channel_id=1, source_target_pairs={{0,8},{8,0},{16,24},{24,16},{32,40},{40,32},{48,56},{56,48},{64,72... | collective-permute-start | bytes 983048 | tf_op jit(solution)/shard_map/ppermute | solution.py:314

commit v6 on v4

--- a/solution.py
+++ b/solution.py
@@ -103,18 +103,8 @@
     s_ref[...] = bottom[:, NB:] - mmt(l10, l10)
 
 
-def factor_second(s_ref, a_ref, i_ref):
-    u, w, (a, i) = eliminate(s_ref[...], identity(), 0, NB // 16)
-    a_ref[: NB // 2] = u
-    a_ref[NB // 2 :] = a
-    i_ref[: NB // 2] = w
-    i_ref[NB // 2 :] = i
-
-
-def factor_third(a_ref, i_ref, l_ref, w0_ref, l1_ref, w1_ref):
-    u, w, _ = eliminate(a_ref[...], i_ref[...], NB // 16, NB // 8)
-    u = jnp.concatenate([a_ref[: NB // 2], u], 0)
-    w = jnp.concatenate([i_ref[: NB // 2], w], 0)
+def factor_second(s_ref, l_ref, w0_ref, l1_ref, w1_ref):
+    u, w, _ = eliminate(s_ref[...], identity(), 0, NB // 8)
     l1_ref[...] = u.T
     w1_ref[:, :NB] = -mm(mm(w, l_ref[NB:, :]), w0_ref[...])
     w1_ref[:, NB:] = w
@@ -286,46 +276,47 @@
     q = jnp.where(core == 0, x, y)
     info = jnp.stack([y, x, row, z]).astype(jnp.int32)
 
+    own = kernel[:NB, :NB]
+    other = whole_permute(own, BOTH, [(r * 8 + a, r * 8 + 1 - a) for r in (0, 1) for a in (0, 1)])
+    corner = jnp.where(z == 0, jnp.concatenate([own, other], 1), jnp.concatenate([other, own], 1))
+    got = [
+        whole_permute(corner, BOTH, [(r * 8 + a, r * 8 + b) for r in (0, 1) for a, b in ((0, 8 - n), (1, 1 + n))])
+        for n in (3, 2, 1)
+    ]
+    corner = pick(z, corner, corner, got[2], got[1], got[0], got[0], got[1], got[2])
+    first = kernel[:, :NB]
+    corner, first = lax.optimization_barrier((corner, first))
+    got = [
+        whole_permute(corner, "row", [(place(c, 0, 0), place(c, 0, n)) for c in (0, 1)]) for n in (2, 1, 3)
+    ]
+    corner = pick(q, corner, got[1], got[0], got[2])
+    got = [
+        whole_permute(corner, "row", [(place(c, 0, i), place(c, n, i)) for c in (0, 1) for i in range(4)])
+        for n in (2, 1, 3)
+    ]
+    corner = pick(p, corner, got[1], got[0], got[2])
     swap = lambda v: lax.ppermute(v, "row", [(i, i ^ 1) for i in range(32)])
-    in_line = lambda pairs: [(r * 8 + a, r * 8 + b) for r in (0, 1) for a, b in pairs]
-    in_lines = lambda pairs: [(r * 8 + a, r * 8 + b) for r in range(32) for a, b in pairs]
+    corner_other = swap(corner)
+
+    mesh_line = lambda pairs: [(r * 8 + a, r * 8 + b) for r in range(32) for a, b in pairs]
+    far = whole_permute(first, BOTH, mesh_line(((0, 4), (1, 5))))
+    half = jnp.where((z == 4) | (z == 5), far, first)
+    near = whole_permute(half, BOTH, mesh_line(((0, 2), (1, 3), (4, 6), (5, 7))))
+    half = jnp.where((z % 4) < 2, half, near)
+    half_other = whole_permute(half, BOTH, mesh_line([(i, i ^ 1) for i in range(8)]))
+
     w = kernel.shape[1] // 4
-
-    own = kernel[:NB, :NB]
     quarters = [kernel[:NB, j * w : (j + 1) * w] for j in range(4)]
-    other = whole_permute(own, BOTH, in_line(((0, 1), (1, 0))))
-    scattered = [
+    got = [
         whole_permute(quarters[j], "row", [(place(c, 0, 0), place(c, j, 0)) for c in (0, 1)]) for j in (2, 1, 3)
     ]
-    corner = jnp.where(z == 0, jnp.concatenate([own, other], 1), jnp.concatenate([other, own], 1))
-    two = whole_permute(corner, BOTH, in_line(((0, 6), (1, 3))))
-    one = whole_permute(corner, BOTH, in_line(((0, 7), (1, 2))))
-    corner = pick(z, corner, corner, one, two, two, two, two, one)
-    quarter = pick(p, quarters[0], scattered[1], scattered[0], scattered[2])
-    first = kernel[:, :NB]
-    corner, quarter, first = lax.optimization_barrier((corner, quarter, first))
-    last = whole_permute(corner, BOTH, in_line(((6, 5), (3, 4))))
-    corner = jnp.where((z == 4) | (z == 5), last, corner)
-
-    far = whole_permute(first, BOTH, in_lines(((0, 4), (1, 5))))
-
-    spread = [
+    quarter = pick(p, quarters[0], got[1], got[0], got[2])
+    got = [
         whole_permute(quarter, "row", [(place(c, j, 0), place(c, j, n)) for c in (0, 1) for j in range(4)])
         for n in (2, 1, 3)
     ]
-    got = [whole_permute(corner, "row", [(place(c, 0, 0), place(c, 0, n)) for c in (0, 1)]) for n in (2, 1, 3)]
-    corner = pick(q, corner, got[1], got[0], got[2])
-    got = [
-        whole_permute(corner, "row", [(place(c, 0, i), place(c, n, i)) for c in (0, 1) for i in range(4)])
-        for n in (2, 1, 3)
-    ]
-    corner = pick(p, corner, got[1], got[0], got[2])
-    quarter = pick(q, quarter, spread[1], spread[0], spread[2])
-    half = jnp.where((z == 4) | (z == 5), far, first)
-    corner, quarter, half = lax.optimization_barrier((corner, quarter, half))
-
-    corner_other = swap(corner)
-    slots = [
+    quarter = pick(q, quarter, got[1], got[0], got[2])
+    slots = [quarter] + [
         lax.ppermute(
             quarter,
             "row",
@@ -333,18 +324,13 @@
         )
         for n in (1, 2, 3)
     ]
-    near = whole_permute(half, BOTH, in_lines(((0, 2), (1, 3), (4, 6), (5, 7))))
+
     l0, w0, s = kernel_call(factor_first, "factor_first", [(2 * NB, NB), (NB, NB), (NB, NB)], 1)(
         core.astype(jnp.int32)[None], corner, corner_other
     )
-    half = jnp.where((z % 4) < 2, half, near)
-    s, half = lax.optimization_barrier((s, half))
-    half_other = whole_permute(half, BOTH, in_lines([(i, i ^ 1) for i in range(8)]))
-    left, right = kernel_call(factor_second, "factor_second", [(NB, NB), (NB, NB)])(s)
-    left, right, quarter, slots = lax.optimization_barrier((left, right, quarter, slots))
-    slots = [quarter, *slots]
+    s, slots = lax.optimization_barrier((s, slots))
     others = [swap(v) for v in slots]
-    l1, w1 = kernel_call(factor_third, "factor_third", [(NB, NB), (NB, 2 * NB)])(left, right, l0, w0)
+    l1, w1 = kernel_call(factor_second, "factor_second", [(NB, NB), (NB, 2 * NB)])(s, l0, w0)
     return update(info, kernel, [half, half_other], slots, others, l0, w0, l1, w1)
 
 

time: 83.3 us -> 77.1 us (0.926)
  waiting for transfers between devices: 37 us -> 30.4 us
  other arithmetic: 2.51 us -> 1.36 us
  starting transfers between devices: 21.4 us -> 22.3 us
    ppermute x19, waiting for transfers between devices: 37 us -> 30.1 us  [whole_permute(): return lax.ppermute(v, axis, sorted(to.items()))]
    select_n x5, other arithmetic: 2.33 us -> 1.2 us  [pick(): out = jnp.where(i == n, values[n], out)]
    ppermute x5, starting transfers between devices: 1.85 us -> 2.81 us  [local(): swap = lambda v: lax.ppermute(v, 'row', [(i, i ^ 1) for i in range(32)])]
    pallas_call x3 -> x2, Pallas kernels: 9.98 us -> 10.6 us  [call(): pl.pallas_call(body, in_specs=[pl.BlockSpec(memory_space=pltpu.SMEM)] * s...]
  transfers between devices with their start and end apart: 27 -> 27, of which waited for: 9 -> 11; matrix products, arithmetic and copies ran while one was open for 4% -> 5% of each run, Pallas kernels for 12% -> 14%
where the time goes in v6:
time: 77.1 us; the launch traced here: 76.2 us
  waiting for transfers between devices  30.4 us (39%)
  starting transfers between devices  22.3 us (29%)
  Pallas kernels  18.7 us (24%)
  local copies, waits for them, and re-layouts  3.09 us (4%)
  other arithmetic  1.36 us (2%)
    ppermute x19, waiting for transfers between devices, whole_permute(): return lax.ppermute(v, axis, sorted(to.items()))  30.1 us
    ppermute x19, starting transfers between devices, whole_permute(): return lax.ppermute(v, axis, sorted(to.items()))  17 us
    pallas_call x2, Pallas kernels, call(): pl.pallas_call(body, in_specs=[pl.BlockSpec(memory_space=pltpu.SMEM)] * s...  10.6 us
    pallas_call x1, Pallas kernels, update(): pl.pallas_call(update_kernel, out_shape=sds(r, c), in_specs=[pl.BlockSpec...  8.09 us
    ppermute x5, starting transfers between devices, local(): swap = lambda v: lax.ppermute(v, 'row', [(i, i ^ 1) for i in range(32)])  2.81 us
    ppermute x3, starting transfers between devices, local(): lax.ppermute(quarter, 'row', [(place(c, j, i), place(c, (j + n) % 4, i))...  2.44 us
  transfers between devices with their start and end apart: 27, of which 11 were waited for; matrix products, arithmetic and copies ran while one was open for 5% of the time, Pallas kernels for 14%

profile of v6, /device:TPU:1, one launch (start us, length us, event | category | flops | bytes accessed | tf_op | source)
XLA Modules:
  0.0 76.2 jit_solution(7697324084579515275)
XLA Ops:
  0.0 0.8 %slice.18 = f32[128,128]{1,0:T(8,128)S(1)} slice(f32[640,2560]{1,0:T(8,128)} %k_ref.1), slice={[0:128], [0:128]} | slice | bytes 131072 | tf_op jit(solution)/shard_map/slice | solution.py:279
  0.8 2.5 %collective-permute-start = (f32[128,128]{1,0:T(8,128)S(1)}, f32[128,128]{1,0:T(8,128)S(1)}, u32[]{:S(2)}, u32[]{:S(2)}) collective-permute-start(f32[128,128]{1,0:T(8,128)S(1)} %slice.18), channel_id=1, source_target_pairs={{0,1},{1,0},{2,10},{3,11},{4,12},{5,13},{6,14},{7,15},{8,9},{9,8},... | collective-permute-start | bytes 196616 | tf_op jit(solution)/shard_map/ppermute | solution.py:261
  3.3 1.7 %collective-permute-done = f32[128,128]{1,0:T(8,128)S(1)} collective-permute-done((f32[128,128]{1,0:T(8,128)S(1)}, f32[128,128]{1,0:T(8,128)S(1)}, u32[]{:S(2)}, u32[]{:S(2)}) %collective-permute-start) | collective-permute-done | bytes 65568 | tf_op jit(solution)/shard_map/ppermute | solution.py:261
  5.0 4.8 %collective-permute-start.3 = (f32[128,256]{1,0:T(8,128)S(1)}, f32[128,256]{1,0:T(8,128)S(1)}, u32[]{:S(2)}, u32[]{:S(2)}) collective-permute-start(f32[128,256]{1,0:T(8,128)S(1)} %maximum_select_fusion), channel_id=1, source_target_pairs={{0,5},{1,4},{2,10},{3,11},{4,1},{5,0},{6,14},{7,15},{8,13},{9,12},... | collective-permute-start | bytes 393224 | tf_op jit(solution)/shard_map/ppermute | solution.py:261
  9.8 1.0 %slice.19 = f32[640,128]{1,0:T(8,128)S(1)} slice(f32[640,2560]{1,0:T(8,128)} %k_ref.1), slice={[0:640], [0:128]} | slice | bytes 655360 | tf_op jit(solution)/shard_map/slice | solution.py:287
  10.8 1.5 %collective-permute-done.3 = f32[128,256]{1,0:T(8,128)S(1)} collective-permute-done((f32[128,256]{1,0:T(8,128)S(1)}, f32[128,256]{1,0:T(8,128)S(1)}, u32[]{:S(2)}, u32[]{:S(2)}) %collective-permute-start.3) | collective-permute-done | bytes 131104 | tf_op jit(solution)/shard_map/ppermute | solution.py:261
  12.3 6.4 %collective-permute-done.2 = f32[128,256]{1,0:T(8,128)S(1)} collective-permute-done((f32[128,256]{1,0:T(8,128)S(1)}, f32[128,256]{1,0:T(8,128)S(1)}, u32[]{:S(2)}, u32[]{:S(2)}) %collective-permute-start.2) | collective-permute-done | bytes 131104 | tf_op jit(solution)/shard_map/ppermute | solution.py:261
  18.8 1.0 %collective-permute-done.1 = f32[128,256]{1,0:T(8,128)S(1)} collective-permute-done((f32[128,256]{1,0:T(8,128)S(1)}, f32[128,256]{1,0:T(8,128)S(1)}, u32[]{:S(2)}, u32[]{:S(2)}) %collective-permute-start.1) | collective-permute-done | bytes 131104 | tf_op jit(solution)/shard_map/ppermute | solution.py:261
  20.0 0.1 collective-permute-start.7
  20.1 1.2 %fusion.2 = (f32[128,640]{1,0:T(8,128)S(1)}, f32[128,640]{1,0:T(8,128)S(1)}, f32[128,640]{1,0:T(8,128)S(1)}) fusion(f32[640,2560]{1,0:T(8,128)} %k_ref.1), kind=kLoop, calls=%fused_computation.12 | loop fusion | bytes 1966080 | tf_op jit(solution)/shard_map/slice | solution.py:309
  21.3 4.3 %collective-permute-start.16 = (f32[128,640]{1,0:T(8,128)S(1)}, f32[128,640]{1,0:T(8,128)S(1)}, u32[]{:S(2)}, u32[]{:S(2)}) collective-permute-start(f32[128,640]{1,0:T(8,128)S(1)} %get-tuple-element.29), channel_id=1, source_target_pairs={{0,192},{8,56},{16,24},{24,16},{32,40},{40,32},{48,8},{56,48},{64,... | collective-permute-start | bytes 983048 | tf_op jit(solution)/shard_map/ppermute | solution.py:261
  25.7 0.4 collective-permute-start.15
  26.0 1.6 %collective-permute-done.9 = f32[128,256]{1,0:T(8,128)S(1)} collective-permute-done((f32[128,256]{1,0:T(8,128)S(1)}, f32[128,256]{1,0:T(8,128)S(1)}, u32[]{:S(2)}, u32[]{:S(2)}) %collective-permute-start.9) | collective-permute-done | bytes 131104 | tf_op jit(solution)/shard_map/ppermute | solution.py:261
  27.8 0.3 collective-permute-start.12
  28.0 7.6 %collective-permute-done.16 = f32[128,640]{1,0:T(8,128)S(1)} collective-permute-done((f32[128,640]{1,0:T(8,128)S(1)}, f32[128,640]{1,0:T(8,128)S(1)}, u32[]{:S(2)}, u32[]{:S(2)}) %collective-permute-start.16) | collective-permute-done | bytes 327712 | tf_op jit(solution)/shard_map/ppermute | solution.py:261
  35.6 1.0 %select_select_fusion.1 = f32[128,640]{1,0:T(8,128)S(1)} fusion(f32[128,640]{1,0:T(8,128)S(1)} %collective-permute-done.14, f32[128,640]{1,0:T(8,128)S(1)} %collective-permute-done.15, f32[128,640]{1,0:T(8,128)S(1)} %collective-permute-done.16, f32[640,2560]{1,0:T(8,128)} %k_ref.1, pred[]{:T(512)S(6)} %eq.69, pred[]{:T(512)S(6)} %eq.68, pred[]{:T(512)S(6)} %eq.64), kind=kLoop, calls=%fused_computation.1 | loop fusion | flops 245760 | bytes 1638403 | tf_op jit(solution)/shard_map/jit(_where)/select_n | solution.py:267
  36.7 0.1 collective-permute-start.19
  36.8 2.8 %collective-permute-start.18 = (f32[128,640]{1,0:T(8,128)S(1)}, f32[128,640]{1,0:T(8,128)S(1)}, u32[]{:S(2)}, u32[]{:S(2)}) collective-permute-start(f32[128,640]{1,0:T(8,128)S(1)} %select_select_fusion.1), channel_id=1, source_target_pairs={{0,32},{8,136},{16,24},{24,152},{32,0},{40,168},{48,56},{56,184},{... | collective-permute-start | bytes 983048 | tf_op jit(solution)/shard_map/ppermute | solution.py:261
  39.6 1.7 %collective-permute-done.11 = f32[128,256]{1,0:T(8,128)S(1)} collective-permute-done((f32[128,256]{1,0:T(8,128)S(1)}, f32[128,256]{1,0:T(8,128)S(1)}, u32[]{:S(2)}, u32[]{:S(2)}) %collective-permute-start.11) | collective-permute-done | bytes 131104 | tf_op jit(solution)/shard_map/ppermute | solution.py:261
  41.3 0.7 collective-permute-start.13
  42.1 1.5 %collective-permute-start.5 = (f32[640,128]{1,0:T(8,128)S(1)}, f32[640,128]{1,0:T(8,128)S(1)}, u32[]{:S(2)}, u32[]{:S(2)}) collective-permute-start(f32[640,128]{1,0:T(8,128)S(1)} %broadcast_select_fusion), channel_id=1, source_target_pairs={{0,2},{1,3},{2,0},{3,1},{4,6},{5,7},{6,4},{7,5},{8,10},{9,11},{10,... | collective-permute-start | bytes 983048 | tf_op jit(solution)/shard_map/ppermute | solution.py:261
  43.5 4.7 %collective-permute-done.19 = f32[128,640]{1,0:T(8,128)S(1)} collective-permute-done((f32[128,640]{1,0:T(8,128)S(1)}, f32[128,640]{1,0:T(8,128)S(1)}, u32[]{:S(2)}, u32[]{:S(2)}) %collective-permute-start.19) | collective-permute-done | bytes 327712 | tf_op jit(solution)/shard_map/ppermute | solution.py:261
  48.4 2.4 %collective-permute-start.21 = (f32[128,640]{1,0:T(8,128)S(1)}, f32[128,640]{1,0:T(8,128)S(1)}, u32[]{:S(2)}, u32[]{:S(2)}) collective-permute-start(f32[128,640]{1,0:T(8,128)S(1)} %select_select_fusion.s0), channel_id=1, source_target_pairs={{0,128},{16,144},{32,160},{48,176},{64,192},{80,208},{96,224},{112... | collective-permute-start | bytes 983048 | tf_op jit(solution)/shard_map/ppermute | solution.py:320
  50.8 5.5 %factor_first.1 = (f32[256,128]{1,0:T(8,128)S(1)}, f32[128,128]{1,0:T(8,128)S(1)}, f32[128,128]{1,0:T(8,128)S(1)}) custom-call(s32[1]{0:T(128)} %bitcast.4.core, f32[128,256]{1,0:T(8,128)S(1)} %select_select_fusion.4.mine, f32[128,256]{1,0:T(8,128)S(1)} %collective-permute-done.13.other), custom_call_target="tpu_custom_call" | custom-call | flops 1000000000 | bytes 1000000 | tf_op jit(solution)/shard_map/factor_first/pallas_call | solution.py:339
  56.3 3.1 %collective-permute-done.5 = f32[640,128]{1,0:T(8,128)S(1)} collective-permute-done((f32[640,128]{1,0:T(8,128)S(1)}, f32[640,128]{1,0:T(8,128)S(1)}, u32[]{:S(2)}, u32[]{:S(2)}) %collective-permute-start.5) | collective-permute-done | bytes 327712 | tf_op jit(solution)/shard_map/ppermute | solution.py:261
  59.4 0.1 collective-permute-start.6
  59.5 0.2 collective-permute-done.20.s1
  59.7 1.6 %collective-permute-start.23 = (f32[128,640]{1,0:T(8,128)S(1)}, f32[128,640]{1,0:T(8,128)S(1)}, u32[]{:S(2)}, u32[]{:S(2)}) collective-permute-start(f32[128,640]{1,0:T(8,128)S(1)} %select_select_fusion.s0), channel_id=1, source_target_pairs={{0,8},{8,0},{16,24},{24,16},{32,40},{40,32},{48,56},{56,48},{64,72... | collective-permute-start | bytes 983048 | tf_op jit(solution)/shard_map/ppermute | solution.py:298
  61.3 0.5 collective-permute-start.25
  61.9 5.1 %factor_second.1 = (f32[128,128]{1,0:T(8,128)S(1)}, f32[128,256]{1,0:T(8,128)S(1)}) custom-call(f32[128,128]{1,0:T(8,128)S(1)} %get-tuple-element.26.s_ref, f32[256,128]{1,0:T(8,128)S(1)} %get-tuple-element.24.l_ref.l0_ref, f32[128,128]{1,0:T(8,128)S(1)} %get-tuple-element.25.w0_ref), custom_call_target="tpu_custom_call" | custom-call | flops 1000000000 | bytes 1000000 | tf_op jit(solution)/shard_map/factor_second/pallas_call | solution.py:339
  67.0 0.9 %collective-permute-done.6.h1 = f32[640,128]{1,0:T(8,128)S(1)} collective-permute-done((f32[640,128]{1,0:T(8,128)S(1)}, f32[640,128]{1,0:T(8,128)S(1)}, u32[]{:S(2)}, u32[]{:S(2)}) %collective-permute-start.6) | collective-permute-done | bytes 327712 | tf_op jit(solution)/shard_map/ppermute | solution.py:261
  68.0 8.1 %update.1 = f32[640,2560]{1,0:T(8,128)} custom-call(s32[4]{0:T(128)S(1)} %pad_add_fusion.info, f32[640,2560]{1,0:T(8,128)S(1)} %bitcast.6, f32[640,128]{1,0:T(8,128)S(1)} %broadcast_select_fusion.1.h0, f32[640,128]{1,0:T(8,128)S(1)} %collective-permute-done.6.h1, f32[128,640]{1,0:T(8,128)S(1)} %select_select_fusion.s0, ...), custom_call_target="tpu_custom_call" | custom-call | flops 5000000000 | bytes 18000000 | tf_op jit(solution)/shard_map/update/pallas_call | solution.py:208
  (42 shorter events, 0.6 us)
Async XLA Ops:
  0.8 4.1 %collective-permute-start = (f32[128,128]{1,0:T(8,128)S(1)}, f32[128,128]{1,0:T(8,128)S(1)}, u32[]{:S(2)}, u32[]{:S(2)}) collective-permute-start(f32[128,128]{1,0:T(8,128)S(1)} %slice.18), channel_id=1, source_target_pairs={{0,1},{1,0},{2,10},{3,11},{4,12},{5,13},{6,14},{7,15},{8,9},{9,8},... | collective-permute-start | bytes 196616 | tf_op jit(solution)/shard_map/ppermute | solution.py:261
  5.0 7.4 %collective-permute-start.3 = (f32[128,256]{1,0:T(8,128)S(1)}, f32[128,256]{1,0:T(8,128)S(1)}, u32[]{:S(2)}, u32[]{:S(2)}) collective-permute-start(f32[128,256]{1,0:T(8,128)S(1)} %maximum_select_fusion), channel_id=1, source_target_pairs={{0,5},{1,4},{2,10},{3,11},{4,1},{5,0},{6,14},{7,15},{8,13},{9,12},... | collective-permute-start | bytes 393224 | tf_op jit(solution)/shard_map/ppermute | solution.py:261
  9.8 9.0 %collective-permute-start.2 = (f32[128,256]{1,0:T(8,128)S(1)}, f32[128,256]{1,0:T(8,128)S(1)}, u32[]{:S(2)}, u32[]{:S(2)}) collective-permute-start(f32[128,256]{1,0:T(8,128)S(1)} %maximum_select_fusion), channel_id=1, source_target_pairs={{0,6},{1,3},{2,10},{3,1},{4,12},{5,13},{6,0},{7,15},{8,14},{9,11},... | collective-permute-start | bytes 393224 | tf_op jit(solution)/shard_map/ppermute | solution.py:261
  9.8 9.9 %collective-permute-start.1 = (f32[128,256]{1,0:T(8,128)S(1)}, f32[128,256]{1,0:T(8,128)S(1)}, u32[]{:S(2)}, u32[]{:S(2)}) collective-permute-start(f32[128,256]{1,0:T(8,128)S(1)} %maximum_select_fusion), channel_id=1, source_target_pairs={{0,7},{1,2},{2,1},{3,11},{4,12},{5,13},{6,14},{7,0},{8,15},{9,10},... | collective-permute-start | bytes 393224 | tf_op jit(solution)/shard_map/ppermute | solution.py:261
  19.8 7.9 %collective-permute-start.9 = (f32[128,256]{1,0:T(8,128)S(1)}, f32[128,256]{1,0:T(8,128)S(1)}, u32[]{:S(2)}, u32[]{:S(2)}) collective-permute-start(f32[128,256]{1,0:T(8,128)S(1)} %select_select_fusion.2), channel_id=1, source_target_pairs={{0,48},{8,200},{16,24},{24,16},{32,40},{40,32},{48,56},{56,0},{64,... | collective-permute-start | bytes 393224 | tf_op jit(solution)/shard_map/ppermute | solution.py:261
  19.9 7.8 %collective-permute-start.8 = (f32[128,256]{1,0:T(8,128)S(1)}, f32[128,256]{1,0:T(8,128)S(1)}, u32[]{:S(2)}, u32[]{:S(2)}) collective-permute-start(f32[128,256]{1,0:T(8,128)S(1)} %select_select_fusion.2), channel_id=1, source_target_pairs={{0,32},{8,136},{16,24},{24,16},{32,40},{40,0},{48,56},{56,48},{64,... | collective-permute-start | bytes 393224 | tf_op jit(solution)/shard_map/ppermute | solution.py:261
  20.0 7.7 %collective-permute-start.7 = (f32[128,256]{1,0:T(8,128)S(1)}, f32[128,256]{1,0:T(8,128)S(1)}, u32[]{:S(2)}, u32[]{:S(2)}) collective-permute-start(f32[128,256]{1,0:T(8,128)S(1)} %select_select_fusion.2), channel_id=1, source_target_pairs={{0,16},{8,72},{16,24},{24,0},{32,40},{40,32},{48,56},{56,48},{64,8... | collective-permute-start | bytes 393224 | tf_op jit(solution)/shard_map/ppermute | solution.py:261
  21.3 14.3 %collective-permute-start.16 = (f32[128,640]{1,0:T(8,128)S(1)}, f32[128,640]{1,0:T(8,128)S(1)}, u32[]{:S(2)}, u32[]{:S(2)}) collective-permute-start(f32[128,640]{1,0:T(8,128)S(1)} %get-tuple-element.29), channel_id=1, source_target_pairs={{0,192},{8,56},{16,24},{24,16},{32,40},{40,32},{48,8},{56,48},{64,... | collective-permute-start | bytes 983048 | tf_op jit(solution)/shard_map/ppermute | solution.py:261
  25.7 9.9 %collective-permute-start.15 = (f32[128,640]{1,0:T(8,128)S(1)}, f32[128,640]{1,0:T(8,128)S(1)}, u32[]{:S(2)}, u32[]{:S(2)}) collective-permute-start(f32[128,640]{1,0:T(8,128)S(1)} %get-tuple-element.30), channel_id=1, source_target_pairs={{0,128},{8,40},{16,24},{24,16},{32,8},{40,32},{48,56},{56,48},{64,... | collective-permute-start | bytes 983048 | tf_op jit(solution)/shard_map/ppermute | solution.py:261
  27.7 8.0 %collective-permute-start.14 = (f32[128,640]{1,0:T(8,128)S(1)}, f32[128,640]{1,0:T(8,128)S(1)}, u32[]{:S(2)}, u32[]{:S(2)}) collective-permute-start(f32[128,640]{1,0:T(8,128)S(1)} %get-tuple-element.31), channel_id=1, source_target_pairs={{0,64},{8,24},{16,8},{24,16},{32,40},{40,32},{48,56},{56,48},{64,7... | collective-permute-start | bytes 983048 | tf_op jit(solution)/shard_map/ppermute | solution.py:261
  27.7 14.3 %collective-permute-start.4 = (f32[640,128]{1,0:T(8,128)S(1)}, f32[640,128]{1,0:T(8,128)S(1)}, u32[]{:S(2)}, u32[]{:S(2)}) collective-permute-start(f32[640,128]{1,0:T(8,128)S(1)} %slice.19), channel_id=1, source_target_pairs={{0,4},{1,5},{2,10},{3,11},{4,0},{5,1},{6,14},{7,15},{8,12},{9,13},... | collective-permute-start | bytes 983048 | tf_op jit(solution)/shard_map/ppermute | solution.py:261
  27.7 40.2 %slice-start = ((s8[6553600]{0:T(1024)(128)(4,1)}), s8[4194304]{0:T(1024)(128)(4,1)S(1)}, s32[]{:S(2)}) async-start(s8[6553600]{0:T(1024)(128)(4,1)} %bitcast.5), calls=%async_computation | async-start | bytes 8388608
  27.8 9.0 %collective-permute-start.12 = (f32[128,256]{1,0:T(8,128)S(1)}, f32[128,256]{1,0:T(8,128)S(1)}, u32[]{:S(2)}, u32[]{:S(2)}) collective-permute-start(f32[128,256]{1,0:T(8,128)S(1)} %select_select_fusion.5), channel_id=1, source_target_pairs={{0,192},{8,56},{16,208},{24,16},{32,224},{40,32},{48,240},{56,8},{... | collective-permute-start | bytes 393224 | tf_op jit(solution)/shard_map/ppermute | solution.py:261
  35.6 5.6 %collective-permute-start.11 = (f32[128,256]{1,0:T(8,128)S(1)}, f32[128,256]{1,0:T(8,128)S(1)}, u32[]{:S(2)}, u32[]{:S(2)}) collective-permute-start(f32[128,256]{1,0:T(8,128)S(1)} %select_select_fusion.5), channel_id=1, source_target_pairs={{0,128},{8,40},{16,144},{24,16},{32,160},{40,8},{48,176},{56,48},{... | collective-permute-start | bytes 393224 | tf_op jit(solution)/shard_map/ppermute | solution.py:261
  35.6 5.6 %collective-permute-start.10 = (f32[128,256]{1,0:T(8,128)S(1)}, f32[128,256]{1,0:T(8,128)S(1)}, u32[]{:S(2)}, u32[]{:S(2)}) collective-permute-start(f32[128,256]{1,0:T(8,128)S(1)} %select_select_fusion.5), channel_id=1, source_target_pairs={{0,64},{8,24},{16,80},{24,8},{32,96},{40,32},{48,112},{56,48},{64,... | collective-permute-start | bytes 393224 | tf_op jit(solution)/shard_map/ppermute | solution.py:261
  36.7 11.6 %collective-permute-start.19 = (f32[128,640]{1,0:T(8,128)S(1)}, f32[128,640]{1,0:T(8,128)S(1)}, u32[]{:S(2)}, u32[]{:S(2)}) collective-permute-start(f32[128,640]{1,0:T(8,128)S(1)} %select_select_fusion.1), channel_id=1, source_target_pairs={{0,48},{8,200},{16,24},{24,216},{32,40},{40,232},{48,0},{56,248},{... | collective-permute-start | bytes 983048 | tf_op jit(solution)/shard_map/ppermute | solution.py:261
  36.8 11.5 %collective-permute-start.18 = (f32[128,640]{1,0:T(8,128)S(1)}, f32[128,640]{1,0:T(8,128)S(1)}, u32[]{:S(2)}, u32[]{:S(2)}) collective-permute-start(f32[128,640]{1,0:T(8,128)S(1)} %select_select_fusion.1), channel_id=1, source_target_pairs={{0,32},{8,136},{16,24},{24,152},{32,0},{40,168},{48,56},{56,184},{... | collective-permute-start | bytes 983048 | tf_op jit(solution)/shard_map/ppermute | solution.py:261
  41.2 7.0 %collective-permute-start.17 = (f32[128,640]{1,0:T(8,128)S(1)}, f32[128,640]{1,0:T(8,128)S(1)}, u32[]{:S(2)}, u32[]{:S(2)}) collective-permute-start(f32[128,640]{1,0:T(8,128)S(1)} %select_select_fusion.1), channel_id=1, source_target_pairs={{0,16},{8,72},{16,0},{24,88},{32,40},{40,104},{48,56},{56,120},{64... | collective-permute-start | bytes 983048 | tf_op jit(solution)/shard_map/ppermute | solution.py:261
  41.3 9.5 %collective-permute-start.13 = (f32[128,256]{1,0:T(8,128)S(1)}, f32[128,256]{1,0:T(8,128)S(1)}, u32[]{:S(2)}, u32[]{:S(2)}) collective-permute-start(f32[128,256]{1,0:T(8,128)S(1)} %select_select_fusion.4.mine), channel_id=1, source_target_pairs={{0,8},{8,0},{16,24},{24,16},{32,40},{40,32},{48,56},{56,48},{64,72... | collective-permute-start | bytes 393224 | tf_op jit(solution)/shard_map/ppermute | solution.py:298
  42.1 17.3 %collective-permute-start.5 = (f32[640,128]{1,0:T(8,128)S(1)}, f32[640,128]{1,0:T(8,128)S(1)}, u32[]{:S(2)}, u32[]{:S(2)}) collective-permute-start(f32[640,128]{1,0:T(8,128)S(1)} %broadcast_select_fusion), channel_id=1, source_target_pairs={{0,2},{1,3},{2,0},{3,1},{4,6},{5,7},{6,4},{7,5},{8,10},{9,11},{10,... | collective-permute-start | bytes 983048 | tf_op jit(solution)/shard_map/ppermute | solution.py:261
  48.3 11.2 %collective-permute-start.22 = (f32[128,640]{1,0:T(8,128)S(1)}, f32[128,640]{1,0:T(8,128)S(1)}, u32[]{:S(2)}, u32[]{:S(2)}) collective-permute-start(f32[128,640]{1,0:T(8,128)S(1)} %select_select_fusion.s0), channel_id=1, source_target_pairs={{0,192},{16,208},{32,224},{48,240},{64,0},{80,16},{96,32},{112,48}... | collective-permute-start | bytes 983048 | tf_op jit(solution)/shard_map/ppermute | solution.py:320
  48.4 11.1 %collective-permute-start.21 = (f32[128,640]{1,0:T(8,128)S(1)}, f32[128,640]{1,0:T(8,128)S(1)}, u32[]{:S(2)}, u32[]{:S(2)}) collective-permute-start(f32[128,640]{1,0:T(8,128)S(1)} %select_select_fusion.s0), channel_id=1, source_target_pairs={{0,128},{16,144},{32,160},{48,176},{64,192},{80,208},{96,224},{112... | collective-permute-start | bytes 983048 | tf_op jit(solution)/shard_map/ppermute | solution.py:320
  50.8 9.0 %collective-permute-start.20 = (f32[128,640]{1,0:T(8,128)S(1)}, f32[128,640]{1,0:T(8,128)S(1)}, u32[]{:S(2)}, u32[]{:S(2)}) collective-permute-start(f32[128,640]{1,0:T(8,128)S(1)} %select_select_fusion.s0), channel_id=1, source_target_pairs={{0,64},{16,80},{32,96},{48,112},{64,128},{80,144},{96,160},{112,17... | collective-permute-start | bytes 983048 | tf_op jit(solution)/shard_map/ppermute | solution.py:320
  50.8 17.2 %slice-start.1 = ((s8[6553600]{0:T(1024)(128)(4,1)}), s8[2359296]{0:T(1024)(128)(4,1)S(1)}, s32[]{:S(2)}) async-start(s8[6553600]{0:T(1024)(128)(4,1)} %bitcast.5), calls=%async_computation.1 | async-start | bytes 4718592
  59.4 8.5 %collective-permute-start.6 = (f32[640,128]{1,0:T(8,128)S(1)}, f32[640,128]{1,0:T(8,128)S(1)}, u32[]{:S(2)}, u32[]{:S(2)}) collective-permute-start(f32[640,128]{1,0:T(8,128)S(1)} %broadcast_select_fusion.1.h0), channel_id=1, source_target_pairs={{0,1},{1,0},{2,3},{3,2},{4,5},{5,4},{6,7},{7,6},{8,9},{9,8},{10,11... | collective-permute-start | bytes 983048 | tf_op jit(solution)/shard_map/ppermute | solution.py:261
  59.7 8.2 %collective-permute-start.23 = (f32[128,640]{1,0:T(8,128)S(1)}, f32[128,640]{1,0:T(8,128)S(1)}, u32[]{:S(2)}, u32[]{:S(2)}) collective-permute-start(f32[128,640]{1,0:T(8,128)S(1)} %select_select_fusion.s0), channel_id=1, source_target_pairs={{0,8},{8,0},{16,24},{24,16},{32,40},{40,32},{48,56},{56,48},{64,72... | collective-permute-start | bytes 983048 | tf_op jit(solution)/shard_map/ppermute | solution.py:298
  61.3 6.6 %collective-permute-start.24 = (f32[128,640]{1,0:T(8,128)S(1)}, f32[128,640]{1,0:T(8,128)S(1)}, u32[]{:S(2)}, u32[]{:S(2)}) collective-permute-start(f32[128,640]{1,0:T(8,128)S(1)} %collective-permute-done.20.s1), channel_id=1, source_target_pairs={{0,8},{8,0},{16,24},{24,16},{32,40},{40,32},{48,56},{56,48},{64,72... | collective-permute-start | bytes 983048 | tf_op jit(solution)/shard_map/ppermute | solution.py:298
  61.3 6.6 %collective-permute-start.25 = (f32[128,640]{1,0:T(8,128)S(1)}, f32[128,640]{1,0:T(8,128)S(1)}, u32[]{:S(2)}, u32[]{:S(2)}) collective-permute-start(f32[128,640]{1,0:T(8,128)S(1)} %collective-permute-done.21.s2), channel_id=1, source_target_pairs={{0,8},{8,0},{16,24},{24,16},{32,40},{40,32},{48,56},{56,48},{64,72... | collective-permute-start | bytes 983048 | tf_op jit(solution)/shard_map/ppermute | solution.py:298
  61.8 6.1 %collective-permute-start.26 = (f32[128,640]{1,0:T(8,128)S(1)}, f32[128,640]{1,0:T(8,128)S(1)}, u32[]{:S(2)}, u32[]{:S(2)}) collective-permute-start(f32[128,640]{1,0:T(8,128)S(1)} %collective-permute-done.22.s3), channel_id=1, source_target_pairs={{0,8},{8,0},{16,24},{24,16},{32,40},{40,32},{48,56},{56,48},{64,72... | collective-permute-start | bytes 983048 | tf_op jit(solution)/shard_map/ppermute | solution.py:298
